TPU v7x, 32 devices: a whole 2x2x4 slice. The times are simulated.
32 devices in a mesh: dp: 8 (over z, x), mp: 4 (over y, core).
Axes of the slice: x: 2, y: 2, z: 4, core: 2. Of those that a mesh axis runs over, the one named last changes fastest.
Arguments:
- decoder_in: bfloat16 [8, 512, 768], P('dp', 'mp'), may hold values from -6 to 6
- encoder_states: bfloat16 [8, 512, 768], P('dp', 'mp'), may hold values from -6 to 6
- dec_segments: int32 [8, 512], P('dp'), may hold values from 0 to 3, never falling along the last dimension, each value on 1 to 386 neighbouring positions
- enc_segments: int32 [8, 512], P('dp'), may hold values from 0 to 3, never falling along the last dimension, each value on 1 to 386 neighbouring positions
- offset_buckets: int32 [512], replicated, may hold values from 0 to 31
- norm_gains: float32 [3, 768], replicated, may hold values from 0.5 to 1.5
- bias_table: float32 [32, 12], P(None, 'mp'), may hold values from -6 to 6
- self_query: bfloat16 [768, 768], P(None, 'mp'), may hold values from -0.21875 to 0.21875
- self_key: bfloat16 [768, 768], P(None, 'mp'), may hold values from -0.21875 to 0.21875
- self_value: bfloat16 [768, 768], P(None, 'mp'), may hold values from -0.21875 to 0.21875
- self_out: bfloat16 [768, 768], P(None, 'mp'), may hold values from -1.25 to 1.25
- cross_query: bfloat16 [768, 768], P(None, 'mp'), may hold values from -0.21875 to 0.21875
- cross_key: bfloat16 [768, 768], P(None, 'mp'), may hold values from -0.21875 to 0.21875
- cross_value: bfloat16 [768, 768], P(None, 'mp'), may hold values from -0.21875 to 0.21875
- cross_out: bfloat16 [768, 768], P(None, 'mp'), may hold values from -1.25 to 1.25
- ffn_up: bfloat16 [768, 3072], P(None, 'mp'), may hold values from -0.21875 to 0.21875
- ffn_down: bfloat16 [768, 3072], P(None, 'mp'), may hold values from -0.15625 to 0.15625
- out_grad: bfloat16 [8, 512, 768], P('dp', 'mp'), may hold values from -8 to 8
Outputs:
- output: bfloat16 [8, 512, 768], P('dp', 'mp')
- grad_decoder: bfloat16 [8, 512, 768], P('dp', 'mp')
- grad_encoder: bfloat16 [8, 512, 768], P('dp', 'mp')
- grad_self_query: float32 [768, 768], P('dp', 'mp')
- grad_self_key: float32 [768, 768], P('dp', 'mp')
- grad_self_value: float32 [768, 768], P('dp', 'mp')
- grad_self_out: float32 [768, 768], P('dp', 'mp')
- grad_cross_query: float32 [768, 768], P('dp', 'mp')
- grad_cross_key: float32 [768, 768], P('dp', 'mp')
- grad_cross_value: float32 [768, 768], P('dp', 'mp')
- grad_cross_out: float32 [768, 768], P('dp', 'mp')
- grad_ffn_up: float32 [768, 3072], P('dp', 'mp')
- grad_ffn_down: float32 [768, 3072], P('dp', 'mp')
- grad_gains: float32 [3, 768], replicated
- grad_table: float32 [32, 12], replicated
Inputs may be any that keep to these rules, and one draw needn't show every extreme that they name: `dec_segments`: in every row the numbers never fall, every number appears, and one document has exactly 386 positions, none more; equal numbers in dec_segments and enc_segments of a row mark one document. `enc_segments`: in every row the numbers never fall, every number appears, and one document has exactly 386 positions, none more.
All inputs are finite; a program needn't handle non-finite values.
Results may differ from a plain program's by a relative error of at most 0.023.
Values may be sent and summed in bfloat16 or wider, within the bound.
No kernel may reach another device: no remote copies, remote signals or barrier semaphores. Data moves between devices by JAX's collectives and lax.ppermute only.
A program may use at most 128 MiB of HBM per device.

v0:
```python
import jax
import jax.numpy as jnp
from jax import lax
from jax.sharding import PartitionSpec as P

HEAD_DIM = 64


epsilon = 1e-06
key_scale = 0.125
masked_score = -1e30
highest = lax.Precision.HIGHEST


def rms_scaled(values_in, gain_row):
    return (
        values_in
        * lax.rsqrt(jnp.mean(values_in * values_in, axis=-1, keepdims=True) + epsilon)
        * gain_row
    )


def norm_back(stream_rows, gain_row, grad_normed, grad_stream):
    unused_value, pullback = jax.vjp(rms_scaled, stream_rows, gain_row)
    grad_rows, grad_gain = pullback(grad_normed)
    return (grad_stream + grad_rows, grad_gain)


def gelu_tanh(values_in):
    return jax.nn.gelu(values_in, approximate=True)


def to_heads(values_in, weight):
    return jnp.einsum("rtd,dh->rth", values_in, weight, preferred_element_type=jnp.float32)


def from_heads(values_in, weight):
    return jnp.einsum("rth,dh->rtd", values_in, weight, preferred_element_type=jnp.float32)


def weight_grad(inputs_low, grads_low):
    return jnp.einsum("rtd,rth->dh", inputs_low, grads_low, preferred_element_type=jnp.float32)


def gather_rows(values_in):
    return lax.all_gather(values_in, "mp", axis=1, tiled=True)


def sum_rows(partial_sum):
    return lax.psum_scatter(partial_sum, "mp", scatter_dimension=1, tiled=True)


def split_heads(values_in):
    return values_in.reshape(values_in.shape[0], values_in.shape[1] // HEAD_DIM, HEAD_DIM)


def skew_bias(by_distance):
    values = by_distance.T
    head_count, length = values.shape
    tail = jnp.broadcast_to(values[:, :1], values.shape)
    ramp = jnp.concatenate([values[:, ::-1], tail], axis=1)
    rolled = jnp.concatenate([ramp[:, length - 1 :], ramp[:, : length - 1]], axis=1)
    tiled = jnp.tile(rolled, (1, length))[:, : length * (2 * length - 1)]
    return tiled.reshape(head_count, length, 2 * length - 1)[:, :, :length]


def diagonal_sums(grad_bias):
    head_count, length, unused_width = grad_bias.shape
    padded = jnp.pad(grad_bias, ((0, 0), (0, 0), (0, length - 1)))
    flat = jnp.pad(padded.reshape(head_count, -1), ((0, 0), (0, length)))
    columns = jnp.sum(flat.reshape(head_count, length, 2 * length), axis=1)
    per_distance = jnp.concatenate([columns[:, :1], columns[:, length + 1 :][:, ::-1]], axis=1)
    return per_distance.T


def allowed_pairs(query_seg, key_seg, causal):
    allowed = query_seg[:, None] == key_seg[None, :]
    if causal:
        places = jnp.arange(query_seg.shape[0])
        allowed = allowed & (places[:, None] >= places[None, :])
    return allowed


def row_scores(query_heads, key_heads, allowed, extra_bias):
    scores = (
        jnp.einsum("qhd,khd->hqk", query_heads, key_heads, preferred_element_type=jnp.float32)
        * key_scale
        + extra_bias
    )
    return jnp.where(allowed[None], scores, masked_score)


def attend_forward(queries, keys_in, values_in, query_segs, key_segs, causal, extra_bias):

    def one_row(row_items):
        query_row, key_row, value_row, query_seg, key_seg = row_items
        scores = row_scores(
            split_heads(query_row),
            split_heads(key_row),
            allowed_pairs(query_seg, key_seg, causal),
            extra_bias,
        )
        row_max = jnp.max(scores, axis=-1, keepdims=True)
        exp_scores = jnp.exp(scores - row_max)
        row_total = jnp.sum(exp_scores, axis=-1, keepdims=True)
        soft_weights = (exp_scores / row_total).astype(jnp.bfloat16)
        mixed_row = jnp.einsum(
            "hqk,khd->qhd", soft_weights, split_heads(value_row), preferred_element_type=jnp.float32
        )
        return (
            mixed_row.reshape(query_row.shape).astype(jnp.bfloat16),
            (row_max + jnp.log(row_total))[..., 0],
        )

    return lax.map(one_row, (queries, keys_in, values_in, query_segs, key_segs))


def attend_backward(
    queries, keys_in, values_in, query_segs, key_segs, causal, extra_bias, log_totals, grad_mixed
):

    def one_row(carried, row_items):
        query_row, key_row, value_row, query_seg, key_seg, log_total, grad_row = row_items
        query_heads = split_heads(query_row)
        key_heads = split_heads(key_row)
        value_heads = split_heads(value_row)
        grad_heads = split_heads(grad_row)
        scores = row_scores(
            query_heads, key_heads, allowed_pairs(query_seg, key_seg, causal), extra_bias
        )
        soft_full = jnp.exp(scores - log_total[..., None])
        grad_soft = jnp.einsum(
            "qhd,khd->hqk", grad_heads, value_heads, preferred_element_type=jnp.float32
        )
        row_dot = jnp.sum(soft_full * grad_soft, axis=-1, keepdims=True)
        grad_scores = (soft_full * (grad_soft - row_dot)).astype(jnp.bfloat16)
        grad_query = (
            jnp.einsum("hqk,khd->qhd", grad_scores, key_heads, preferred_element_type=jnp.float32)
            * key_scale
        ).astype(jnp.bfloat16)
        grad_key = (
            jnp.einsum("hqk,qhd->khd", grad_scores, query_heads, preferred_element_type=jnp.float32)
            * key_scale
        ).astype(jnp.bfloat16)
        grad_value = jnp.einsum(
            "hqk,qhd->khd",
            soft_full.astype(jnp.bfloat16),
            grad_heads,
            preferred_element_type=jnp.float32,
        ).astype(jnp.bfloat16)
        if causal:
            carried = carried + grad_scores.astype(jnp.float32)
        return (
            carried,
            (
                grad_query.reshape(query_row.shape),
                grad_key.reshape(key_row.shape),
                grad_value.reshape(value_row.shape),
            ),
        )

    if causal:
        start_sum = jnp.zeros(extra_bias.shape, jnp.float32)
    else:
        start_sum = jnp.zeros((), jnp.float32)
    return lax.scan(
        one_row,
        start_sum,
        (queries, keys_in, values_in, query_segs, key_segs, log_totals, grad_mixed),
    )


def local(
    decoder_in,
    encoder_states,
    dec_segments,
    enc_segments,
    offset_buckets,
    norm_gains,
    bias_table,
    self_query,
    self_key,
    self_value,
    self_out,
    cross_query,
    cross_key,
    cross_value,
    cross_out,
    ffn_up,
    ffn_down,
    out_grad,
):
    bucket_count = bias_table.shape[0]
    heads_here = bias_table.shape[1]
    one_hot = (offset_buckets[:, None] == jnp.arange(bucket_count)[None, :]).astype(jnp.float32)
    by_distance = jnp.dot(one_hot, bias_table, precision=highest)
    self_bias = skew_bias(by_distance)
    no_bias = jnp.zeros((), jnp.float32)
    stream_in = decoder_in.astype(jnp.float32)
    normed_one = rms_scaled(stream_in, norm_gains[0]).astype(jnp.bfloat16)
    gathered_one = gather_rows(normed_one)
    query_one = to_heads(gathered_one, self_query).astype(jnp.bfloat16)
    key_one = to_heads(gathered_one, self_key).astype(jnp.bfloat16)
    value_one = to_heads(gathered_one, self_value).astype(jnp.bfloat16)
    mixed_one, log_one = attend_forward(
        query_one, key_one, value_one, dec_segments, dec_segments, True, self_bias
    )
    stream_mid = stream_in + sum_rows(from_heads(mixed_one, self_out))
    normed_two = rms_scaled(stream_mid, norm_gains[1]).astype(jnp.bfloat16)
    gathered_two = gather_rows(normed_two)
    query_two = to_heads(gathered_two, cross_query).astype(jnp.bfloat16)
    encoder_all = lax.all_gather(encoder_states, "mp", axis=1, tiled=True)
    key_two = to_heads(encoder_all, cross_key).astype(jnp.bfloat16)
    value_two = to_heads(encoder_all, cross_value).astype(jnp.bfloat16)
    mixed_two, log_two = attend_forward(
        query_two, key_two, value_two, dec_segments, enc_segments, False, no_bias
    )
    stream_end = stream_mid + sum_rows(from_heads(mixed_two, cross_out))
    normed_three = rms_scaled(stream_end, norm_gains[2]).astype(jnp.bfloat16)
    gathered_three = gather_rows(normed_three)
    hidden_pre = to_heads(gathered_three, ffn_up)
    hidden_act = gelu_tanh(hidden_pre).astype(jnp.bfloat16)
    result = stream_end + sum_rows(from_heads(hidden_act, ffn_down))
    grad_stream = out_grad.astype(jnp.float32)
    grad_ffn = gather_rows(grad_stream.astype(jnp.bfloat16))
    grad_down = weight_grad(grad_ffn, hidden_act)
    grad_act = to_heads(grad_ffn, ffn_down)
    unused_act, gelu_pull = jax.vjp(gelu_tanh, hidden_pre)
    grad_pre = gelu_pull(grad_act)[0].astype(jnp.bfloat16)
    grad_up = weight_grad(gathered_three, grad_pre)
    grad_normed = sum_rows(from_heads(grad_pre, ffn_up))
    grad_stream, gain_three = norm_back(stream_end, norm_gains[2], grad_normed, grad_stream)
    grad_cross = gather_rows(grad_stream.astype(jnp.bfloat16))
    grad_cross_out = weight_grad(grad_cross, mixed_two)
    grad_mixed_two = to_heads(grad_cross, cross_out).astype(jnp.bfloat16)
    unused_sum, cross_grads = attend_backward(
        query_two,
        key_two,
        value_two,
        dec_segments,
        enc_segments,
        False,
        no_bias,
        log_two,
        grad_mixed_two,
    )
    grad_query_two, grad_key_two, grad_value_two = cross_grads
    grad_cross_query = weight_grad(gathered_two, grad_query_two)
    grad_normed = sum_rows(from_heads(grad_query_two, cross_query))
    grad_cross_key = weight_grad(encoder_all, grad_key_two)
    grad_cross_value = weight_grad(encoder_all, grad_value_two)
    encoder_terms = from_heads(grad_key_two, cross_key) + from_heads(grad_value_two, cross_value)
    grad_encoder = lax.psum_scatter(
        encoder_terms.astype(jnp.bfloat16), "mp", scatter_dimension=1, tiled=True
    )
    grad_stream, gain_two = norm_back(stream_mid, norm_gains[1], grad_normed, grad_stream)
    grad_self = gather_rows(grad_stream.astype(jnp.bfloat16))
    grad_self_out = weight_grad(grad_self, mixed_one)
    grad_mixed_one = to_heads(grad_self, self_out).astype(jnp.bfloat16)
    grad_bias, self_grads = attend_backward(
        query_one,
        key_one,
        value_one,
        dec_segments,
        dec_segments,
        True,
        self_bias,
        log_one,
        grad_mixed_one,
    )
    grad_query_one, grad_key_one, grad_value_one = self_grads
    grad_self_query = weight_grad(gathered_one, grad_query_one)
    grad_self_key = weight_grad(gathered_one, grad_key_one)
    grad_self_value = weight_grad(gathered_one, grad_value_one)
    input_terms = (
        from_heads(grad_query_one, self_query)
        + from_heads(grad_key_one, self_key)
        + from_heads(grad_value_one, self_value)
    )
    grad_normed = sum_rows(input_terms)
    grad_stream, gain_one = norm_back(stream_in, norm_gains[0], grad_normed, grad_stream)
    distance_sums = diagonal_sums(grad_bias)
    table_here = jnp.dot(one_hot.T, distance_sums, precision=highest)
    table_full = jnp.zeros((bucket_count, heads_here * lax.axis_size("mp")), jnp.float32)
    table_full = lax.dynamic_update_slice(
        table_full, table_here, (jnp.int32(0), lax.axis_index("mp") * heads_here)
    )
    gain_grads = jnp.stack([gain_one, gain_two, gain_three])
    gain_total, table_total = lax.psum((gain_grads, table_full), ("dp", "mp"))
    summed = (
        lax.psum_scatter(grad_self_query, "dp", scatter_dimension=0, tiled=True),
        lax.psum_scatter(grad_self_key, "dp", scatter_dimension=0, tiled=True),
        lax.psum_scatter(grad_self_value, "dp", scatter_dimension=0, tiled=True),
        lax.psum_scatter(grad_self_out, "dp", scatter_dimension=0, tiled=True),
        lax.psum_scatter(grad_cross_query, "dp", scatter_dimension=0, tiled=True),
        lax.psum_scatter(grad_cross_key, "dp", scatter_dimension=0, tiled=True),
        lax.psum_scatter(grad_cross_value, "dp", scatter_dimension=0, tiled=True),
        lax.psum_scatter(grad_cross_out, "dp", scatter_dimension=0, tiled=True),
        lax.psum_scatter(grad_up, "dp", scatter_dimension=0, tiled=True),
        lax.psum_scatter(grad_down, "dp", scatter_dimension=0, tiled=True),
    )
    return (
        result.astype(jnp.bfloat16),
        grad_stream.astype(jnp.bfloat16),
        grad_encoder,
        summed[0],
        summed[1],
        summed[2],
        summed[3],
        summed[4],
        summed[5],
        summed[6],
        summed[7],
        summed[8],
        summed[9],
        gain_total,
        table_total,
    )


def solution(mesh):
    in_specs = (
        P("dp", "mp", None),
        P("dp", "mp", None),
        P("dp", None),
        P("dp", None),
        P(),
        P(),
        P(None, "mp"),
        P(None, "mp"),
        P(None, "mp"),
        P(None, "mp"),
        P(None, "mp"),
        P(None, "mp"),
        P(None, "mp"),
        P(None, "mp"),
        P(None, "mp"),
        P(None, "mp"),
        P(None, "mp"),
        P("dp", "mp", None),
    )
    out_specs = (
        P("dp", "mp", None),
        P("dp", "mp", None),
        P("dp", "mp", None),
        P("dp", "mp"),
        P("dp", "mp"),
        P("dp", "mp"),
        P("dp", "mp"),
        P("dp", "mp"),
        P("dp", "mp"),
        P("dp", "mp"),
        P("dp", "mp"),
        P("dp", "mp"),
        P("dp", "mp"),
        P(),
        P(),
    )
    return jax.shard_map(local, mesh=mesh, in_specs=in_specs, out_specs=out_specs, check_vma=False)
```

profile of v0, /device:TPU:0, one launch (start us, length us, event | category | flops | bytes accessed | tf_op | source)
XLA Modules:
  0.0 1015.0 jit_solution(13265030339387532127)
XLA Ops:
  12.9 10.2 %all_gather.21 = bf16[1,512,768]{2,1,0:T(8,128)(2,1)S(1)} all-gather(bf16[1,128,768]{2,1,0:T(8,128)(2,1)S(1)} %fusion.66), channel_id=1, replica_groups=mesh['dp'=8,'mp'=4] {'mp'}, dimensions={1}, use_global_device_ids=true | all-gather | bytes 983040 | tf_op jit(solution)/shard_map/all_gather | solution.py:46
  40.9 13.2 %reshape.500 = f32[3,512,1023]{2,1,0:T(8,128)} reshape(f32[3,523776]{1,0:T(4,128)} %slice.49) | data formatting | bytes 12570624 | tf_op jit(solution)/shard_map/reshape | solution.py:64
  69.0 8.9 all_gather.22
  79.2 18.9 %reduce-scatter.24.cloned.1.call-done = f32[1,128,768]{2,1,0:T(8,128)} async-done(((f32[1,512,768]{2,1,0:T(8,128)}), f32[1,128,768]{2,1,0:T(8,128)}) %reduce-scatter.24.cloned.1.call-update) | async-done | bytes 393232 | tf_op jit(solution)/shard_map/reduce_scatter | solution.py:50
  99.3 8.4 all_gather.23
  113.3 8.7 all_gather.25
  122.1 19.9 %reduce-scatter.26.cloned.1.call-done = f32[1,128,768]{2,1,0:T(8,128)} async-done(((f32[1,512,768]{2,1,0:T(8,128)}), f32[1,128,768]{2,1,0:T(8,128)}) %reduce-scatter.26.cloned.1.call-update) | async-done | bytes 393232 | tf_op jit(solution)/shard_map/reduce_scatter | solution.py:50
  143.2 8.2 all_gather.24
  158.1 28.0 %reduce-scatter.30.cloned.1.call-done = f32[1,128,768]{2,1,0:T(8,128)} async-done(((f32[1,512,768]{2,1,0:T(8,128)}), f32[1,128,768]{2,1,0:T(8,128)}) %reduce-scatter.30.cloned.1.call-update) | async-done | bytes 393232 | tf_op jit(solution)/shard_map/reduce_scatter | solution.py:50
  189.9 8.2 all_gather.26
  210.0 23.9 %reduce-scatter.32.cloned.1.call-done = f32[1,128,768]{2,1,0:T(8,128)} async-done(((f32[1,512,768]{2,1,0:T(8,128)}), f32[1,128,768]{2,1,0:T(8,128)}) %reduce-scatter.32.cloned.1.call-update) | async-done | bytes 393232 | tf_op jit(solution)/shard_map/reduce_scatter | solution.py:50
  236.8 27.6 %reduce-scatter.28.cloned.1.call-done = f32[1,128,768]{2,1,0:T(8,128)} async-done(((f32[1,512,768]{2,1,0:T(8,128)}), f32[1,128,768]{2,1,0:T(8,128)}) %reduce-scatter.28.cloned.1.call-update) | async-done | bytes 393232 | tf_op jit(solution)/shard_map/reduce_scatter | solution.py:50
  267.1 8.4 all_gather.27
  343.7 40.3 %all-reduce.2 = (f32[3,768]{1,0:T(4,128)}, f32[32,12]{0,1:T(8,128)}) all-reduce(f32[3,768]{1,0:T(4,128)S(1)} %pad_maximum_fusion.1, f32[32,12]{0,1:T(8,128)S(1)} %dynamic_update_slice.25), channel_id=1, replica_groups=mesh['dp'=8,'mp'=4] {'dp','mp'}, use_global_device_ids=true, to_apply=%region_32.33 | all-reduce | flops 2688 | bytes 21504 | tf_op jit(solution)/shard_map/psum | solution.py:289
  385.9 58.9 %reduce-scatter.54.cloned.1.call-done = f32[96,192]{1,0:T(8,128)} async-done(((f32[768,192]{1,0:T(8,128)}), f32[96,192]{1,0:T(8,128)}) %reduce-scatter.54.cloned.1.call-update) | async-done | bytes 73744
  444.8 65.3 %reduce-scatter.46.cloned.1.call-done = f32[96,192]{1,0:T(8,128)} async-done(((f32[768,192]{1,0:T(8,128)}), f32[96,192]{1,0:T(8,128)}) %reduce-scatter.46.cloned.1.call-update) | async-done | bytes 73744 | tf_op jit(solution)/shard_map/reduce_scatter | solution.py:295
  510.0 65.6 %reduce-scatter.52.cloned.1.call-done = f32[96,192]{1,0:T(8,128)} async-done(((f32[768,192]{1,0:T(8,128)}), f32[96,192]{1,0:T(8,128)}) %reduce-scatter.52.cloned.1.call-update) | async-done | bytes 73744
  575.6 72.2 %reduce-scatter.56.cloned.1.call-done = f32[96,768]{1,0:T(8,128)} async-done(((f32[768,768]{1,0:T(8,128)}), f32[96,768]{1,0:T(8,128)}) %reduce-scatter.56.cloned.1.call-update) | async-done | bytes 294928
  647.8 72.2 %reduce-scatter.50.cloned.1.call-done = f32[96,768]{1,0:T(8,128)} async-done(((f32[768,768]{1,0:T(8,128)}), f32[96,768]{1,0:T(8,128)}) %reduce-scatter.50.cloned.1.call-update) | async-done | bytes 294928 | tf_op jit(solution)/shard_map/reduce_scatter | solution.py:299
  720.0 25.4 %reduce-scatter.36.cloned.1.call-done = bf16[1,128,768]{2,1,0:T(8,128)(2,1)} async-done(((bf16[1,512,768]{2,1,0:T(8,128)(2,1)}), bf16[1,128,768]{2,1,0:T(8,128)(2,1)}) %reduce-scatter.36.cloned.1.call-update) | async-done | bytes 196624 | tf_op jit(solution)/shard_map/reduce_scatter | solution.py:253
  745.4 66.6 %reduce-scatter.44.cloned.1.call-done = f32[96,192]{1,0:T(8,128)} async-done(((f32[768,192]{1,0:T(8,128)}), f32[96,192]{1,0:T(8,128)}) %reduce-scatter.44.cloned.1.call-update) | async-done | bytes 73744 | tf_op jit(solution)/shard_map/reduce_scatter | solution.py:294
  812.0 65.3 %reduce-scatter.42.cloned.1.call-done = f32[96,192]{1,0:T(8,128)} async-done(((f32[768,192]{1,0:T(8,128)}), f32[96,192]{1,0:T(8,128)}) %reduce-scatter.42.cloned.1.call-update) | async-done | bytes 73744 | tf_op jit(solution)/shard_map/reduce_scatter | solution.py:293
  877.3 65.6 %reduce-scatter.40.cloned.1.call-done = f32[96,192]{1,0:T(8,128)} async-done(((f32[768,192]{1,0:T(8,128)}), f32[96,192]{1,0:T(8,128)}) %reduce-scatter.40.cloned.1.call-update) | async-done | bytes 73744 | tf_op jit(solution)/shard_map/reduce_scatter | solution.py:292
  942.9 65.2 %reduce-scatter.38.cloned.1.call-done = f32[96,192]{1,0:T(8,128)} async-done(((f32[768,192]{1,0:T(8,128)}), f32[96,192]{1,0:T(8,128)}) %reduce-scatter.38.cloned.1.call-update) | async-done | bytes 73744 | tf_op jit(solution)/shard_map/reduce_scatter | solution.py:291
  (333 shorter events, 144.5 us)
Async XLA Ops:
  7.2 144.2 %copy-start = (bf16[768,768]{1,0:T(8,128)(2,1)S(1)}, bf16[768,768]{1,0:T(8,128)(2,1)}, u32[]{:S(2)}) copy-start(bf16[768,768]{1,0:T(8,128)(2,1)} %param.33) | copy-start | bytes 3538948
  7.2 90.8 %reduce-scatter.24.cloned.1.call-start = ((), (), s32[]{:S(2)}) async-start(), calls=%async_computation.17 | async-start | bytes 1966080 | tf_op jit(solution)/shard_map/reduce_scatter | solution.py:50
  11.8 87.4 %copy-start.77 = (f32[768]{0:T(1024)}, f32[768]{0:T(1024)S(1)}, u32[]{:S(2)}) copy-start(f32[768]{0:T(1024)S(1)} %get-tuple-element.185) | copy-start | bytes 9220
  11.8 176.1 %copy-start.71 = (f32[768]{0:T(1024)}, f32[768]{0:T(1024)S(1)}, u32[]{:S(2)}) copy-start(f32[768]{0:T(1024)S(1)} %get-tuple-element.183) | copy-start | bytes 9220
  68.9 73.0 %reduce-scatter.26.cloned.1.call-start = ((), (), s32[]{:S(2)}) async-start(), calls=%async_computation.18 | async-start | bytes 1966080 | tf_op jit(solution)/shard_map/reduce_scatter | solution.py:50
  113.3 72.9 %reduce-scatter.30.cloned.1.call-start = ((), (), s32[]{:S(2)}) async-start(), calls=%async_computation.20 | async-start | bytes 1966080 | tf_op jit(solution)/shard_map/reduce_scatter | solution.py:50
  143.1 44.8 %copy-start.84 = (f32[128]{0:T(128)}, f32[128]{0:T(128)S(1)}, u32[]{:S(2)}) copy-start(f32[128]{0:T(128)S(1)} %fusion.83) | copy-start | bytes 1540
  157.4 76.5 %reduce-scatter.32.cloned.1.call-start = ((), (), s32[]{:S(2)}) async-start(), calls=%async_computation.21 | async-start | bytes 1966080 | tf_op jit(solution)/shard_map/reduce_scatter | solution.py:50
  205.1 59.3 %reduce-scatter.28.cloned.1.call-start = ((), (), s32[]{:S(2)}) async-start(), calls=%async_computation.19 | async-start | bytes 1966080 | tf_op jit(solution)/shard_map/reduce_scatter | solution.py:50
  209.2 133.3 %reduce-scatter.34.cloned.1.call-start = ((), (), s32[]{:S(2)}) async-start(), calls=%async_computation.22 | async-start | bytes 1966080 | tf_op jit(solution)/shard_map/reduce_scatter | solution.py:50
  283.7 102.2 %reduce-scatter.48.cloned.1.call-start = ((), (), s32[]{:S(2)}) async-start(), calls=%async_computation.29 | async-start | bytes 884736 | tf_op jit(solution)/shard_map/reduce_scatter | solution.py:298
  286.3 158.5 %reduce-scatter.54.cloned.1.call-start = ((), (), s32[]{:S(2)}) async-start(), calls=%async_computation.32 | async-start | bytes 884736
  289.2 220.9 %reduce-scatter.46.cloned.1.call-start = ((), (), s32[]{:S(2)}) async-start(), calls=%async_computation.28 | async-start | bytes 884736 | tf_op jit(solution)/shard_map/reduce_scatter | solution.py:295
  290.6 285.1 %reduce-scatter.52.cloned.1.call-start = ((), (), s32[]{:S(2)}) async-start(), calls=%async_computation.31 | async-start | bytes 884736
  293.3 354.5 %reduce-scatter.56.cloned.1.call-start = ((), (), s32[]{:S(2)}) async-start(), calls=%async_computation.33 | async-start | bytes 2654208
  297.9 422.1 %reduce-scatter.50.cloned.1.call-start = ((), (), s32[]{:S(2)}) async-start(), calls=%async_computation.30 | async-start | bytes 2654208 | tf_op jit(solution)/shard_map/reduce_scatter | solution.py:299
  301.5 443.9 %reduce-scatter.36.cloned.1.call-start = ((), (), s32[]{:S(2)}) async-start(), calls=%async_computation.23 | async-start | bytes 983040 | tf_op jit(solution)/shard_map/reduce_scatter | solution.py:253
  304.2 507.8 %reduce-scatter.44.cloned.1.call-start = ((), (), s32[]{:S(2)}) async-start(), calls=%async_computation.27 | async-start | bytes 884736 | tf_op jit(solution)/shard_map/reduce_scatter | solution.py:294
  305.6 571.7 %reduce-scatter.42.cloned.1.call-start = ((), (), s32[]{:S(2)}) async-start(), calls=%async_computation.26 | async-start | bytes 884736 | tf_op jit(solution)/shard_map/reduce_scatter | solution.py:293
  307.0 635.9 %reduce-scatter.40.cloned.1.call-start = ((), (), s32[]{:S(2)}) async-start(), calls=%async_computation.25 | async-start | bytes 884736 | tf_op jit(solution)/shard_map/reduce_scatter | solution.py:292
  326.5 681.6 %reduce-scatter.38.cloned.1.call-start = ((), (), s32[]{:S(2)}) async-start(), calls=%async_computation.24 | async-start | bytes 884736 | tf_op jit(solution)/shard_map/reduce_scatter | solution.py:291
  334.6 49.4 %copy-start.92 = (f32[128]{0:T(128)S(1)}, f32[128]{0:T(128)}, u32[]{:S(2)}) copy-start(f32[128]{0:T(128)} %copy-done.91) | copy-start | bytes 1540
  334.6 49.4 %copy-start.44 = (f32[1,128,768]{2,1,0:T(8,128)S(1)}, f32[1,128,768]{2,1,0:T(8,128)}, u32[]{:S(2)}) copy-start(f32[1,128,768]{2,1,0:T(8,128)} %get-tuple-element.189) | copy-start | bytes 1179652
  334.6 673.4 %copy-start.1 = (bf16[768,768]{1,0:T(8,128)(2,1)S(1)}, bf16[768,768]{1,0:T(8,128)(2,1)}, u32[]{:S(2)}) copy-start(bf16[768,768]{1,0:T(8,128)(2,1)} %param.33) | copy-start | bytes 3538948
  (91 other events, 622.9 us)
Sparse Core Ops, SparseCore 0:
  69.0 29.0 reduce-scatter.23
  113.4 28.5 reduce-scatter.25
  157.5 28.5 reduce-scatter.29
  205.2 28.5 reduce-scatter.31
  236.2 28.1 reduce-scatter.27
  283.8 28.5 reduce-scatter.33
  316.3 62.6 reduce-scatter.47
  383.2 61.4 reduce-scatter.53
  448.6 61.3 reduce-scatter.45
  514.1 61.4 reduce-scatter.51
  579.7 68.0 reduce-scatter.55
  651.8 68.1 reduce-scatter.49
  723.1 22.2 reduce-scatter.35
  749.5 62.4 reduce-scatter.43
  815.7 61.5 reduce-scatter.41
  881.4 61.4 reduce-scatter.39
  946.6 61.3 reduce-scatter.37
where the time goes:
time: 1020 us
  waiting for transfers between devices  741 us (73%)
  blocking collectives  101 us (10%)
  local copies, waits for them, and re-layouts  75.9 us (7%)
  matrix products  46.9 us (5%)
  other arithmetic  33.7 us (3%)
  between operations  15.6 us (2%)
    unnamed x20, waiting for transfers between devices  197 us
    reduce_scatter x6, waiting for transfers between devices, sum_rows(): return lax.psum_scatter(partial_sum, 'mp', scatter_dimension=1, tiled=True)  118 us
    reduce_scatter x1, waiting for transfers between devices, local(): lax.psum_scatter(grad_up, 'dp', scatter_dimension=0, tiled=True)  72.2 us
    reduce_scatter x1, waiting for transfers between devices, local(): lax.psum_scatter(grad_self_out, 'dp', scatter_dimension=0, tiled=True)  66.6 us
    reduce_scatter x1, waiting for transfers between devices, local(): lax.psum_scatter(grad_self_key, 'dp', scatter_dimension=0, tiled=True)  65.6 us
    reduce_scatter x1, waiting for transfers between devices, local(): lax.psum_scatter(grad_self_value, 'dp', scatter_dimension=0, tiled=True)  65.3 us
    reduce_scatter x1, waiting for transfers between devices, local(): lax.psum_scatter(grad_cross_query, 'dp', scatter_dimension=0, tiled=True)  65.3 us
    reduce_scatter x1, waiting for transfers between devices, local(): lax.psum_scatter(grad_self_query, 'dp', scatter_dimension=0, tiled=True)  65.2 us
  transfers between devices with their start and end apart: 17, of which 15 were waited for; matrix products, arithmetic and copies ran while one was open for 6% of the time, Pallas kernels for 0%

commit v1 on v0

v1 whole, which is shorter than its diff:
```python
import functools

import jax
import jax.numpy as jnp
from jax import lax
from jax.experimental import pallas as pl
from jax.experimental.pallas import tpu as pltpu
from jax.sharding import PartitionSpec as P

HEAD_DIM = 64
epsilon = 1e-06
key_scale = 0.125
masked_score = -1e30
highest = lax.Precision.HIGHEST
bf16 = jnp.bfloat16
f32 = jnp.float32


def dot(a, b):
    return lax.dot_general(a, b, (((1,), (0,)), ((), ())), preferred_element_type=f32)


def dot_nt(a, b):
    return lax.dot_general(a, b, (((1,), (1,)), ((), ())), preferred_element_type=f32)


def dot_tn(a, b):
    return lax.dot_general(a, b, (((0,), (0,)), ((), ())), preferred_element_type=f32)


def norm_parts(rows):
    inv = lax.rsqrt(jnp.mean(rows * rows, axis=-1, keepdims=True) + epsilon)
    return rows * inv, inv


def norm_back(rows, gain, grad):
    unit, inv = norm_parts(rows)
    grad_unit = grad * gain
    grad_rows = inv * (grad_unit - unit * jnp.mean(grad_unit * unit, axis=-1, keepdims=True))
    return grad_rows, jnp.sum(grad * unit, axis=0, keepdims=True)


def at(index, size):
    return pl.ds(pl.multiple_of(index * size, size), size)


def kernel_call(body, name, outs, *args, scratch=(), limit=40):
    specs = [pl.BlockSpec(memory_space=pltpu.SMEM)]
    specs += [pl.BlockSpec(memory_space=pltpu.VMEM)] * (len(args) - 1)
    moved = sum(v.size * v.dtype.itemsize for v in args)
    moved += sum(v.size * v.dtype.itemsize for v in outs)
    return pl.pallas_call(
        body,
        out_shape=outs,
        in_specs=specs,
        out_specs=[pl.BlockSpec(memory_space=pltpu.VMEM)] * len(outs),
        scratch_shapes=list(scratch),
        compiler_params=pltpu.CompilerParams(vmem_limit_bytes=limit * 1024 * 1024),
        cost_estimate=pl.CostEstimate(flops=moved * 400, bytes_accessed=moved, transcendentals=0),
        name=name,
    )(*args)


def shape(dims, dtype=bf16):
    return jax.ShapeDtypeStruct(dims, dtype)


def head_masks(width, dtype):
    lane = lax.broadcasted_iota(jnp.int32, (1, width), 1) // HEAD_DIM
    return [(lane == h).astype(f32).astype(dtype) for h in range(width // HEAD_DIM)]


def bias_body(idx, u_ref, segc_ref, segr_ref, enc_ref, bias_ref, cross_ref, *, Q):
    core = idx[1]
    L = 4 * Q
    heads = bias_ref.shape[0]
    order = (core, 2 + core, 1 - core, 3 - core)
    enc = jnp.concatenate([enc_ref[:, at(o, Q)] for o in order], axis=1)
    for b in range(2):
        own = at(2 * b + core, Q)
        segc = segc_ref[own, :]
        rows = pl.ds(b * Q, Q)
        cross_ref[rows, :] = jnp.where(segc == enc, 0.0, masked_score)
        place = (2 * b + core) * Q + lax.broadcasted_iota(jnp.int32, (Q, L), 0)
        col = lax.broadcasted_iota(jnp.int32, (Q, L), 1)
        allowed = (segc == segr_ref[...]) & (col <= place)
        turned = pltpu.roll(u_ref[...], (2 * b + core) * Q, 1)
        for h in range(heads):
            line = jnp.broadcast_to(turned[h : h + 1, :], (Q, L))
            line = pltpu.roll(line, 0, 1, stride=1, stride_axis=0)
            bias_ref[h, rows, :] = jnp.where(allowed, line, masked_score)


def soft_mix(q, k, v, extra, masks, masks_f, p_ref, first, rows, nk):
    mixed = None
    for h in range(len(masks)):
        s = dot_nt(q * masks[h], k) * key_scale + extra(h)
        top = jnp.max(s, axis=-1, keepdims=True)
        e = jnp.exp(s - top)
        p = (e * (1.0 / jnp.sum(e, axis=-1, keepdims=True))).astype(bf16)
        p_ref[first + h, rows, pl.ds(0, nk)] = p
        term = dot(p, v) * masks_f[h]
        mixed = term if mixed is None else mixed + term
    return mixed.astype(bf16)


def self_forward(idx, x_ref, g_ref, wo_ref, wp_ref, bias_ref, part_ref, h_ref, q_ref, k_ref, v_ref, p_ref, o_ref, *, Q):
    core = idx[1]
    L = 4 * Q
    W = wo_ref.shape[2]
    heads = W // HEAD_DIM
    masks, masks_f = head_masks(W, bf16), head_masks(W, f32)
    gain = g_ref[0:1, :]
    for t in range(4):
        rows = pl.ds(t * Q, Q)
        unit, _ = norm_parts(x_ref[rows, :].astype(f32))
        h_ref[rows, :] = (unit * gain).astype(bf16)
    ws = (wo_ref, wp_ref)
    for grp in range(2):
        k_ref[grp] = dot(h_ref[...], ws[grp][1]).astype(bf16)
        v_ref[grp] = dot(h_ref[...], ws[grp][2]).astype(bf16)
    for b in range(2):
        hb = h_ref[at(2 * b + core, Q), :]
        nk = 2 * Q * (b + 1)
        rows = pl.ds(b * Q, Q)
        part = None
        for grp in range(2):
            q = dot(hb, ws[grp][0]).astype(bf16)
            q_ref[grp, rows, :] = q
            mixed = soft_mix(
                q,
                k_ref[grp, pl.ds(0, nk), :],
                v_ref[grp, pl.ds(0, nk), :],
                lambda h: bias_ref[grp * heads + h, rows, pl.ds(0, nk)],
                masks,
                masks_f,
                p_ref,
                grp * heads,
                rows,
                nk,
            )
            o_ref[grp, rows, :] = mixed
            term = dot_nt(mixed, ws[grp][3])
            part = term if part is None else part + term
        part_ref[rows, :] = part.astype(bf16)
    for i in range(2 * heads):
        p_ref[i, pl.ds(0, Q), pl.ds(2 * Q, 2 * Q)] = jnp.zeros((Q, 2 * Q), bf16)


def encoder_keys(idx, eo_ref, ep_ref, wo_ref, wp_ref, k_ref, v_ref, *, Q):
    for grp, w in enumerate((wo_ref, wp_ref)):
        for half, e in enumerate((eo_ref, ep_ref)):
            rows = pl.ds(half * 2 * Q, 2 * Q)
            k_ref[grp, rows, :] = dot(e[...], w[1]).astype(bf16)
            v_ref[grp, rows, :] = dot(e[...], w[2]).astype(bf16)


def cross_forward(idx, x_ref, part_ref, recv_ref, g_ref, wo_ref, wp_ref, k_ref, v_ref, mask_ref, out_ref, x1_ref, h_ref, q_ref, p_ref, o_ref, *, Q):
    core = idx[1]
    W = wo_ref.shape[2]
    heads = W // HEAD_DIM
    masks, masks_f = head_masks(W, bf16), head_masks(W, f32)
    ws = (wo_ref, wp_ref)
    for b in range(2):
        rows = pl.ds(b * Q, Q)
        x1 = x_ref[at(2 * b + core, Q), :].astype(f32) + (
            part_ref[rows, :].astype(f32) + recv_ref[rows, :].astype(f32)
        )
        x1_ref[rows, :] = x1
        unit, _ = norm_parts(x1)
        hb = (unit * g_ref[1:2, :]).astype(bf16)
        h_ref[rows, :] = hb
        part = None
        for grp in range(2):
            q = dot(hb, ws[grp][0]).astype(bf16)
            q_ref[grp, rows, :] = q
            mixed = soft_mix(
                q, k_ref[grp], v_ref[grp], lambda h: mask_ref[rows, :], masks, masks_f, p_ref, grp * heads, rows, 4 * Q
            )
            o_ref[grp, rows, :] = mixed
            term = dot_nt(mixed, ws[grp][3])
            part = term if part is None else part + term
        out_ref[rows, :] = part.astype(bf16)


gelu_c = 0.7978845608028654
gelu_k = 0.044715


def ffn_both(idx, x1_ref, part_ref, recv_ref, g_ref, uo_ref, up_ref, do_ref, dp_ref, gr_ref, out_ref, x2_ref, a_ref, du_ref, send_ref, *, Q):
    for b in range(2):
        rows = pl.ds(b * Q, Q)
        x2 = x1_ref[rows, :] + (part_ref[rows, :].astype(f32) + recv_ref[rows, :].astype(f32))
        x2_ref[rows, :] = x2
        unit, _ = norm_parts(x2)
        send_ref[0, rows, :] = (unit * g_ref[2:3, :]).astype(bf16)
    for grp, (up, down) in enumerate(((uo_ref, do_ref), (up_ref, dp_ref))):
        u = dot(send_ref[0], up[...])
        t = jnp.tanh(gelu_c * (u + gelu_k * (u * u * u)))
        half = 0.5 * (1.0 + t)
        a = (u * half).astype(bf16)
        slope = half + 0.5 * u * (1.0 - t * t) * (gelu_c * (1.0 + 3.0 * gelu_k * (u * u)))
        du = (dot(gr_ref[...], down[...]) * slope).astype(bf16)
        if grp == 0:
            a_ref[...] = a
            du_ref[...] = du
        else:
            send_ref[1] = a
            send_ref[2] = du
    out_ref[...] = (dot_nt(du_ref[...], uo_ref[...]) + dot_nt(send_ref[2], up_ref[...])).astype(bf16)


def ffn_out(idx, a_ref, send_ref, do_ref, dp_ref, keep_ref, out_ref, sum_ref, *, Q):
    y = idx[0]
    sum_ref[...] = dot_nt(a_ref[...], do_ref[...]) + dot_nt(send_ref[1], dp_ref[...])
    keep_ref[...] = sum_ref[at(y, Q), :]
    out_ref[...] = sum_ref[at(1 - y, Q), :].astype(bf16)


def output_body(idx, x2_ref, keep_ref, recv_ref, out_ref, *, Q):
    out_ref[...] = (x2_ref[at(idx[0], Q), :] + (keep_ref[...] + recv_ref[...].astype(f32))).astype(bf16)


def attend_back(q, k, v, go, p_ref, ds_ref, first, rows, nk, masks, masks_f):
    grad_q = None
    for h in range(len(masks)):
        p = p_ref[first + h, rows, pl.ds(0, nk)].astype(f32)
        gp = dot_nt(go * masks[h], v)
        ds = (p * (gp - jnp.sum(p * gp, axis=-1, keepdims=True))).astype(bf16)
        ds_ref[first + h, rows, pl.ds(0, nk)] = ds
        term = dot(ds, k) * masks_f[h]
        grad_q = term if grad_q is None else grad_q + term
    return (grad_q * key_scale).astype(bf16)


def cross_back(idx, gr_ref, part_ref, recv_ref, x2_ref, g_ref, wo_ref, wp_ref, k_ref, v_ref, p_ref, h2_ref, out_ref, dx_ref, sendh_ref, do_ref, ds_ref, dqo_ref, dqp_ref, gain_ref, *, Q):
    W = wo_ref.shape[2]
    heads = W // HEAD_DIM
    masks, masks_f = head_masks(W, bf16), head_masks(W, f32)
    ws = (wo_ref, wp_ref)
    sendh_ref[1] = h2_ref[...]
    total = None
    for b in range(2):
        rows = pl.ds(b * Q, Q)
        dh = part_ref[rows, :].astype(f32) + recv_ref[rows, :].astype(f32)
        grad_rows, grad_gain = norm_back(x2_ref[rows, :], g_ref[2:3, :], dh)
        dx = gr_ref[rows, :].astype(f32) + grad_rows
        dx_ref[rows, :] = dx
        total = grad_gain if total is None else total + grad_gain
        gc = dx.astype(bf16)
        sendh_ref[0, rows, :] = gc
        part = None
        for grp in range(2):
            go = dot(gc, ws[grp][3]).astype(bf16)
            do_ref[grp, rows, :] = go
            dq = attend_back(
                None, k_ref[grp], v_ref[grp], go, p_ref, ds_ref, grp * heads, rows, 4 * Q, masks, masks_f
            )
            if grp == 0:
                dqo_ref[rows, :] = dq
            else:
                dqp_ref[rows, :] = dq
            term = dot_nt(dq, ws[grp][0])
            part = term if part is None else part + term
        out_ref[rows, :] = part.astype(bf16)
    gain_ref[...] = jnp.broadcast_to(total * 0.5, gain_ref.shape)


def key_grads(ds_ref, p_ref, q_ref, do_ref, grp, heads, masks):
    first = grp * heads
    n, m = ds_ref.shape[1:]
    q, go = q_ref[grp], do_ref[grp]
    qs = jnp.concatenate([q * masks[h] for h in range(heads)], axis=0)
    gs = jnp.concatenate([go * masks[h] for h in range(heads)], axis=0)
    ds = ds_ref[first : first + heads].reshape(heads * n, m)
    p = p_ref[first : first + heads].reshape(heads * n, m)
    return dot_tn(ds, qs) * key_scale, dot_tn(p, gs)


def keys_body(idx, ds_ref, p_ref, q_ref, do_ref, dqp_ref, o_ref, dk_ref, dv_ref, send_ref, *, Q):
    W = q_ref.shape[2]
    heads = W // HEAD_DIM
    masks = head_masks(W, bf16)
    dk, dv = key_grads(ds_ref, p_ref, q_ref, do_ref, 0, heads, masks)
    dk_ref[...] = dk
    dv_ref[...] = dv
    dk, dv = key_grads(ds_ref, p_ref, q_ref, do_ref, 1, heads, masks)
    send_ref[pl.ds(0, 2 * Q), :] = dqp_ref[...]
    send_ref[pl.ds(2 * Q, 4 * Q), :] = dk.astype(bf16)
    send_ref[pl.ds(6 * Q, 4 * Q), :] = dv.astype(bf16)
    send_ref[pl.ds(10 * Q, 2 * Q), :] = o_ref[1]


def self_back(idx, dx_ref, part_ref, recv_ref, x1_ref, g_ref, wo_ref, wp_ref, k_ref, v_ref, p_ref, q_ref, o_ref, dx1_ref, gs_ref, dqo_ref, dk_ref, dv_ref, send_ref, gain_ref, dist_ref, ds_ref, do_ref, *, Q):
    core = idx[1]
    L = 4 * Q
    W = wo_ref.shape[2]
    heads = W // HEAD_DIM
    masks, masks_f = head_masks(W, bf16), head_masks(W, f32)
    ws = (wo_ref, wp_ref)
    total = None
    for i in range(2 * heads):
        ds_ref[i, pl.ds(0, Q), pl.ds(2 * Q, 2 * Q)] = jnp.zeros((Q, 2 * Q), bf16)
    for b in range(2):
        rows = pl.ds(b * Q, Q)
        nk = 2 * Q * (b + 1)
        dh = part_ref[rows, :].astype(f32) + recv_ref[rows, :].astype(f32)
        grad_rows, grad_gain = norm_back(x1_ref[rows, :], g_ref[1:2, :], dh)
        dx = dx_ref[rows, :] + grad_rows
        dx1_ref[rows, :] = dx
        total = grad_gain if total is None else total + grad_gain
        gs = dx.astype(bf16)
        gs_ref[rows, :] = gs
        for grp in range(2):
            go = dot(gs, ws[grp][3]).astype(bf16)
            do_ref[grp, rows, :] = go
            dq = attend_back(
                None,
                k_ref[grp, pl.ds(0, nk), :],
                v_ref[grp, pl.ds(0, nk), :],
                go,
                p_ref,
                ds_ref,
                grp * heads,
                rows,
                nk,
                masks,
                masks_f,
            )
            if grp == 0:
                dqo_ref[rows, :] = dq
            else:
                send_ref[rows, :] = dq
    gain_ref[...] = jnp.broadcast_to(total * 0.5, gain_ref.shape)
    dk, dv = key_grads(ds_ref, p_ref, q_ref, do_ref, 0, heads, masks)
    dk_ref[...] = dk
    dv_ref[...] = dv
    dk, dv = key_grads(ds_ref, p_ref, q_ref, do_ref, 1, heads, masks)
    send_ref[pl.ds(2 * Q, 4 * Q), :] = dk.astype(bf16)
    send_ref[pl.ds(6 * Q, 4 * Q), :] = dv.astype(bf16)
    send_ref[pl.ds(10 * Q, 2 * Q), :] = o_ref[1]
    for h in range(2 * heads):
        line = ds_ref[h, pl.ds(0, Q), :].astype(f32) + pltpu.roll(
            ds_ref[h, pl.ds(Q, Q), :].astype(f32), L - 2 * Q, 1
        )
        n = Q // 2
        while n >= 1:
            line = line[:n] + pltpu.roll(line[n : 2 * n], L - n, 1)
            n //= 2
        dist_ref[h : h + 1, :] = line
    dist_ref[2 * heads :, :] = jnp.zeros((dist_ref.shape[0] - 2 * heads, L), f32)
    dist_ref[...] = pltpu.roll(dist_ref[...], (4 - core) * Q, 1)


def self_weights(idx, h_ref, gs_ref, gsr_ref, o_ref, dqo_ref, dk_ref, dv_ref, recv_ref, w_ref, g_ref, *rest, Q, split):
    core = idx[1]
    if split:
        keep_ref, send_ref, dq_ref, dkf_ref, dvf_ref, gain_ref, sum_ref, d_ref = rest
    else:
        sum_ref, dq_ref, dkf_ref, dvf_ref, gain_ref, d_ref = rest
    W = dqo_ref.shape[1]
    for b in range(2):
        rows = pl.ds(b * Q, Q)
        dq_ref[at(2 * b + core, Q), :] = dqo_ref[rows, :]
        dq_ref[at(2 * b + 1 - core, Q), :] = recv_ref[rows, :]
    dkf_ref[...] = (dk_ref[...] + recv_ref[pl.ds(2 * Q, 4 * Q), :].astype(f32)).astype(bf16)
    dvf_ref[...] = (dv_ref[...] + recv_ref[pl.ds(6 * Q, 4 * Q), :].astype(f32)).astype(bf16)
    d_ref[:, 0:W] = dq_ref[...]
    d_ref[:, W : 2 * W] = dkf_ref[...]
    d_ref[:, 2 * W : 3 * W] = dvf_ref[...]
    sum_ref[:, 0 : 3 * W] = dot_tn(h_ref[...], d_ref[...])
    sum_ref[:, 3 * W : 4 * W] = dot_tn(gs_ref[...], o_ref[0]) + dot_tn(gsr_ref[...], recv_ref[pl.ds(10 * Q, 2 * Q), :])
    prod = None
    for i in range(3):
        term = sum_ref[:, i * W : (i + 1) * W] * w_ref[i].astype(f32)
        prod = term if prod is None else prod + term
    line = lax.dot_general(
        jnp.ones((8, W), f32), prod, (((1,), (1,)), ((), ())), precision=highest, preferred_element_type=f32
    )
    gain_ref[...] = line / g_ref[0:1, :]
    if split:
        split_rows(idx, sum_ref, keep_ref, send_ref)


def split_rows(idx, sum_ref, keep_ref, send_ref):
    x = idx[2]
    n = keep_ref.shape[1]
    for z in range(keep_ref.shape[0]):
        keep_ref[z] = sum_ref[at(2 * z + x, n), :].astype(keep_ref.dtype)
        send_ref[z] = sum_ref[at(2 * z + 1 - x, n), :].astype(send_ref.dtype)


def cross_weights(idx, sendh_ref, recvh_ref, eo_ref, ep_ref, dqo_ref, dk_ref, dv_ref, o_ref, recv_ref, *rest, Q, split):
    if split:
        keep_ref, send_ref, sum_ref = rest
    else:
        (sum_ref,) = rest
    W = dqo_ref.shape[1]
    sum_ref[:, 0:W] = dot_tn(sendh_ref[1], dqo_ref[...]) + dot_tn(recvh_ref[1], recv_ref[pl.ds(0, 2 * Q), :])
    for i, d in enumerate((dk_ref, dv_ref)):
        sum_ref[:, (i + 1) * W : (i + 2) * W] = dot_tn(eo_ref[...], d[pl.ds(0, 2 * Q), :]) + dot_tn(
            ep_ref[...], d[pl.ds(2 * Q, 2 * Q), :]
        )
    sum_ref[:, 3 * W : 4 * W] = dot_tn(sendh_ref[0], o_ref[0]) + dot_tn(recvh_ref[0], recv_ref[pl.ds(10 * Q, 2 * Q), :])
    if split:
        split_rows(idx, sum_ref, keep_ref, send_ref)


def ffn_weights(idx, lo_ref, lr_ref, ro_ref, rr_ref, *rest, Q, split, left, right):
    if split:
        keep_ref, send_ref, sum_ref = rest
    else:
        (sum_ref,) = rest
    lo = lo_ref[...] if left is None else lo_ref[left]
    lr = lr_ref[...] if left is None else lr_ref[left]
    sum_ref[...] = dot_tn(lo, ro_ref[...]) + dot_tn(lr, rr_ref[right])
    if split:
        split_rows(idx, sum_ref, keep_ref, send_ref)


def encoder_grad(idx, dk_ref, dv_ref, recv_ref, w_ref, keep_ref, send_ref, dkf_ref, dvf_ref, *, Q):
    for half, out in enumerate((keep_ref, send_ref)):
        rows = pl.ds(half * 2 * Q, 2 * Q)
        from_k, from_v = pl.ds((4 - 2 * half) * Q, 2 * Q), pl.ds((8 - 2 * half) * Q, 2 * Q)
        dkf_ref[rows, :] = (dk_ref[rows, :] + recv_ref[from_k, :].astype(f32)).astype(bf16)
        dvf_ref[rows, :] = (dv_ref[rows, :] + recv_ref[from_v, :].astype(f32)).astype(bf16)
        out[...] = (dot_nt(dkf_ref[rows, :], w_ref[1]) + dot_nt(dvf_ref[rows, :], w_ref[2])).astype(out.dtype)


def input_grad(idx, dq_ref, dk_ref, dv_ref, w_ref, keep_ref, send_ref, *, Q):
    core = idx[1]
    for b in range(2):
        rows = pl.ds(b * Q, Q)
        for out, place in ((keep_ref, 2 * b + core), (send_ref, 2 * b + 1 - core)):
            take = at(place, Q)
            total = dot_nt(dq_ref[take, :], w_ref[0]) + dot_nt(dk_ref[take, :], w_ref[1])
            out[rows, :] = (total + dot_nt(dv_ref[take, :], w_ref[2])).astype(out.dtype)


def halve_body(idx, keep_ref, recv_ref, own_ref, send_ref, *, Q):
    y = idx[0]
    mine, theirs = at(y, Q), at(1 - y, Q)
    own_ref[...] = keep_ref[mine, :] + recv_ref[mine, :].astype(f32)
    send_ref[...] = (keep_ref[theirs, :] + recv_ref[theirs, :].astype(f32)).astype(bf16)


def add_body(idx, own_ref, recv_ref, out_ref, *, Q):
    out_ref[...] = (own_ref[...] + recv_ref[...].astype(f32)).astype(out_ref.dtype)


def decoder_grad(idx, own_ref, recv_ref, x_ref, dx_ref, g_ref, out_ref, *, Q):
    y, core = idx[0], idx[1]
    dh = own_ref[...] + recv_ref[...].astype(f32)
    grad_rows, _ = norm_back(x_ref[at(2 * y + core, Q), :].astype(f32), g_ref[0:1, :], dh)
    out_ref[...] = (dx_ref[at(y, Q), :] + grad_rows).astype(bf16)


def pair_sum(idx, keep_ref, recv_ref, own_ref, *send_refs):
    z = idx[3]
    own_ref[...] = keep_ref[z].astype(f32) + recv_ref[z].astype(f32)
    for i, out in enumerate(send_refs):
        place = lax.bitwise_xor(z, i + 1)
        out[...] = (keep_ref[place].astype(f32) + recv_ref[place].astype(f32)).astype(bf16)


def last_sum(idx, own_ref, *rest):
    recvs, outs = rest[:3], rest[3:]
    total = own_ref[...]
    for r in recvs:
        total = total + r[...].astype(f32)
    width = outs[0].shape[1]
    for i, out in enumerate(outs):
        out[...] = total[:, i * width : (i + 1) * width]


def local(
    decoder_in,
    encoder_states,
    dec_segments,
    enc_segments,
    offset_buckets,
    norm_gains,
    bias_table,
    self_query,
    self_key,
    self_value,
    self_out,
    cross_query,
    cross_key,
    cross_value,
    cross_out,
    ffn_up,
    ffn_down,
    out_grad,
    dp_size,
):
    Q, D = decoder_in.shape[1:]
    L = 4 * Q
    W = self_query.shape[1]
    F = ffn_up.shape[1]
    heads = bias_table.shape[1]
    buckets = bias_table.shape[0]
    split = dp_size == 8
    mp = lax.axis_index("mp")
    dp = lax.axis_index("dp")
    y, core = mp // 2, mp % 2
    idx = jnp.stack([y, core, dp % 2, dp // 2]).astype(jnp.int32)

    def over_mp(v, flip):
        return lax.ppermute(v, "mp", [(i, i ^ flip) for i in range(4)])

    def over_dp(v, flip):
        return lax.ppermute(v, "dp", [(i, i ^ flip) for i in range(dp_size)])

    def call(body, name, outs, *args, scratch=(), limit=40, **static):
        static["Q"] = Q
        return kernel_call(
            functools.partial(body, **static), name, outs, idx, *args, scratch=scratch, limit=limit
        )

    w_self = jnp.stack([self_query, self_key, self_value, self_out])
    w_cross = jnp.stack([cross_query, cross_key, cross_value, cross_out])
    w_self_p = over_mp(w_self, 1)
    x_full = lax.all_gather(decoder_in[0], "mp", axis=0, tiled=True)
    w_cross_p = over_mp(w_cross, 1)
    up_p = over_mp(ffn_up, 1)
    down_p = over_mp(ffn_down, 1)

    def rows_of_chip(v):
        other = over_mp(v, 2)
        own = jnp.where(y == 0, jnp.concatenate([v, other]), jnp.concatenate([other, v]))
        return own, over_mp(own, 1)

    enc_own, enc_oth = rows_of_chip(encoder_states[0])
    g_own, g_oth = rows_of_chip(out_grad[0])

    turned = jnp.concatenate([offset_buckets[:1], offset_buckets[1:][::-1]])
    one_hot = (turned[:, None] == jnp.arange(buckets)[None, :]).astype(f32)
    table_p = over_mp(bias_table, 1)
    table_both = jnp.concatenate([bias_table, table_p, jnp.zeros((buckets, 8 - 2 * heads), f32)], axis=1)
    by_place = jnp.dot(table_both.T, one_hot.T, precision=highest)
    bias, cross_mask = call(
        bias_body,
        "bias",
        [shape((2 * heads, 2 * Q, L), f32), shape((2 * Q, L), f32)],
        by_place,
        dec_segments.reshape(L, 1),
        dec_segments,
        enc_segments,
    )

    grp_rows, grp_all = shape((2, 2 * Q, W)), shape((2, L, W))
    square = shape((2 * heads, 2 * Q, L))
    half = shape((2 * Q, D))
    half_f = shape((2 * Q, D), f32)
    line = shape((8, D), f32)

    part1, h1, q1, k1, v1, p1, o1 = call(
        self_forward,
        "self_forward",
        [half, shape((L, D)), grp_rows, grp_all, grp_all, square, grp_rows],
        x_full,
        norm_gains,
        w_self,
        w_self_p,
        bias,
    )
    recv1 = over_mp(part1, 2)
    k2, v2 = call(encoder_keys, "encoder_keys", [grp_all, grp_all], enc_own, enc_oth, w_cross, w_cross_p)
    part2, x1, h2, q2, p2, o2 = call(
        cross_forward,
        "cross_forward",
        [half, half_f, half, grp_rows, square, grp_rows],
        x_full,
        part1,
        recv1,
        norm_gains,
        w_cross,
        w_cross_p,
        k2,
        v2,
        cross_mask,
    )
    recv2 = over_mp(part2, 2)
    part3, x2, a_own, du_own, send3 = call(
        ffn_both,
        "ffn_both",
        [half, half_f, shape((2 * Q, F)), shape((2 * Q, F)), shape((3, 2 * Q, D))],
        x1,
        part2,
        recv2,
        norm_gains,
        ffn_up,
        up_p,
        ffn_down,
        down_p,
        g_own,
    )
    recv3 = over_mp(part3, 2)
    recv_ffn = over_mp(send3, 1)
    quarter, quarter_f = shape((Q, D)), shape((Q, D), f32)
    y_keep, y_send = call(
        ffn_out,
        "ffn_out",
        [quarter_f, quarter],
        a_own,
        send3,
        ffn_down,
        down_p,
        scratch=[pltpu.VMEM((2 * Q, D), f32)],
    )
    y_recv = over_mp(y_send, 2)
    (output,) = call(output_body, "output", [quarter], x2, y_keep, y_recv)

    def grad_kernel(body, name, cols, *args, extra=(), scratch=(), **static):
        if split:
            keep = shape((dp_size // 2, D // dp_size, cols))
            outs = [keep, keep, *extra]
            scratch = [pltpu.VMEM((D, cols), f32), *scratch]
        else:
            outs = [shape((D, cols), f32), *extra]
        res = call(body, name, outs, *args, scratch=scratch, split=split, **static)
        return (res[:2], res[2:]) if split else (res[:1], res[1:])

    def reduce_rows(parts, count):
        cols = parts[0].shape[-1]
        if not split:
            total = lax.psum_scatter(parts[0], "dp", scatter_dimension=0, tiled=True)
            return jnp.split(total, count, axis=1)
        keep, send = parts
        n = D // dp_size
        recv = over_dp(send, 1)
        own, *sends = kernel_call(
            pair_sum, "pair_sum", [shape((n, cols), f32)] + [shape((n, cols))] * 3, idx, keep, recv
        )
        recvs = [over_dp(v, 2 * (i + 1)) for i, v in enumerate(sends)]
        return kernel_call(
            last_sum, "last_sum", [shape((n, cols // count), f32)] * count, idx, own, *recvs
        )

    down_parts, _ = grad_kernel(ffn_weights, "down_weights", F, g_own, g_oth, a_own, recv_ffn, left=None, right=1)
    up_parts, _ = grad_kernel(ffn_weights, "up_weights", F, send3, recv_ffn, du_own, recv_ffn, left=0, right=2)
    (grad_down,) = reduce_rows(down_parts, 1)
    (grad_up,) = reduce_rows(up_parts, 1)

    own_cols = shape((2 * Q, W))
    all_f, all_low = shape((L, W), f32), shape((L, W))
    packed = shape((12 * Q, W))
    part4, dx2, send4, do2, ds2, dq2, dq2_p, gain3 = call(
        cross_back,
        "cross_back",
        [half, half_f, shape((2, 2 * Q, D)), grp_rows, square, own_cols, own_cols, line],
        g_own,
        part3,
        recv3,
        x2,
        norm_gains,
        w_cross,
        w_cross_p,
        k2,
        v2,
        p2,
        h2,
    )
    recv4 = over_mp(part4, 2)
    recv_h = over_mp(send4, 1)
    dk2, dv2, send_k = call(keys_body, "cross_keys", [all_f, all_f, packed], ds2, p2, q2, do2, dq2_p, o2)
    recv_k = over_mp(send_k, 1)
    enc_keep, enc_send, dk2_full, dv2_full = call(
        encoder_grad, "encoder_grad", [half_f, half, all_low, all_low], dk2, dv2, recv_k, w_cross
    )
    enc_recv = over_mp(enc_send, 1)
    cross_parts, _ = grad_kernel(
        cross_weights, "cross_weights", 4 * W, send4, recv_h, enc_own, enc_oth, dq2, dk2_full, dv2_full, o2, recv_k
    )
    grad_cq, grad_ck, grad_cv, grad_co = reduce_rows(cross_parts, 4)
    enc_mine, enc_theirs = call(halve_body, "encoder_halve", [quarter_f, quarter], enc_keep, enc_recv)
    enc_last = over_mp(enc_theirs, 2)
    (grad_encoder,) = call(add_body, "encoder_add", [quarter], enc_mine, enc_last)

    dx1, gs, dq1, dk1, dv1, send_s, gain2, dist = call(
        self_back,
        "self_back",
        [half_f, half, own_cols, all_f, all_f, packed, line, shape((8, L), f32)],
        dx2,
        part4,
        recv4,
        x1,
        norm_gains,
        w_self,
        w_self_p,
        k1,
        v1,
        p1,
        q1,
        o1,
        scratch=[pltpu.VMEM((2 * heads, 2 * Q, L), bf16), pltpu.VMEM((2, 2 * Q, W), bf16)],
    )
    recv_s = over_mp(send_s, 1)
    gs_oth = over_mp(gs, 1)
    self_parts, (dq1_full, dk1_full, dv1_full, gain1) = grad_kernel(
        self_weights,
        "self_weights",
        4 * W,
        h1,
        gs,
        gs_oth,
        o1,
        dq1,
        dk1,
        dv1,
        recv_s,
        w_self,
        norm_gains,
        extra=[all_low, all_low, all_low, line],
        scratch=[pltpu.VMEM((L, 3 * W), bf16)],
    )
    grad_sq, grad_sk, grad_sv, grad_so = reduce_rows(self_parts, 4)
    in_keep, in_send = call(input_grad, "input_grad", [half_f, half], dq1_full, dk1_full, dv1_full, w_self)
    in_recv = over_mp(in_send, 1)
    in_mine, in_theirs = call(halve_body, "input_halve", [quarter_f, quarter], in_keep, in_recv)
    in_last = over_mp(in_theirs, 2)
    (grad_decoder,) = call(decoder_grad, "decoder_grad", [quarter], in_mine, in_last, x_full, dx1, norm_gains)

    per_head = jnp.dot(dist, one_hot, precision=highest)
    table = jnp.zeros((4 * heads, buckets), f32)
    table = lax.dynamic_update_slice(table, per_head[:heads], (mp * heads, jnp.int32(0)))
    table = lax.dynamic_update_slice(table, per_head[heads : 2 * heads], ((mp + 1 - 2 * core) * heads, jnp.int32(0)))
    small = jnp.concatenate([gain1[0], gain2[0], gain3[0], table.reshape(-1)]).reshape(-1, 128)
    small = small + over_mp(small, 1)
    small = small + over_mp(small, 2)
    flip = 1
    while flip < dp_size:
        small = small + over_dp(small, flip)
        flip *= 2
    small = small.reshape(-1)
    gain_total = small[: 3 * D].reshape(3, D)
    table_total = small[3 * D :].reshape(4 * heads, buckets).T

    def row(v):
        return v.reshape((1,) + v.shape)

    return (
        row(output),
        row(grad_decoder),
        row(grad_encoder),
        grad_sq,
        grad_sk,
        grad_sv,
        grad_so,
        grad_cq,
        grad_ck,
        grad_cv,
        grad_co,
        grad_up,
        grad_down,
        gain_total,
        table_total,
    )


def solution(mesh):
    rows = P("dp", "mp", None)
    cols = P(None, "mp")
    grads = P("dp", "mp")
    in_specs = (rows, rows, P("dp", None), P("dp", None), P(), P(), cols) + (cols,) * 10 + (rows,)
    out_specs = (rows, rows, rows) + (grads,) * 10 + (P(), P())
    body = functools.partial(local, dp_size=mesh.shape["dp"])
    return jax.shard_map(body, mesh=mesh, in_specs=in_specs, out_specs=out_specs, check_vma=False)
```

time: 1020 us -> 309 us (0.30)
  waiting for transfers between devices: 741 us -> 57.5 us
  blocking collectives: 101 us -> 9.62 us
  Pallas kernels: 0 us -> 86.1 us
  starting transfers between devices: 0.96 us -> 51 us
  matrix products: 46.9 us -> 1.3 us
  other arithmetic: 33.7 us -> 4.26 us
  local copies, waits for them, and re-layouts: 75.9 us -> 94.4 us
  between operations: 15.6 us -> 1.75 us
    reduce_scatter x14 -> x0, waiting for transfers between devices: 544 us -> none  [the longest x6 118 us: sum_rows(): return lax.psum_scatter(partial_sum, 'mp', scatter_dimension=1, tiled=True)]
    unnamed x20 -> x0, waiting for transfers between devices: 197 us -> none
    pallas_call x0 -> x28, Pallas kernels: none -> 86.1 us  [kernel_call(): pl.pallas_call(body, out_shape=outs, in_specs=specs, out_specs=[pl.BlockS...]
    ppermute x0 -> x44, waiting for transfers between devices: none -> 57.5 us  [the longest x19 32.8 us: over_dp(): return lax.ppermute(v, 'dp', [(i, i ^ flip) for i in range(dp_size)])]
    all_gather x7 -> x1, blocking collectives: 61 us -> 9.62 us  [local(): x_full = lax.all_gather(decoder_in[0], 'mp', axis=0, tiled=True)]
    ppermute x0 -> x44, starting transfers between devices: none -> 51 us  [the longest x19 33.4 us: over_dp(): return lax.ppermute(v, 'dp', [(i, i ^ flip) for i in range(dp_size)])]
    dot_general x44 -> x2, matrix products: 46.9 us -> 1.3 us  [the longest x1 0.99 us: local(): per_head = jnp.dot(dist, one_hot, precision=highest)]
    psum x1 -> x0, blocking collectives: 40.3 us -> none  [local(): gain_total, table_total = lax.psum((gain_grads, table_full), ('dp', 'mp'))]
  transfers between devices with their start and end apart: 17 -> 44, of which waited for: 15 -> 9; matrix products, arithmetic and copies ran while one was open for 6% -> 11% of each run, Pallas kernels for 0% -> 26%
where the time goes in v1:
time: 309 us; the launch traced here: 306 us
  local copies, waits for them, and re-layouts  94.4 us (31%)
  Pallas kernels  86.1 us (28%)
  waiting for transfers between devices  57.5 us (19%)
  starting transfers between devices  51 us (17%)
  blocking collectives  9.62 us (3%)
  other arithmetic  4.26 us (1%)
    pallas_call x28, Pallas kernels, kernel_call(): pl.pallas_call(body, out_shape=outs, in_specs=specs, out_specs=[pl.BlockS...  86.1 us
    unnamed x256, local copies, waits for them, and re-layouts  68 us
    ppermute x19, starting transfers between devices, over_dp(): return lax.ppermute(v, 'dp', [(i, i ^ flip) for i in range(dp_size)])  33.4 us
    ppermute x19, waiting for transfers between devices, over_dp(): return lax.ppermute(v, 'dp', [(i, i ^ flip) for i in range(dp_size)])  32.8 us
    ppermute x25, waiting for transfers between devices, over_mp(): return lax.ppermute(v, 'mp', [(i, i ^ flip) for i in range(4)])  24.6 us
    ppermute x25, starting transfers between devices, over_mp(): return lax.ppermute(v, 'mp', [(i, i ^ flip) for i in range(4)])  17.7 us
    all_gather x1, blocking collectives, local(): x_full = lax.all_gather(decoder_in[0], 'mp', axis=0, tiled=True)  9.62 us
    ppermute x4, local copies, waits for them, and re-layouts, over_mp(): return lax.ppermute(v, 'mp', [(i, i ^ flip) for i in range(4)])  8.82 us
  transfers between devices with their start and end apart: 44, of which 9 were waited for; matrix products, arithmetic and copies ran while one was open for 11% of the time, Pallas kernels for 26%

profile of v1, /device:TPU:0, one launch (start us, length us, event | category | flops | bytes accessed | tf_op | source)
XLA Modules:
  0.0 305.9 jit_solution(12398436765951393971)
XLA Ops:
  16.7 9.6 %all-gather = bf16[1,512,768]{2,1,0:T(8,128)(2,1)} all-gather(bf16[1,128,768]{2,1,0:T(8,128)(2,1)S(1)} %copy-done.116), channel_id=2, replica_groups=mesh['dp'=8,'mp'=4] {'mp'}, dimensions={1}, use_global_device_ids=true | all-gather | bytes 983040 | tf_op jit(solution)/shard_map/all_gather | solution.py:524
  40.0 7.9 %self_forward.1 = (bf16[256,768]{1,0:T(8,128)(2,1)}, bf16[512,768]{1,0:T(8,128)(2,1)S(1)}, bf16[2,256,192]{2,1,0:T(8,128)(2,1)S(1)}, bf16[2,512,192]{2,1,0:T(8,1...) custom-call(s32[4]{0:T(128)S(1)} %pad_add_fusion.1.idx, ...), custom_call_target="tpu_custom_call" | custom-call | flops 4093139200 | bytes 10232848 | tf_op jit(solution)/shard_map/self_forward/pallas_call | solution.py:52
  54.8 2.7 copy.63.wp_ref
  61.1 3.6 %collective-permute-done.2.recv_ref = bf16[256,768]{1,0:T(8,128)(2,1)} collective-permute-done((bf16[256,768]{1,0:T(8,128)(2,1)}, bf16[256,768]{1,0:T(8,128)(2,1)}, u32[]{:S(2)}, u32[]{:S(2)}) %collective-permute-start.2) | collective-permute-done | bytes 393248 | tf_op jit(solution)/shard_map/ppermute | solution.py:510
  64.8 7.3 %cross_forward.1 = (bf16[256,768]{1,0:T(8,128)(2,1)S(1)}, f32[256,768]{1,0:T(8,128)S(1)}, bf16[256,768]{1,0:T(8,128)(2,1)S(1)}, bf16[2,256,192]{2,1,0:T(8,128)(2...) custom-call(s32[4]{0:T(128)S(1)} %pad_add_fusion.1.idx, bf16[512,768]{1,0:T(8,128)(2,1)S(1)} %bitcast.30, ...), custom_call_target="tpu_custom_call" | custom-call | flops 3516422400 | bytes 8791056 | tf_op jit(solution)/shard_map/cross_forward/pallas_call | solution.py:52
  76.6 12.8 %collective-permute-done.9 = bf16[128,768]{1,0:T(8,128)(2,1)S(1)} collective-permute-done((bf16[128,768]{1,0:T(8,128)(2,1)S(1)}, bf16[128,768]{1,0:T(8,128)(2,1)S(1)}, u32[]{:S(2)}, u32[]{:S(2)}) %collective-permute-start.9) | collective-permute-done | bytes 196640 | tf_op jit(solution)/shard_map/ppermute | solution.py:510
  89.5 5.1 %ffn_both.1 = (bf16[256,768]{1,0:T(8,128)(2,1)}, f32[256,768]{1,0:T(8,128)S(1)}, bf16[256,768]{1,0:T(8,128)(2,1)S(1)}, bf16[256,768]{1,0:T(8,128)(2,1)S(1)}, bf16[3,256,768]{2,1,0:T(8,128)(2,1)S(1)}) custom-call(s32[4]{0:T(128)S(1)} %pad_add_fusion.1.idx, f32[256,768]{1,0:T(8,128)S(1)} %get-tuple-element.109.x1_ref, ...), custom_call_target="tpu_custom_call" | custom-call | flops 3935852800 | bytes 9839632 | tf_op jit(solution)/shard_map/ffn_both/pallas_call | solution.py:52
  99.8 8.2 %collective-permute-done.11.recv_ref = bf16[256,768]{1,0:T(8,128)(2,1)} collective-permute-done((bf16[256,768]{1,0:T(8,128)(2,1)}, bf16[256,768]{1,0:T(8,128)(2,1)}, u32[]{:S(2)}, u32[]{:S(2)}) %collective-permute-start.11) | collective-permute-done | bytes 393248 | tf_op jit(solution)/shard_map/ppermute | solution.py:510
  116.1 7.1 %cross_back.1 = (bf16[256,768]{1,0:T(8,128)(2,1)}, f32[256,768]{1,0:T(8,128)S(1)}, bf16[2,256,768]{2,1,0:T(8,128)(2,1)S(1)}, bf16[2,256,192]{2,1,0:T(8,128)(2,1)...) custom-call(s32[4]{0:T(128)S(1)} %pad_add_fusion.1.idx, ...), custom_call_target="tpu_custom_call" | custom-call | flops 4417542144 | bytes 11043856 | tf_op jit(solution)/shard_map/cross_back/pallas_call | solution.py:52
  125.9 3.0 ffn_out.1
  129.6 13.3 %cross_keys.1 = (f32[512,192]{1,0:T(8,128)S(1)}, f32[512,192]{1,0:T(8,128)S(1)}, bf16[1536,192]{1,0:T(8,128)(2,1)S(1)}) custom-call(s32[4]{0:T(128)S(1)} %pad_add_fusion.1.idx, bf16[6,256,512]{2,1,0:T(8,128)(2,1)S(1)} %get-tuple-element.140.ds_ref, bf16[6,256,512]{2,1,0:T(8,128)(2,1)S(1)} %copy-done.59, bf16[2,256,192]{2,1,0:T(8,128)(2,1)S(1)} %copy-done.87, ...), custom_call_target="tpu_custom_call" | custom-call | flops 2084051200 | bytes 5210128 | tf_op jit(solution)/shard_map/cross_keys/pallas_call | solution.py:52
  158.5 7.3 %self_back.1 = (f32[256,768]{1,0:T(8,128)S(1)}, bf16[256,768]{1,0:T(8,128)(2,1)}, bf16[256,192]{1,0:T(8,128)(2,1)S(1)}, f32[512,192]{1,0:T(8,128)S(1)}, f32[512,...) custom-call(s32[4]{0:T(128)S(1)} %pad_add_fusion.1.idx, ...), custom_call_target="tpu_custom_call" | custom-call | flops 4070201600 | bytes 10175504 | tf_op jit(solution)/shard_map/self_back/pallas_call | solution.py:52
  198.2 4.3 %self_weights.1 = (bf16[4,96,768]{2,1,0:T(8,128)(2,1)S(1)}, bf16[4,96,768]{2,1,0:T(8,128)(2,1)}, bf16[512,192]{1,0:T(8,128)(2,1)S(1)}, bf16[512,192]{1,0:T(8,128...) custom-call(s32[4]{0:T(128)S(1)} %pad_add_fusion.1.idx, bf16[512,768]{1,0:T(8,128)(2,1)S(1)} %copy-done.67, ...), custom_call_target="tpu_custom_call" | custom-call | flops 2490784000 | bytes 6226960 | tf_op jit(solution)/shard_map/self_weights/pallas_call | solution.py:52
  202.9 2.8 cross_weights.1
  209.2 2.8 up_weights.1
  217.3 16.9 %collective-permute-done.41 = f32[21,128]{1,0:T(8,128)S(1)} collective-permute-done((f32[21,128]{1,0:T(8,128)S(1)}, f32[21,128]{1,0:T(8,128)S(1)}, u32[]{:S(2)}, u32[]{:S(2)}) %collective-permute-start.41) | collective-permute-done | bytes 10784 | tf_op jit(solution)/shard_map/ppermute | solution.py:513
  239.7 2.7 collective-permute-start.43
  253.4 2.7 collective-permute-start.27
  257.6 3.6 %collective-permute-start.32 = (bf16[96,768]{1,0:T(8,128)(2,1)}, bf16[96,768]{1,0:T(8,128)(2,1)}, u32[]{:S(2)}, u32[]{:S(2)}) collective-permute-start(bf16[96,768]{1,0:T(8,128)(2,1)} %get-tuple-element.181), channel_id=1, source_target_pairs={{0,16},{4,20},{8,24},{12,28},{16,0},{20,4},{24,8},{28,12},{1,17},{... | collective-permute-start | bytes 442376 | tf_op jit(solution)/shard_map/ppermute | solution.py:513
  264.9 2.9 collective-permute-done.27.rest_1_
  267.7 6.0 %collective-permute-start.33 = (bf16[96,768]{1,0:T(8,128)(2,1)S(1)}, bf16[96,768]{1,0:T(8,128)(2,1)S(1)}, u32[]{:S(2)}, u32[]{:S(2)}) collective-permute-start(bf16[96,768]{1,0:T(8,128)(2,1)S(1)} %get-tuple-element.182), channel_id=1, source_target_pairs={{0,24},{4,28},{8,16},{12,20},{16,8},{20,12},{24,0},{28,4},{1,25},{... | collective-permute-start | bytes 442376 | tf_op jit(solution)/shard_map/ppermute | solution.py:513
  277.8 2.6 collective-permute-done.32.rest_1_
  289.6 3.5 %collective-permute-done.37.rest_1_ = bf16[96,768]{1,0:T(8,128)(2,1)S(1)} collective-permute-done((bf16[96,768]{1,0:T(8,128)(2,1)S(1)}, bf16[96,768]{1,0:T(8,128)(2,1)S(1)}, u32[]{:S(2)}, u32[]{:S(2)}) %collective-permute-start.37) | collective-permute-done | bytes 147488 | tf_op jit(solution)/shard_map/ppermute | solution.py:513
  299.5 4.8 %collective-permute-done.22.rest_1_ = bf16[96,768]{1,0:T(8,128)(2,1)S(1)} collective-permute-done((bf16[96,768]{1,0:T(8,128)(2,1)S(1)}, bf16[96,768]{1,0:T(8,128)(2,1)S(1)}, u32[]{:S(2)}, u32[]{:S(2)}) %collective-permute-start.22) | collective-permute-done | bytes 147488 | tf_op jit(solution)/shard_map/ppermute | solution.py:513
  (387 shorter events, 160.5 us)
Async XLA Ops:
  5.3 27.7 %collective-permute-start = (bf16[4,768,192]{1,2,0:T(8,128)(2,1)}, bf16[4,768,192]{1,2,0:T(8,128)(2,1)}, u32[]{:S(2)}, u32[]{:S(2)}) collective-permute-start(bf16[4,768,192]{1,2,0:T(8,128)(2,1)} %copy.54), channel_id=1, source_target_pairs={{0,1},{1,0},{2,3},{3,2},{4,5},{5,4},{6,7},{7,6},{8,9},{9,8},{10,11... | collective-permute-start | bytes 3538952 | tf_op jit(solution)/shard_map/ppermute | solution.py:510
  5.8 20.8 %collective-permute-start.1 = (f32[32,3]{0,1:T(4,128)S(1)}, f32[32,3]{0,1:T(4,128)S(1)}, u32[]{:S(2)}, u32[]{:S(2)}) collective-permute-start(f32[32,3]{0,1:T(4,128)S(1)} %copy-done.122), channel_id=1, source_target_pairs={{0,1},{1,0},{2,3},{3,2},{4,5},{5,4},{6,7},{7,6},{8,9},{9,8},{10,11... | collective-permute-start | bytes 1160 | tf_op jit(solution)/shard_map/ppermute | solution.py:510
  12.0 42.8 %collective-permute-start.3 = (bf16[4,768,192]{1,2,0:T(8,128)(2,1)}, bf16[4,768,192]{1,2,0:T(8,128)(2,1)}, u32[]{:S(2)}, u32[]{:S(2)}) collective-permute-start(bf16[4,768,192]{1,2,0:T(8,128)(2,1)} %copy.61), channel_id=1, source_target_pairs={{0,1},{1,0},{2,3},{3,2},{4,5},{5,4},{6,7},{7,6},{8,9},{9,8},{10,11... | collective-permute-start | bytes 3538952 | tf_op jit(solution)/shard_map/ppermute | solution.py:510
  12.5 19.0 %collective-permute-start.4 = (bf16[128,768]{1,0:T(8,128)(2,1)}, bf16[128,768]{1,0:T(8,128)(2,1)}, u32[]{:S(2)}, u32[]{:S(2)}) collective-permute-start(bf16[128,768]{1,0:T(8,128)(2,1)} %bitcast.14), channel_id=1, source_target_pairs={{0,2},{1,3},{2,0},{3,1},{4,6},{5,7},{6,4},{7,5},{8,10},{9,11},{10,... | collective-permute-start | bytes 589832 | tf_op jit(solution)/shard_map/ppermute | solution.py:510
  15.0 74.4 %collective-permute-start.7 = (bf16[768,768]{1,0:T(8,128)(2,1)}, bf16[768,768]{1,0:T(8,128)(2,1)}, u32[]{:S(2)}, u32[]{:S(2)}) collective-permute-start(bf16[768,768]{1,0:T(8,128)(2,1)} %uo_ref.1), channel_id=1, source_target_pairs={{0,1},{1,0},{2,3},{3,2},{4,5},{5,4},{6,7},{7,6},{8,9},{9,8},{10,11... | collective-permute-start | bytes 3538952 | tf_op jit(solution)/shard_map/ppermute | solution.py:510
  26.6 62.9 %collective-permute-start.8 = (bf16[768,768]{1,0:T(8,128)(2,1)}, bf16[768,768]{1,0:T(8,128)(2,1)}, u32[]{:S(2)}, u32[]{:S(2)}) collective-permute-start(bf16[768,768]{1,0:T(8,128)(2,1)} %do_ref.3), channel_id=1, source_target_pairs={{0,1},{1,0},{2,3},{3,2},{4,5},{5,4},{6,7},{7,6},{8,9},{9,8},{10,11... | collective-permute-start | bytes 3538952 | tf_op jit(solution)/shard_map/ppermute | solution.py:510
  32.8 24.7 %collective-permute-start.5 = (bf16[256,768]{1,0:T(8,128)(2,1)S(1)}, bf16[256,768]{1,0:T(8,128)(2,1)}, u32[]{:S(2)}, u32[]{:S(2)}) collective-permute-start(bf16[256,768]{1,0:T(8,128)(2,1)S(1)} %maximum_select_fusion.eo_ref), channel_id=1, source_target_pairs={{0,1},{1,0},{2,3},{3,2},{4,5},{5,4},{6,7},{7,6},{8,9},{9,8},{10,11... | collective-permute-start | bytes 1179656 | tf_op jit(solution)/shard_map/ppermute | solution.py:510
  99.8 107.7 %collective-permute-start.29 = (bf16[3,256,768]{2,1,0:T(8,128)(2,1)}, bf16[3,256,768]{2,1,0:T(8,128)(2,1)}, u32[]{:S(2)}, u32[]{:S(2)}) collective-permute-start(bf16[3,256,768]{2,1,0:T(8,128)(2,1)} %copy-done.21), channel_id=1, source_target_pairs={{0,1},{1,0},{2,3},{3,2},{4,5},{5,4},{6,7},{7,6},{8,9},{9,8},{10,11... | collective-permute-start | bytes 3538952 | tf_op jit(solution)/shard_map/ppermute | solution.py:510
  124.1 25.3 %collective-permute-start.12 = (bf16[256,768]{1,0:T(8,128)(2,1)}, bf16[256,768]{1,0:T(8,128)(2,1)}, u32[]{:S(2)}, u32[]{:S(2)}) collective-permute-start(bf16[256,768]{1,0:T(8,128)(2,1)} %get-tuple-element.121.part_ref), channel_id=1, source_target_pairs={{0,2},{1,3},{2,0},{3,1},{4,6},{5,7},{6,4},{7,5},{8,10},{9,11},{10,... | collective-permute-start | bytes 1179656 | tf_op jit(solution)/shard_map/ppermute | solution.py:510
  147.6 33.8 %collective-permute-start.17 = (bf16[1536,192]{0,1:T(8,128)(2,1)}, bf16[1536,192]{0,1:T(8,128)(2,1)}, u32[]{:S(2)}, u32[]{:S(2)}) collective-permute-start(bf16[1536,192]{0,1:T(8,128)(2,1)} %copy.68), channel_id=1, source_target_pairs={{0,1},{1,0},{2,3},{3,2},{4,5},{5,4},{6,7},{7,6},{8,9},{9,8},{10,11... | collective-permute-start | bytes 1769480 | tf_op jit(solution)/shard_map/ppermute | solution.py:510
  147.6 55.0 %collective-permute-start.24 = (bf16[2,256,768]{2,1,0:T(8,128)(2,1)}, bf16[2,256,768]{2,1,0:T(8,128)(2,1)}, u32[]{:S(2)}, u32[]{:S(2)}) collective-permute-start(bf16[2,256,768]{2,1,0:T(8,128)(2,1)} %copy-done.24), channel_id=1, source_target_pairs={{0,1},{1,0},{2,3},{3,2},{4,5},{5,4},{6,7},{7,6},{8,9},{9,8},{10,11... | collective-permute-start | bytes 2359304 | tf_op jit(solution)/shard_map/ppermute | solution.py:510
  171.1 21.7 %collective-permute-start.13 = (bf16[256,768]{1,0:T(8,128)(2,1)}, bf16[256,768]{1,0:T(8,128)(2,1)}, u32[]{:S(2)}, u32[]{:S(2)}) collective-permute-start(bf16[256,768]{1,0:T(8,128)(2,1)} %get-tuple-element.127.gs_ref), channel_id=1, source_target_pairs={{0,1},{1,0},{2,3},{3,2},{4,5},{5,4},{6,7},{7,6},{8,9},{9,8},{10,11... | collective-permute-start | bytes 1179656 | tf_op jit(solution)/shard_map/ppermute | solution.py:510
  181.4 31.2 %collective-permute-start.34 = (bf16[256,768]{1,0:T(8,128)(2,1)}, bf16[256,768]{1,0:T(8,128)(2,1)}, u32[]{:S(2)}, u32[]{:S(2)}) collective-permute-start(bf16[256,768]{1,0:T(8,128)(2,1)} %copy-done.12), channel_id=1, source_target_pairs={{0,1},{1,0},{2,3},{3,2},{4,5},{5,4},{6,7},{7,6},{8,9},{9,8},{10,11... | collective-permute-start | bytes 1179656 | tf_op jit(solution)/shard_map/ppermute | solution.py:510
  191.1 44.8 %collective-permute-start.10 = (bf16[128,768]{1,0:T(8,128)(2,1)}, bf16[128,768]{1,0:T(8,128)(2,1)}, u32[]{:S(2)}, u32[]{:S(2)}) collective-permute-start(bf16[128,768]{1,0:T(8,128)(2,1)} %get-tuple-element.115), channel_id=1, source_target_pairs={{0,2},{1,3},{2,0},{3,1},{4,6},{5,7},{6,4},{7,5},{8,10},{9,11},{10,... | collective-permute-start | bytes 589832 | tf_op jit(solution)/shard_map/ppermute | solution.py:510
  192.7 47.0 %collective-permute-start.18 = (bf16[256,768]{1,0:T(8,128)(2,1)}, bf16[256,768]{1,0:T(8,128)(2,1)S(1)}, u32[]{:S(2)}, u32[]{:S(2)}) collective-permute-start(bf16[256,768]{1,0:T(8,128)(2,1)} %copy-done.26), channel_id=1, source_target_pairs={{0,1},{1,0},{2,3},{3,2},{4,5},{5,4},{6,7},{7,6},{8,9},{9,8},{10,11... | collective-permute-start | bytes 1179656 | tf_op jit(solution)/shard_map/ppermute | solution.py:510
  205.8 40.5 %collective-permute-start.25 = (bf16[4,96,768]{2,1,0:T(8,128)(2,1)S(1)}, bf16[4,96,768]{2,1,0:T(8,128)(2,1)S(1)}, u32[]{:S(2)}, u32[]{:S(2)}) collective-permute-start(bf16[4,96,768]{2,1,0:T(8,128)(2,1)S(1)} %get-tuple-element.167), channel_id=1, source_target_pairs={{0,4},{4,0},{8,12},{12,8},{16,20},{20,16},{24,28},{28,24},{1,5},{5... | collective-permute-start | bytes 1769480 | tf_op jit(solution)/shard_map/ppermute | solution.py:513
  212.0 38.0 %collective-permute-start.30 = (bf16[4,96,768]{2,1,0:T(8,128)(2,1)S(1)}, bf16[4,96,768]{2,1,0:T(8,128)(2,1)S(1)}, u32[]{:S(2)}, u32[]{:S(2)}) collective-permute-start(bf16[4,96,768]{2,1,0:T(8,128)(2,1)S(1)} %get-tuple-element.178), channel_id=1, source_target_pairs={{0,4},{4,0},{8,12},{12,8},{16,20},{20,16},{24,28},{28,24},{1,5},{5... | collective-permute-start | bytes 1769480 | tf_op jit(solution)/shard_map/ppermute | solution.py:513
  212.6 21.6 %collective-permute-start.41 = (f32[21,128]{1,0:T(8,128)S(1)}, f32[21,128]{1,0:T(8,128)S(1)}, u32[]{:S(2)}, u32[]{:S(2)}) collective-permute-start(f32[21,128]{1,0:T(8,128)S(1)} %fusion.13), channel_id=1, source_target_pairs={{0,4},{4,0},{8,12},{12,8},{16,20},{20,16},{24,28},{28,24},{1,5},{5... | collective-permute-start | bytes 32264 | tf_op jit(solution)/shard_map/ppermute | solution.py:513
  234.2 22.1 %collective-permute-start.35 = (bf16[4,96,768]{2,1,0:T(8,128)(2,1)S(1)}, bf16[4,96,768]{2,1,0:T(8,128)(2,1)S(1)}, u32[]{:S(2)}, u32[]{:S(2)}) collective-permute-start(bf16[4,96,768]{2,1,0:T(8,128)(2,1)S(1)} %get-tuple-element.184), channel_id=1, source_target_pairs={{0,4},{4,0},{8,12},{12,8},{16,20},{20,16},{24,28},{28,24},{1,5},{5... | collective-permute-start | bytes 1769480 | tf_op jit(solution)/shard_map/ppermute | solution.py:513
  244.4 38.2 %collective-permute-start.20 = (bf16[4,96,768]{2,1,0:T(8,128)(2,1)}, bf16[4,96,768]{2,1,0:T(8,128)(2,1)S(1)}, u32[]{:S(2)}, u32[]{:S(2)}) collective-permute-start(bf16[4,96,768]{2,1,0:T(8,128)(2,1)} %get-tuple-element.153), channel_id=1, source_target_pairs={{0,4},{4,0},{8,12},{12,8},{16,20},{20,16},{24,28},{28,24},{1,5},{5... | collective-permute-start | bytes 1769480 | tf_op jit(solution)/shard_map/ppermute | solution.py:513
  256.4 18.6 %collective-permute-start.31 = (bf16[96,768]{1,0:T(8,128)(2,1)}, bf16[96,768]{1,0:T(8,128)(2,1)}, u32[]{:S(2)}, u32[]{:S(2)}) collective-permute-start(bf16[96,768]{1,0:T(8,128)(2,1)} %get-tuple-element.180), channel_id=1, source_target_pairs={{0,8},{4,12},{8,0},{12,4},{16,24},{20,28},{24,16},{28,20},{1,9},{5... | collective-permute-start | bytes 442376 | tf_op jit(solution)/shard_map/ppermute | solution.py:513
  257.6 22.8 %collective-permute-start.32 = (bf16[96,768]{1,0:T(8,128)(2,1)}, bf16[96,768]{1,0:T(8,128)(2,1)}, u32[]{:S(2)}, u32[]{:S(2)}) collective-permute-start(bf16[96,768]{1,0:T(8,128)(2,1)} %get-tuple-element.181), channel_id=1, source_target_pairs={{0,16},{4,20},{8,24},{12,28},{16,0},{20,4},{24,8},{28,12},{1,17},{... | collective-permute-start | bytes 442376 | tf_op jit(solution)/shard_map/ppermute | solution.py:513
  267.7 19.7 %collective-permute-start.33 = (bf16[96,768]{1,0:T(8,128)(2,1)S(1)}, bf16[96,768]{1,0:T(8,128)(2,1)S(1)}, u32[]{:S(2)}, u32[]{:S(2)}) collective-permute-start(bf16[96,768]{1,0:T(8,128)(2,1)S(1)} %get-tuple-element.182), channel_id=1, source_target_pairs={{0,24},{4,28},{8,16},{12,20},{16,8},{20,12},{24,0},{28,4},{1,25},{... | collective-permute-start | bytes 442376 | tf_op jit(solution)/shard_map/ppermute | solution.py:513
  275.0 18.2 %collective-permute-start.37 = (bf16[96,768]{1,0:T(8,128)(2,1)S(1)}, bf16[96,768]{1,0:T(8,128)(2,1)S(1)}, u32[]{:S(2)}, u32[]{:S(2)}) collective-permute-start(bf16[96,768]{1,0:T(8,128)(2,1)S(1)} %get-tuple-element.187), channel_id=1, source_target_pairs={{0,16},{4,20},{8,24},{12,28},{16,0},{20,4},{24,8},{28,12},{1,17},{... | collective-permute-start | bytes 442376 | tf_op jit(solution)/shard_map/ppermute | solution.py:513
  (143 other events, 756.2 us)

commit v2 on v1

v2 whole, which is shorter than its diff:
```python
import functools

import jax
import jax.numpy as jnp
from jax import lax
from jax.experimental import pallas as pl
from jax.experimental.pallas import tpu as pltpu
from jax.sharding import PartitionSpec as P

HEAD_DIM = 64
epsilon = 1e-06
key_scale = 0.125
masked_score = -1e30
highest = lax.Precision.HIGHEST
bf16 = jnp.bfloat16
f32 = jnp.float32


def dot(a, b):
    return lax.dot_general(a, b, (((1,), (0,)), ((), ())), preferred_element_type=f32)


def dot_nt(a, b):
    return lax.dot_general(a, b, (((1,), (1,)), ((), ())), preferred_element_type=f32)


def dot_tn(a, b):
    return lax.dot_general(a, b, (((0,), (0,)), ((), ())), preferred_element_type=f32)


def norm_parts(rows):
    inv = lax.rsqrt(jnp.mean(rows * rows, axis=-1, keepdims=True) + epsilon)
    return rows * inv, inv


def norm_back(rows, gain, grad):
    unit, inv = norm_parts(rows)
    grad_unit = grad * gain
    grad_rows = inv * (grad_unit - unit * jnp.mean(grad_unit * unit, axis=-1, keepdims=True))
    return grad_rows, jnp.sum(grad * unit, axis=0, keepdims=True)


def at(index, size):
    return pl.ds(pl.multiple_of(index * size, size), size)


def shape(dims, dtype=bf16):
    return jax.ShapeDtypeStruct(dims, dtype)


class Whole:
    def __init__(self, array):
        self.arrays = [array]
        self.scratch = [(array.shape, array.dtype)]
        self.copies = 1

    def plan(self, idx, refs, scr, Q):
        return [(refs[0], scr[0])]

    def view(self, lazy, scr):
        return Late(scr[0], lazy)


class Quarters:
    def __init__(self, pieces, n, first=0):
        self.arrays = list(pieces)
        self.first = first
        d = pieces[0].shape[1]
        self.scratch = [((4 * n, d), pieces[0].dtype)]
        self.copies = 4

    def plan(self, idx, refs, scr, Q):
        y, c = idx[0], idx[1]
        places = (2 * y + c, 2 * (1 - y) + c, 2 * y + 1 - c, 2 * (1 - y) + 1 - c)
        return [(r.at[pl.ds(self.first, Q)], scr[0].at[at(p, Q)]) for r, p in zip(refs, places)]

    def view(self, lazy, scr):
        return Late(scr[0], lazy)


class Joined:
    def __init__(self, own, other, picks, count):
        self.arrays = [own, other]
        self.picks = picks
        self.rows = own.shape[0] // count
        self.scratch = [((2 * self.rows, own.shape[1]), own.dtype) for _ in picks]
        self.copies = 2 * len(picks)

    def plan(self, idx, refs, scr, Q):
        n = self.rows
        out = []
        for s, i in zip(scr, self.picks):
            for half, r in enumerate(refs):
                out.append((r.at[pl.ds(i * n, n)], s.at[pl.ds(half * n, n)]))
        return out

    def view(self, lazy, scr):
        return [Late(s, lazy[2 * i : 2 * i + 2]) for i, s in enumerate(scr)]


class Part:
    def __init__(self, array, first, rows):
        self.arrays = [array]
        self.first, self.rows = first, rows
        self.scratch = [((rows,) + array.shape[1:], array.dtype)]
        self.copies = 1

    def plan(self, idx, refs, scr, Q):
        return [(refs[0].at[pl.ds(self.first, self.rows)], scr[0])]

    def view(self, lazy, scr):
        return Late(scr[0], lazy)


class Late:
    def __init__(self, ref, copies):
        self.ref, self.copies = ref, list(copies)
        self.shape, self.dtype = ref.shape, ref.dtype

    def __getitem__(self, index):
        while self.copies:
            self.copies.pop().wait()
        return self.ref[index]


class Result:
    def __init__(self, ref, copy):
        self.ref, self.copy, self.started = ref, copy, False
        self.shape, self.dtype = ref.shape, ref.dtype

    def __getitem__(self, index):
        return self.ref[index]

    def __setitem__(self, index, value):
        self.ref[index] = value

    def flush(self):
        if not self.started:
            self.copy.start()
            self.started = True


def kernel_call(body, name, outs, *args, scratch=(), Q=128, flops=0):
    specs = [a if not hasattr(a, "dtype") else Whole(a) for a in args]
    arrays = [v for s in specs for v in s.arrays]
    in_scr = [x for s in specs for x in s.scratch]
    n_copies = sum(s.copies for s in specs)

    def whole(*refs):
        refs = list(refs)
        mp, dp = lax.axis_index("mp"), lax.axis_index("dp")
        idx_ref = (mp >> 1, mp & 1, dp & 1, dp >> 1)
        ins = [refs.pop(0) for _ in arrays]
        out_refs = [refs.pop(0) for _ in outs]
        scrs = [refs.pop(0) for _ in in_scr]
        out_scr = [refs.pop(0) for _ in outs]
        in_sem, out_sem = refs.pop(0), refs.pop(0)
        views, sem = [], 0
        for s in specs:
            mine = [ins.pop(0) for _ in s.arrays]
            scr = [scrs.pop(0) for _ in s.scratch]
            copies = []
            for src, dst in s.plan(idx_ref, mine, scr, Q):
                copy = pltpu.make_async_copy(src, dst, in_sem.at[sem])
                copy.start()
                sem += 1
                copies.append(copy)
            views.append((s, copies, scr))
        lates = [s.view(copies, scr) for s, copies, scr in views]
        results = [
            Result(s, pltpu.make_async_copy(s, o, out_sem.at[i]))
            for i, (s, o) in enumerate(zip(out_scr, out_refs))
        ]
        body(idx_ref, *lates, *results, *refs)
        for late in lates:
            for v in late if isinstance(late, list) else [late]:
                while v.copies:
                    v.copies.pop().wait()
        for r in results:
            r.flush()
        for r in results:
            r.copy.wait()

    moved = sum(v.size * v.dtype.itemsize for v in arrays)
    moved += sum(v.size * v.dtype.itemsize for v in outs)
    return pl.pallas_call(
        whole,
        out_shape=outs,
        in_specs=[pl.BlockSpec(memory_space=pl.ANY)] * len(arrays),
        out_specs=[pl.BlockSpec(memory_space=pl.ANY)] * len(outs),
        scratch_shapes=[pltpu.VMEM(d, t) for d, t in in_scr]
        + [pltpu.VMEM(o.shape, o.dtype) for o in outs]
        + [pltpu.SemaphoreType.DMA((n_copies,)), pltpu.SemaphoreType.DMA((len(outs),))]
        + list(scratch),
        compiler_params=pltpu.CompilerParams(vmem_limit_bytes=58 * 1024 * 1024),
        cost_estimate=pl.CostEstimate(flops=flops, bytes_accessed=moved, transcendentals=0),
        name=name,
    )(*arrays)


def pair_masks(dtype):
    lane = lax.broadcasted_iota(jnp.int32, (1, 2 * HEAD_DIM), 1) // HEAD_DIM
    return [(lane == h).astype(f32).astype(dtype) for h in range(2)]


def bucket_rows(bucket_ref, count):
    L = bucket_ref.shape[1]
    return (lax.broadcasted_iota(jnp.int32, (count, L), 0) == bucket_ref[...]).astype(f32)


def backwards(L):
    row = lax.broadcasted_iota(jnp.int32, (L, L), 0)
    col = lax.broadcasted_iota(jnp.int32, (L, L), 1)
    return ((row + col == L) | ((row == 0) & (col == 0))).astype(f32)


def exact_dot(a, b, dims):
    return lax.dot_general(a, b, (dims, ((), ())), precision=highest, preferred_element_type=f32)


def bias_body(idx, to_ref, tp_ref, bucket_ref, segr_ref, enc_ref, bias_ref, cross_ref, *, Q):
    core = idx[1]
    L = 4 * Q
    heads, buckets = to_ref.shape
    hot = exact_dot(bucket_rows(bucket_ref, buckets), backwards(L), ((1,), (0,)))
    lines = [exact_dot(t[...], hot, ((1,), (0,))) for t in (to_ref, tp_ref)]
    seg = segr_ref[...]
    columns = jnp.broadcast_to(seg.astype(f32), (Q, L)).T
    for b in range(2):
        rows = pl.ds(b * Q, Q)
        low = columns[2 * b * Q : (2 * b + 1) * Q, 0:1]
        high = columns[(2 * b + 1) * Q : (2 * b + 2) * Q, 0:1]
        segc = jnp.where(core == 0, low, high).astype(jnp.int32)
        cross_ref[rows, :] = jnp.where(segc == enc_ref[...], 0.0, masked_score)
        place = (2 * b + core) * Q + lax.broadcasted_iota(jnp.int32, (Q, L), 0)
        col = lax.broadcasted_iota(jnp.int32, (Q, L), 1)
        allowed = (segc == seg) & (col <= place)
        for grp in range(2):
            turned = pltpu.roll(lines[grp], (2 * b + core) * Q, 1)
            for h in range(heads):
                line = jnp.broadcast_to(turned[h : h + 1, :], (Q, L))
                line = pltpu.roll(line, 0, 1, stride=1, stride_axis=0)
                bias_ref[grp * heads + h, rows, :] = jnp.where(allowed, line, masked_score)


def soft_mix(q_ref, k_ref, v_ref, extra, p_ref, o_ref, rows, nk):
    low, wide = pair_masks(bf16), pair_masks(f32)
    keys = pl.ds(0, nk)
    for pair in range(p_ref.shape[0] // 2):
        lanes = pl.ds(pair * 2 * HEAD_DIM, 2 * HEAD_DIM)
        q, k, v = q_ref[rows, lanes], k_ref[keys, lanes], v_ref[keys, lanes]
        mixed = None
        for i in range(2):
            h = 2 * pair + i
            s = dot_nt(q * low[i], k) * key_scale + extra(h)
            top = jnp.max(s, axis=-1, keepdims=True)
            e = jnp.exp(s - top)
            p = (e * (1.0 / jnp.sum(e, axis=-1, keepdims=True))).astype(bf16)
            p_ref[h, rows, keys] = p
            term = dot(p, v) * wide[i]
            mixed = term if mixed is None else mixed + term
        o_ref[rows, lanes] = mixed.astype(bf16)


def self_forward(idx, x_ref, g_ref, w, bias_ref, part_ref, h_ref, q_ref, k_ref, v_ref, p_ref, o_ref, *, Q):
    core = idx[1]
    gain = g_ref[0:1, :]
    for t in range(4):
        rows = pl.ds(t * Q, Q)
        unit, _ = norm_parts(x_ref[rows, :].astype(f32))
        h_ref[rows, :] = (unit * gain).astype(bf16)
    h_ref.flush()
    k_ref[...] = dot_nt(h_ref[...], w[1][...]).astype(bf16)
    k_ref.flush()
    v_ref[...] = dot_nt(h_ref[...], w[2][...]).astype(bf16)
    v_ref.flush()
    for b in range(2):
        hb = h_ref[at(2 * b + core, Q), :]
        q_ref[pl.ds(b * Q, Q), :] = dot_nt(hb, w[0][...]).astype(bf16)
    q_ref.flush()
    for i in range(p_ref.shape[0]):
        p_ref[i, pl.ds(0, Q), pl.ds(2 * Q, 2 * Q)] = jnp.zeros((Q, 2 * Q), bf16)
    for b in range(2):
        nk = 2 * Q * (b + 1)
        rows = pl.ds(b * Q, Q)
        soft_mix(q_ref, k_ref, v_ref, lambda h: bias_ref[h, rows, pl.ds(0, nk)], p_ref, o_ref, rows, nk)
    p_ref.flush()
    o_ref.flush()
    part_ref[...] = dot(o_ref[...], w[3][...]).astype(bf16)


def encoder_keys(idx, e_ref, w, k_ref, v_ref, *, Q):
    k_ref[...] = dot_nt(e_ref[...], w[0][...]).astype(bf16)
    v_ref[...] = dot_nt(e_ref[...], w[1][...]).astype(bf16)


def cross_forward(idx, x_ref, part_ref, recv_ref, g_ref, w, k_ref, v_ref, mask_ref, out_ref, x1_ref, h_ref, q_ref, p_ref, o_ref, *, Q):
    core = idx[1]
    for b in range(2):
        rows = pl.ds(b * Q, Q)
        x1 = x_ref[at(2 * b + core, Q), :].astype(f32) + (
            part_ref[rows, :].astype(f32) + recv_ref[rows, :].astype(f32)
        )
        x1_ref[rows, :] = x1
        unit, _ = norm_parts(x1)
        h_ref[rows, :] = (unit * g_ref[1:2, :]).astype(bf16)
    x1_ref.flush()
    h_ref.flush()
    q_ref[...] = dot_nt(h_ref[...], w[0][...]).astype(bf16)
    q_ref.flush()
    for b in range(2):
        rows = pl.ds(b * Q, Q)
        soft_mix(q_ref, k_ref, v_ref, lambda h: mask_ref[rows, :], p_ref, o_ref, rows, 4 * Q)
    p_ref.flush()
    o_ref.flush()
    out_ref[...] = dot(o_ref[...], w[1][...]).astype(bf16)


gelu_c = 0.7978845608028654
gelu_k = 0.044715


def act_grads(idx, g_ref, w, out_ref, *, Q):
    n = w[0].shape[0] // 2
    core = idx[1]
    for half in range(2):
        for b in range(2):
            out_ref[half, pl.ds(b * Q, Q), :] = dot(
                g_ref[at(2 * b + core, Q), :], w[0][pl.ds(half * n, n), :]
            ).astype(bf16)


def ffn_both(idx, x1_ref, part_ref, recv_ref, g_ref, up, ga_ref, out_ref, x2_ref, a_ref, du_ref, send_ref, *, Q):
    for b in range(2):
        rows = pl.ds(b * Q, Q)
        x2 = x1_ref[rows, :] + (part_ref[rows, :].astype(f32) + recv_ref[rows, :].astype(f32))
        x2_ref[rows, :] = x2
        unit, _ = norm_parts(x2)
        send_ref[0, rows, :] = (unit * g_ref[2:3, :]).astype(bf16)
    x2_ref.flush()
    n = up[0].shape[0] // 2
    for grp in range(2):
        u = dot(send_ref[0], up[0][pl.ds(grp * n, n), :])
        t = jnp.tanh(gelu_c * (u + gelu_k * (u * u * u)))
        half = 0.5 * (1.0 + t)
        a = (u * half).astype(bf16)
        slope = half + 0.5 * u * (1.0 - t * t) * (gelu_c * (1.0 + 3.0 * gelu_k * (u * u)))
        du = (ga_ref[grp].astype(f32) * slope).astype(bf16)
        if grp == 0:
            a_ref[...] = a
            du_ref[...] = du
            a_ref.flush()
            du_ref.flush()
        else:
            send_ref[1] = a
            send_ref[2] = du
            send_ref.flush()
    out_ref[...] = (
        dot_nt(du_ref[...], up[0][pl.ds(0, n), :]) + dot_nt(send_ref[2], up[0][pl.ds(n, n), :])
    ).astype(bf16)


def ffn_out(idx, a_ref, b_ref, down, x2_ref, keep_ref, out_ref, sum_ref, *, Q):
    y = idx[0]
    n = down[0].shape[0] // 2
    sum_ref[...] = dot_nt(a_ref[...], down[0][pl.ds(0, n), :]) + dot_nt(b_ref[0], down[0][pl.ds(n, n), :])
    out_ref[...] = sum_ref[at(1 - y, Q), :].astype(bf16)
    out_ref.flush()
    keep_ref[...] = sum_ref[at(y, Q), :] + x2_ref[at(y, Q), :]


def attend_back(k_ref, v_ref, do_ref, p_ref, ds_ref, dq_ref, rows, nk):
    low, wide = pair_masks(bf16), pair_masks(f32)
    keys = pl.ds(0, nk)
    for pair in range(ds_ref.shape[0] // 2):
        lanes = pl.ds(pair * 2 * HEAD_DIM, 2 * HEAD_DIM)
        go, k, v = do_ref[rows, lanes], k_ref[keys, lanes], v_ref[keys, lanes]
        total = None
        for i in range(2):
            h = 2 * pair + i
            p = p_ref[h, rows, keys].astype(f32)
            gp = dot_nt(go * low[i], v)
            ds = (p * (gp - jnp.sum(p * gp, axis=-1, keepdims=True))).astype(bf16)
            ds_ref[h, rows, keys] = ds
            term = dot(ds, k) * wide[i]
            total = term if total is None else total + term
        dq_ref[rows, lanes] = (total * key_scale).astype(bf16)


def cross_back(idx, gr_ref, part_ref, recv_ref, x2_ref, g_ref, w, k_ref, v_ref, p_ref, h2_ref, out_ref, dx_ref, sendh_ref, do_ref, ds_ref, dq_ref, gain_ref, *, Q):
    core = idx[1]
    total = None
    for b in range(2):
        rows = pl.ds(b * Q, Q)
        dh = part_ref[rows, :].astype(f32) + recv_ref[rows, :].astype(f32)
        grad_rows, grad_gain = norm_back(x2_ref[rows, :], g_ref[2:3, :], dh)
        dx = gr_ref[at(2 * b + core, Q), :].astype(f32) + grad_rows
        dx_ref[rows, :] = dx
        total = grad_gain if total is None else total + grad_gain
        sendh_ref[0, rows, :] = dx.astype(bf16)
    dx_ref.flush()
    do_ref[...] = dot_nt(sendh_ref[0], w[1][...]).astype(bf16)
    do_ref.flush()
    for b in range(2):
        attend_back(k_ref, v_ref, do_ref, p_ref, ds_ref, dq_ref, pl.ds(b * Q, Q), 4 * Q)
    ds_ref.flush()
    dq_ref.flush()
    out_ref[...] = dot(dq_ref[...], w[0][...]).astype(bf16)
    out_ref.flush()
    sendh_ref[1] = h2_ref[...]
    gain_ref[...] = jnp.broadcast_to(total * 0.5, gain_ref.shape)


def key_grads(ds_ref, p_ref, q, go, dkt_ref, dvt_ref):
    qt = q.astype(f32).T.astype(bf16)
    gt = go.astype(f32).T.astype(bf16)
    for h in range(ds_ref.shape[0]):
        rows = pl.ds(h * HEAD_DIM, HEAD_DIM)
        take = slice(h * HEAD_DIM, (h + 1) * HEAD_DIM)
        dkt_ref[rows, :] = dot(qt[take], ds_ref[h]) * key_scale
        dvt_ref[rows, :] = dot(gt[take], p_ref[h])


def pack_keys(dkt_ref, dvt_ref, dq_ref, o_ref, dk_ref, dv_ref, send_ref, Q):
    W = dk_ref.shape[1]
    dk, dv = dkt_ref[...].T, dvt_ref[...].T
    send_ref[pl.ds(0, 4 * Q), 0:W] = dk[:, W:].astype(bf16)
    send_ref[pl.ds(0, 4 * Q), W:] = dv[:, W:].astype(bf16)
    send_ref[pl.ds(4 * Q, 2 * Q), 0:W] = dq_ref[:, W:]
    send_ref[pl.ds(4 * Q, 2 * Q), W:] = o_ref[:, W:]
    send_ref.flush()
    dk_ref[...] = dk[:, :W]
    dv_ref[...] = dv[:, :W]


def keys_body(idx, ds_ref, p_ref, q_ref, do_ref, dq_ref, o_ref, dk_ref, dv_ref, send_ref, dkt_ref, dvt_ref, *, Q):
    key_grads(ds_ref, p_ref, q_ref[...], do_ref[...], dkt_ref, dvt_ref)
    pack_keys(dkt_ref, dvt_ref, dq_ref, o_ref, dk_ref, dv_ref, send_ref, Q)


def self_back(idx, dx_ref, part_ref, recv_ref, x1_ref, g_ref, w, k_ref, v_ref, p_ref, q_ref, o_ref, gain3_ref, dx1_ref, gs_ref, dq_ref, dk_ref, dv_ref, send_ref, gain_ref, ds_ref, do_ref, dkt_ref, dvt_ref, sum_ref, *, Q):
    total = None
    for b in range(2):
        rows = pl.ds(b * Q, Q)
        dh = part_ref[rows, :].astype(f32) + recv_ref[rows, :].astype(f32)
        grad_rows, grad_gain = norm_back(x1_ref[rows, :], g_ref[1:2, :], dh)
        dx = dx_ref[rows, :] + grad_rows
        sum_ref[rows, :] = dx
        total = grad_gain if total is None else total + grad_gain
        gs_ref[rows, :] = dx.astype(bf16)
    gs_ref.flush()
    dx1_ref[...] = sum_ref[at(idx[0], Q), :]
    dx1_ref.flush()
    for i in range(ds_ref.shape[0]):
        ds_ref[i, pl.ds(0, Q), pl.ds(2 * Q, 2 * Q)] = jnp.zeros((Q, 2 * Q), bf16)
    do_ref[...] = dot_nt(gs_ref[...], w[0][...]).astype(bf16)
    for b in range(2):
        attend_back(k_ref, v_ref, do_ref, p_ref, ds_ref, dq_ref, pl.ds(b * Q, Q), 2 * Q * (b + 1))
    ds_ref.flush()
    dq_ref.flush()
    key_grads(ds_ref, p_ref, q_ref[...], do_ref[...], dkt_ref, dvt_ref)
    pack_keys(dkt_ref, dvt_ref, dq_ref, o_ref, dk_ref, dv_ref, send_ref, Q)
    gain_ref[0:1, :] = total * 0.5
    gain_ref[1:, :] = gain3_ref[1:, :]


def small_sums(idx, ds_ref, bucket_ref, gain1_ref, gain23_ref, out_ref, *, Q, buckets):
    y, core = idx[0], idx[1]
    L = 4 * Q
    heads = ds_ref.shape[0]
    lines = []
    for h in range(heads):
        line = ds_ref[h, pl.ds(0, Q), :].astype(f32) + pltpu.roll(
            ds_ref[h, pl.ds(Q, Q), :].astype(f32), L - 2 * Q, 1
        )
        n = Q // 2
        while n >= 1:
            line = line[:n] + pltpu.roll(line[n : 2 * n], L - n, 1)
            n //= 2
        lines.append(line)
    lines.append(jnp.zeros((8 - heads, L), f32))
    lines = pltpu.roll(jnp.concatenate(lines, axis=0), (4 - core) * Q, 1)
    lines = exact_dot(lines, backwards(L), ((1,), (0,)))
    sums = exact_dot(lines, bucket_rows(bucket_ref, buckets), ((1,), (1,)))
    out_ref[...] = jnp.zeros(out_ref.shape, f32)
    out_ref[0:1, :] = gain1_ref[0:1, :]
    out_ref[1:3, :] = gain23_ref[0:2, :]
    row = lax.broadcasted_iota(jnp.int32, (out_ref.shape[0], buckets), 0)
    table = out_ref[:, 0:buckets]
    for grp in range(2):
        first = (2 * y + (core if grp == 0 else 1 - core)) * (heads // 2)
        for h in range(heads // 2):
            k = grp * (heads // 2) + h
            table = jnp.where(row == first + h + 3, jnp.broadcast_to(sums[k : k + 1, :], row.shape), table)
    out_ref[:, 0:buckets] = table


def self_weights(idx, h_ref, gs_ref, gsr_ref, o_ref, dq_ref, dk_ref, dv_ref, recv_ref, *rest, Q, split):
    core = idx[1]
    if split:
        keep_ref, send_ref, d_ref, sum_ref = rest
    else:
        sum_ref, d_ref = rest
    W = dk_ref.shape[1]
    for b in range(2):
        rows = pl.ds(b * Q, Q)
        d_ref[at(2 * b + core, Q), 0:W] = dq_ref[rows, 0:W]
        d_ref[at(2 * b + 1 - core, Q), 0:W] = recv_ref[pl.ds((4 + b) * Q, Q), 0:W]
    keys = pl.ds(0, 4 * Q)
    d_ref[:, W : 2 * W] = (dk_ref[...] + recv_ref[keys, 0:W].astype(f32)).astype(bf16)
    d_ref[:, 2 * W : 3 * W] = (dv_ref[...] + recv_ref[keys, W:].astype(f32)).astype(bf16)
    d_ref.flush()
    sum_ref[:, 0 : 3 * W] = dot_tn(h_ref[...], d_ref[...])
    sum_ref[:, 3 * W : 4 * W] = dot_tn(gs_ref[...], o_ref[:, 0:W]) + dot_tn(
        gsr_ref[...], recv_ref[pl.ds(4 * Q, 2 * Q), W:]
    )
    if split:
        split_rows(idx, sum_ref, keep_ref, send_ref)


def split_rows(idx, sum_ref, keep_ref, send_ref):
    x, z = idx[2], idx[3]
    n = keep_ref.shape[1]
    for i in range(keep_ref.shape[0]):
        place = 2 * lax.bitwise_xor(z, i)
        send_ref[i] = sum_ref[at(place + 1 - x, n), :].astype(send_ref.dtype)
    send_ref.flush()
    for i in range(keep_ref.shape[0]):
        place = 2 * lax.bitwise_xor(z, i)
        keep_ref[i] = sum_ref[at(place + x, n), :].astype(keep_ref.dtype)


def cross_weights(idx, sendh_ref, recvh_ref, e_ref, dq_ref, d_ref, o_ref, recv_ref, *rest, Q, split):
    if split:
        keep_ref, send_ref, sum_ref = rest
    else:
        (sum_ref,) = rest
    W = dq_ref.shape[1] // 2
    low = pl.ds(4 * Q, 2 * Q)
    sum_ref[:, 0:W] = dot_tn(sendh_ref[1], dq_ref[:, 0:W]) + dot_tn(recvh_ref[1], recv_ref[low, 0:W])
    sum_ref[:, W : 3 * W] = dot_tn(e_ref[...], d_ref[...])
    sum_ref[:, 3 * W : 4 * W] = dot_tn(sendh_ref[0], o_ref[:, 0:W]) + dot_tn(recvh_ref[0], recv_ref[low, W:])
    if split:
        split_rows(idx, sum_ref, keep_ref, send_ref)


def down_weights(idx, g_ref, a_ref, r_ref, *rest, Q, split):
    core = idx[1]
    if split:
        keep_ref, send_ref, sum_ref, all_ref = rest
    else:
        sum_ref, all_ref = rest
    for b in range(2):
        all_ref[at(2 * b + core, Q), :] = a_ref[pl.ds(b * Q, Q), :]
        all_ref[at(2 * b + 1 - core, Q), :] = r_ref[0, pl.ds(b * Q, Q), :]
    sum_ref[...] = dot_tn(g_ref[...], all_ref[...])
    if split:
        split_rows(idx, sum_ref, keep_ref, send_ref)


def up_weights(idx, h_ref, d_ref, hr_ref, dr_ref, *rest, Q, split):
    if split:
        keep_ref, send_ref, sum_ref = rest
    else:
        (sum_ref,) = rest
    sum_ref[...] = dot_tn(h_ref[0], d_ref[...]) + dot_tn(hr_ref[0], dr_ref[0])
    if split:
        split_rows(idx, sum_ref, keep_ref, send_ref)


def shares(idx):
    y, core = idx[0], idx[1]
    return (2 * y + core, 2 * (1 - y) + core), (2 * y + 1 - core, 2 * (1 - y) + 1 - core)


def encoder_grad(idx, dk_ref, dv_ref, recv_ref, wk_ref, wv_ref, keep_ref, send_ref, d_ref, *, Q):
    W = dk_ref.shape[1]
    keys = pl.ds(0, 4 * Q)
    d_ref[:, 0:W] = (dk_ref[...] + recv_ref[keys, 0:W].astype(f32)).astype(bf16)
    d_ref[:, W:] = (dv_ref[...] + recv_ref[keys, W:].astype(f32)).astype(bf16)
    d_ref.flush()
    keep, send = shares(idx)
    for out, places in ((send_ref, send), (keep_ref, keep)):
        for i, place in enumerate(places):
            take = d_ref[at(place, Q), :]
            out[i] = (dot(take[:, :W], wk_ref[...]) + dot(take[:, W:], wv_ref[...])).astype(out.dtype)
        out.flush()


def input_grad(idx, d_ref, w_ref, h_ref, g_ref, keep_ref, send_ref, gain_ref, *, Q):
    keep, send = shares(idx)
    total = None
    for out, places in ((send_ref, send), (keep_ref, keep)):
        for i, place in enumerate(places):
            rows = at(place, Q)
            grad = dot(d_ref[rows, :], w_ref[...])
            out[i] = grad.astype(out.dtype)
            term = jnp.sum(grad * h_ref[rows, :].astype(f32), axis=0, keepdims=True)
            total = term if total is None else total + term
        out.flush()
    gain_ref[...] = jnp.broadcast_to(total / g_ref[0:1, :], gain_ref.shape)


def after(value, *others):
    return lax.optimization_barrier((value, others))[0]


def local(
    decoder_in,
    encoder_states,
    dec_segments,
    enc_segments,
    offset_buckets,
    norm_gains,
    bias_table,
    self_query,
    self_key,
    self_value,
    self_out,
    cross_query,
    cross_key,
    cross_value,
    cross_out,
    ffn_up,
    ffn_down,
    out_grad,
    dp_size,
):
    Q, D = decoder_in.shape[1:]
    L = 4 * Q
    W = self_query.shape[1]
    F = ffn_up.shape[1]
    heads = bias_table.shape[1]
    buckets = bias_table.shape[0]
    split = dp_size == 8
    mp = lax.axis_index("mp")
    y = mp // 2

    def over_mp(v, flip):
        return lax.ppermute(v, "mp", [(i, i ^ flip) for i in range(4)])

    def over_dp(v, flip):
        return lax.ppermute(v, "dp", [(i, i ^ flip) for i in range(dp_size)])

    def call(body, name, outs, *args, scratch=(), **static):
        static["Q"] = Q
        return kernel_call(functools.partial(body, **static), name, outs, *args, scratch=scratch, Q=Q)

    def quarters(v):
        across = over_mp(v, 2)
        return v, across, over_mp(v, 1), over_mp(across, 1)

    x4 = quarters(decoder_in[0])
    w_self = jnp.concatenate([self_query.T, self_key.T, self_value.T, self_out.T])
    w_self_p = over_mp(w_self, 1)
    table_p = over_mp(bias_table.T, 1)
    eg4 = quarters(jnp.concatenate([encoder_states[0], out_grad[0]]))
    w_cross = jnp.concatenate([cross_query.T, cross_key.T, cross_value.T, cross_out.T])
    w_cross_p = over_mp(w_cross, 1)
    up_p = over_mp(ffn_up, 1)
    down_p = over_mp(ffn_down, 1)

    def x_rows():
        return Quarters(x4, Q)

    def e_rows():
        return Quarters(eg4, Q)

    def g_rows():
        return Quarters(eg4, Q, Q)

    def self_w(*picks):
        return Joined(w_self, w_self_p, picks, 4)

    def cross_w(*picks):
        return Joined(w_cross, w_cross_p, picks, 4)

    up = Joined(ffn_up, up_p, (0,), 1)
    down = Joined(ffn_down, down_p, (0,), 1)

    bucket_line = offset_buckets.reshape(1, L)
    bias, cross_mask = call(
        bias_body,
        "bias",
        [shape((2 * heads, 2 * Q, L), f32), shape((2 * Q, L), f32)],
        bias_table.T,
        table_p,
        bucket_line,
        dec_segments,
        enc_segments,
    )

    both_rows, both_all = shape((2 * Q, 2 * W)), shape((L, 2 * W))
    square = shape((2 * heads, 2 * Q, L))
    half = shape((2 * Q, D))
    half_f = shape((2 * Q, D), f32)
    line = shape((8, D), f32)

    part1, h1, q1, k1, v1, p1, o1 = call(
        self_forward,
        "self_forward",
        [half, shape((L, D)), both_rows, both_all, both_all, square, both_rows],
        x_rows(),
        norm_gains,
        self_w(0, 1, 2, 3),
        bias,
    )
    recv1 = over_mp(part1, 2)
    k2, v2 = call(encoder_keys, "encoder_keys", [both_all, both_all], e_rows(), cross_w(1, 2))
    part2, x1, h2, q2, p2, o2 = call(
        cross_forward,
        "cross_forward",
        [half, half_f, half, both_rows, square, both_rows],
        x_rows(),
        part1,
        recv1,
        norm_gains,
        cross_w(0, 3),
        k2,
        v2,
        cross_mask,
    )
    recv2 = over_mp(part2, 2)
    (grad_act,) = call(act_grads, "act_grads", [shape((2, 2 * Q, F))], g_rows(), down)
    part3, x2, a_own, du_own, send3 = call(
        ffn_both,
        "ffn_both",
        [half, half_f, shape((2 * Q, F)), shape((2 * Q, F)), shape((3, 2 * Q, D))],
        x1,
        part2,
        recv2,
        norm_gains,
        up,
        grad_act,
    )
    recv3 = over_mp(part3, 2)
    recv_ffn = over_mp(send3, 1)
    quarter, quarter_f = shape((Q, D)), shape((Q, D), f32)

    def grad_kernel(body, name, cols, *args, extra=(), scratch=(), **static):
        if split:
            keep = shape((dp_size // 2, D // dp_size, cols))
            outs = [keep, keep, *extra]
            scratch = [pltpu.VMEM((D, cols), f32), *scratch]
        else:
            outs = [shape((D, cols), f32), *extra]
        res = call(body, name, outs, *args, scratch=scratch, split=split, **static)
        return (res[:2], res[2:]) if split else (res[:1], res[1:])

    def reduce_x(parts):
        if not split:
            return parts
        keep, send = parts
        recv = over_dp(send, 1)
        return [(keep[i].astype(f32) + recv[i].astype(f32)) for i in range(dp_size // 2)]

    def reduce_z(sums, count):
        if not split:
            total = lax.psum_scatter(sums[0], "dp", scatter_dimension=0, tiled=True)
        else:
            total = sums[0]
            for i in range(1, dp_size // 2):
                total = total + over_dp(sums[i].astype(bf16), 2 * i).astype(f32)
        width = total.shape[1] // count
        return [total[:, i * width : (i + 1) * width] for i in range(count)]

    down_parts, _ = grad_kernel(
        down_weights, "down_weights", F, g_rows(), a_own, Part(recv_ffn, 1, 1), scratch=[pltpu.VMEM((L, F), bf16)]
    )
    up_parts, _ = grad_kernel(
        up_weights, "up_weights", F, Part(send3, 0, 1), du_own, Part(recv_ffn, 0, 1), Part(recv_ffn, 2, 1)
    )
    y_keep, y_send = call(
        ffn_out,
        "ffn_out",
        [quarter_f, quarter],
        a_own,
        Part(send3, 1, 1),
        down,
        x2,
        scratch=[pltpu.VMEM((2 * Q, D), f32)],
    )
    output = (y_keep + over_mp(y_send, 2).astype(f32)).astype(bf16)

    own_f = shape((L, W), f32)
    packed = shape((6 * Q, 2 * W))
    turned_f = pltpu.VMEM((2 * W, L), f32)
    recv3 = after(recv3, down_parts, up_parts)
    part4, dx2, send4, do2, ds2, dq2, gain3 = call(
        cross_back,
        "cross_back",
        [half, half_f, shape((2, 2 * Q, D)), both_rows, square, both_rows, line],
        g_rows(),
        part3,
        recv3,
        x2,
        norm_gains,
        cross_w(0, 3),
        k2,
        v2,
        p2,
        h2,
    )
    recv4 = over_mp(part4, 2)
    recv_h = over_mp(send4, 1)
    dk2, dv2, send_k = call(
        keys_body, "cross_keys", [own_f, own_f, packed], ds2, p2, q2, do2, dq2, o2, scratch=[turned_f, turned_f]
    )
    recv_k = over_mp(send_k, 1)
    pair_f, pair = shape((2, Q, D), f32), shape((2, Q, D))
    enc_keep, enc_send, d2 = call(
        encoder_grad,
        "encoder_grad",
        [pair_f, pair, both_all],
        dk2,
        dv2,
        recv_k,
        Part(w_cross, W, W),
        Part(w_cross, 2 * W, W),
    )
    cross_parts, _ = grad_kernel(
        cross_weights, "cross_weights", 4 * W, send4, recv_h, e_rows(), dq2, d2, o2, recv_k
    )

    def finish_rows(keep, send):
        recv = over_mp(send, 1).astype(f32)
        across = over_mp((keep[1] + recv[1]).astype(bf16), 2)
        return keep[0] + recv[0] + across.astype(f32)

    grad_encoder = finish_rows(enc_keep, enc_send).astype(bf16)

    recv4 = after(recv4, cross_parts)
    dx1, gs, dq1, dk1, dv1, send_s, gain23, ds1 = call(
        self_back,
        "self_back",
        [quarter_f, half, both_rows, own_f, own_f, packed, line, square],
        dx2,
        part4,
        recv4,
        x1,
        norm_gains,
        self_w(3),
        k1,
        v1,
        p1,
        q1,
        o1,
        gain3,
        scratch=[pltpu.VMEM((2 * Q, 2 * W), bf16), turned_f, turned_f, pltpu.VMEM((2 * Q, D), f32)],
    )
    recv_s = over_mp(send_s, 1)
    gs_oth = over_mp(gs, 1)
    self_parts, (d1,) = grad_kernel(
        self_weights, "self_weights", 4 * W, h1, gs, gs_oth, o1, dq1, dk1, dv1, recv_s, extra=[shape((L, 3 * W))]
    )
    in_keep, in_send, gain1 = call(
        input_grad, "input_grad", [pair_f, pair, line], d1, Part(w_self, 0, 3 * W), h1, norm_gains
    )
    grad_rows, _ = norm_back(decoder_in[0].astype(f32), norm_gains[0:1], finish_rows(in_keep, in_send))
    grad_decoder = (dx1 + grad_rows).astype(bf16)

    (small,) = call(
        small_sums, "small_sums", [shape((16, D), f32)], ds1, bucket_line, gain1, gain23, buckets=buckets
    )
    small = small + over_mp(small, 1)
    small = small + over_mp(small, 2)
    flip = dp_size // 2
    while flip:
        small = small + over_dp(small, flip)
        flip //= 2
    gain_total = small[:3]
    table_total = small[3 : 3 + 4 * heads, :buckets].T

    (grad_down,) = reduce_z(reduce_x(down_parts), 1)
    (grad_up,) = reduce_z(reduce_x(up_parts), 1)
    grad_cq, grad_ck, grad_cv, grad_co = reduce_z(reduce_x(cross_parts), 4)
    grad_sq, grad_sk, grad_sv, grad_so = reduce_z(reduce_x(self_parts), 4)

    def row(v):
        return v.reshape((1,) + v.shape)

    return (
        row(output),
        row(grad_decoder),
        row(grad_encoder),
        grad_sq,
        grad_sk,
        grad_sv,
        grad_so,
        grad_cq,
        grad_ck,
        grad_cv,
        grad_co,
        grad_up,
        grad_down,
        gain_total,
        table_total,
    )


def solution(mesh):
    rows = P("dp", "mp", None)
    cols = P(None, "mp")
    grads = P("dp", "mp")
    in_specs = (rows, rows, P("dp", None), P("dp", None), P(), P(), cols) + (cols,) * 10 + (rows,)
    out_specs = (rows, rows, rows) + (grads,) * 10 + (P(), P())
    body = functools.partial(local, dp_size=mesh.shape["dp"])
    return jax.shard_map(body, mesh=mesh, in_specs=in_specs, out_specs=out_specs, check_vma=False)
```

time: 309 us -> 208 us (0.67)
  local copies, waits for them, and re-layouts: 94.4 us -> 11.1 us
  blocking collectives: 9.62 us -> 0 us
  starting transfers between devices: 51 us -> 42.9 us
  other arithmetic: 4.26 us -> 8.72 us
    unnamed x256 -> x84, local copies, waits for them, and re-layouts: 68 us -> 7.56 us
    all_gather x1 -> x0, blocking collectives: 9.62 us -> none  [local(): x_full = lax.all_gather(decoder_in[0], 'mp', axis=0, tiled=True)]
    ppermute x4 -> x0, local copies, waits for them, and re-layouts: 8.82 us -> none  [over_mp(): return lax.ppermute(v, 'mp', [(i, i ^ flip) for i in range(4)])]
    ppermute x19, starting transfers between devices: 33.4 us -> 25.4 us  [over_dp(): return lax.ppermute(v, 'dp', [(i, i ^ flip) for i in range(dp_size)])]
    pallas_call x2 -> x0, local copies, waits for them, and re-layouts: 4.45 us -> none  [kernel_call(): pl.pallas_call(body, out_shape=outs, in_specs=specs, out_specs=[pl.BlockS...]
    pallas_call x28 -> x17, Pallas kernels: 86.1 us -> 84.8 us  [kernel_call(): pl.pallas_call(whole, out_shape=outs, in_specs=[pl.BlockSpec(memory_space...]
    ppermute x25 -> x27, waiting for transfers between devices: 24.6 us -> 23.4 us  [over_mp(): return lax.ppermute(v, 'mp', [(i, i ^ flip) for i in range(4)])]
    ppermute x25 -> x27, starting transfers between devices: 17.7 us -> 17.5 us  [over_mp(): return lax.ppermute(v, 'mp', [(i, i ^ flip) for i in range(4)])]
  transfers between devices with their start and end apart: 44 -> 46, of which waited for: 9 -> 16; matrix products, arithmetic and copies ran while one was open for 11% -> 5% of each run, Pallas kernels for 26% -> 38%
where the time goes in v2:
time: 208 us
  Pallas kernels  84.8 us (41%)
  waiting for transfers between devices  58.8 us (28%)
  starting transfers between devices  42.9 us (21%)
  local copies, waits for them, and re-layouts  11.1 us (5%)
  other arithmetic  8.72 us (4%)
    pallas_call x17, Pallas kernels, kernel_call(): pl.pallas_call(whole, out_shape=outs, in_specs=[pl.BlockSpec(memory_space...  84.8 us
    ppermute x19, waiting for transfers between devices, over_dp(): return lax.ppermute(v, 'dp', [(i, i ^ flip) for i in range(dp_size)])  35.4 us
    ppermute x19, starting transfers between devices, over_dp(): return lax.ppermute(v, 'dp', [(i, i ^ flip) for i in range(dp_size)])  25.4 us
    ppermute x27, waiting for transfers between devices, over_mp(): return lax.ppermute(v, 'mp', [(i, i ^ flip) for i in range(4)])  23.4 us
    ppermute x27, starting transfers between devices, over_mp(): return lax.ppermute(v, 'mp', [(i, i ^ flip) for i in range(4)])  17.5 us
    unnamed x84, local copies, waits for them, and re-layouts  7.56 us
  transfers between devices with their start and end apart: 46, of which 16 were waited for; matrix products, arithmetic and copies ran while one was open for 5% of the time, Pallas kernels for 38%

profile of v2, /device:TPU:0, one launch (start us, length us, event | category | flops | bytes accessed | tf_op | source)
XLA Modules:
  0.0 207.6 jit_solution(2262567554485007538)
XLA Ops:
  12.6 6.6 %collective-permute-done.7.refs_1_.refs_3_ = bf16[256,768]{1,0:T(8,128)(2,1)S(1)} collective-permute-done((bf16[256,768]{1,0:T(8,128)(2,1)S(1)}, bf16[256,768]{1,0:T(8,128)(2,1)S(1)}, u32[]{:S(2)}, u32[]{:S(2)}) %collective-permute-start.7) | collective-permute-done | bytes 393248 | tf_op jit(solution)/shard_map/ppermute | solution.py:640
  19.2 4.7 %bias.1 = (f32[6,256,512]{2,1,0:T(8,128)}, f32[256,512]{1,0:T(8,128)}) custom-call(f32[3,32]{1,0:T(4,128)} %bitcast.110, f32[3,32]{1,0:T(4,128)} %copy-done.38, s32[1,512]{1,0:T(1,128)} %bitcast.108, s32[1,512]{1,0:T(1,128)} %refs_3_.3, s32[1,512]{1,0:T(1,128)} %refs_4_.5), custom_call_target="tpu_custom_call" | custom-call | bytes 3676928 | tf_op jit(solution)/shard_map/bias/pallas_call | solution.py:186
  25.0 7.7 %self_forward.1 = (bf16[256,768]{1,0:T(8,128)(2,1)}, bf16[512,768]{1,0:T(8,128)(2,1)}, bf16[256,384]{1,0:T(8,128)(2,1)}, bf16[512,384]{1,0:T(8,128)(2,1)}, bf16[...) custom-call(bf16[128,768]{1,0:T(8,128)(2,1)} %bitcast.94, ...), custom_call_target="tpu_custom_call" | custom-call | bytes 10232832 | tf_op jit(solution)/shard_map/self_forward/pallas_call | solution.py:186
  36.4 3.5 %encoder_keys.1 = (bf16[512,384]{1,0:T(8,128)(2,1)}, bf16[512,384]{1,0:T(8,128)(2,1)}) custom-call(bf16[256,768]{1,0:T(8,128)(2,1)} %copy-done.2, bf16[256,768]{1,0:T(8,128)(2,1)} %copy-done.5, bf16[256,768]{1,0:T(8,128)(2,1)} %copy-done.6, bf16[256,768]{1,0:T(8,128)(2,1)} %copy-done.7, bf16[768,768]{1,0:T(8,128)(2,1)} %copy-done, bf16[768,768]{1,0:T(8,128)(2,1)} %copy-done.3), custom_call_target="tpu_custom_call" | custom-call | bytes 4718592 | tf_op jit(solution)/shard_map/encoder_keys/pallas_call | solution.py:186
  39.9 4.6 %collective-permute-done.5.refs_5_ = bf16[256,768]{1,0:T(8,128)(2,1)S(1)} collective-permute-done((bf16[256,768]{1,0:T(8,128)(2,1)}, bf16[256,768]{1,0:T(8,128)(2,1)S(1)}, u32[]{:S(2)}, u32[]{:S(2)}) %collective-permute-start.5) | collective-permute-done | bytes 393248 | tf_op jit(solution)/shard_map/ppermute | solution.py:640
  45.2 8.0 %cross_forward.1 = (bf16[256,768]{1,0:T(8,128)(2,1)}, f32[256,768]{1,0:T(8,128)}, bf16[256,768]{1,0:T(8,128)(2,1)}, bf16[256,384]{1,0:T(8,128)(2,1)}, bf16[6,256...) custom-call(bf16[128,768]{1,0:T(8,128)(2,1)} %bitcast.95, bf16[128,768]{1,0:T(8,128)(2,1)} %copy-done.13, ...), custom_call_target="tpu_custom_call" | custom-call | bytes 8791040 | tf_op jit(solution)/shard_map/cross_forward/pallas_call | solution.py:186
  55.0 3.7 %act_grads.1.refs_6_ = bf16[2,256,768]{2,1,0:T(8,128)(2,1)} custom-call(bf16[256,768]{1,0:T(8,128)(2,1)} %copy-done.2, bf16[256,768]{1,0:T(8,128)(2,1)} %copy-done.5, bf16[256,768]{1,0:T(8,128)(2,1)} %copy-done.6, bf16[256,768]{1,0:T(8,128)(2,1)} %copy-done.7, bf16[768,768]{1,0:T(8,128)(2,1)} %refs_2_.1, bf16[768,768]{1,0:T(8,128)(2,1)} %collective-permute-done.12.refs_5_.refs_3_), custom_call_target="tpu_custom_call" | custom-call | bytes 4718592 | tf_op jit(solution)/shard_map/act_grads/pallas_call | solution.py:186
  58.8 5.3 %collective-permute-done.10.refs_2_ = bf16[256,768]{1,0:T(8,128)(2,1)S(1)} collective-permute-done((bf16[256,768]{1,0:T(8,128)(2,1)}, bf16[256,768]{1,0:T(8,128)(2,1)S(1)}, u32[]{:S(2)}, u32[]{:S(2)}) %collective-permute-start.10) | collective-permute-done | bytes 393248 | tf_op jit(solution)/shard_map/ppermute | solution.py:640
  64.8 6.2 %ffn_both.1 = (bf16[256,768]{1,0:T(8,128)(2,1)}, f32[256,768]{1,0:T(8,128)}, bf16[256,768]{1,0:T(8,128)(2,1)}, bf16[256,768]{1,0:T(8,128)(2,1)}, bf16[3,256,768]{2,1,0:T(8,128)(2,1)}) custom-call(f32[256,768]{1,0:T(8,128)} %get-tuple-element.79.refs_0_.refs_3_, bf16[256,768]{1,0:T(8,128)(2,1)} %get-tuple-element.80.refs_1_, bf16[256,768]{1,0:T(8,128)(2,1)} %copy-done.30, ...), custom_call_target="tpu_custom_call" | custom-call | bytes 7873536 | tf_op jit(solution)/shard_map/ffn_both/pallas_call | solution.py:186
  80.3 3.5 %down_weights.1 = (bf16[4,96,768]{2,1,0:T(8,128)(2,1)}, bf16[4,96,768]{2,1,0:T(8,128)(2,1)}) custom-call(bf16[256,768]{1,0:T(8,128)(2,1)} %copy-done.2, bf16[256,768]{1,0:T(8,128)(2,1)} %copy-done.5, bf16[256,768]{1,0:T(8,128)(2,1)} %copy-done.6, bf16[256,768]{1,0:T(8,128)(2,1)} %copy-done.7, bf16[256,768]{1,0:T(8,128)(2,1)} %get-tuple-element.81.refs_0_.refs_4_, ...), custom_call_target="tpu_custom_call" | custom-call | bytes 4325376 | tf_op jit(solution)/shard_map/down_weights/pallas_call | solution.py:186
  85.0 7.7 %cross_back.1 = (bf16[256,768]{1,0:T(8,128)(2,1)}, f32[256,768]{1,0:T(8,128)}, bf16[2,256,768]{2,1,0:T(8,128)(2,1)}, bf16[256,384]{1,0:T(8,128)(2,1)}, bf16[6,25...) custom-call(bf16[256,768]{1,0:T(8,128)(2,1)} %copy-done.2, bf16[256,768]{1,0:T(8,128)(2,1)} %copy-done.5, ...), custom_call_target="tpu_custom_call" | custom-call | bytes 12223488 | tf_op jit(solution)/shard_map/cross_back/pallas_call | solution.py:186
  92.8 4.6 %cross_keys.1 = (f32[512,192]{1,0:T(8,128)}, f32[512,192]{1,0:T(8,128)}, bf16[768,384]{1,0:T(8,128)(2,1)}) custom-call(bf16[6,256,512]{2,1,0:T(8,128)(2,1)} %get-tuple-element.99.refs_0_, bf16[6,256,512]{2,1,0:T(8,128)(2,1)} %get-tuple-element.93.refs_12_.refs_1_, bf16[256,384]{1,0:T(8,128)(2,1)} %get-tuple-element.100.refs_2_, ...), custom_call_target="tpu_custom_call" | custom-call | bytes 5308416 | tf_op jit(solution)/shard_map/cross_keys/pallas_call | solution.py:186
  98.9 3.8 %ffn_out.1 = (f32[128,768]{1,0:T(8,128)}, bf16[128,768]{1,0:T(8,128)(2,1)}) custom-call(bf16[256,768]{1,0:T(8,128)(2,1)} %get-tuple-element.81.refs_0_.refs_4_, bf16[3,256,768]{2,1,0:T(8,128)(2,1)} %get-tuple-element.82.refs_1_.refs_0_, bf16[768,768]{1,0:T(8,128)(2,1)} %refs_2_.1, bf16[768,768]{1,0:T(8,128)(2,1)} %collective-permute-done.12.refs_5_.refs_3_, ...), custom_call_target="tpu_custom_call" | custom-call | bytes 5308416 | tf_op jit(solution)/shard_map/ffn_out/pallas_call | solution.py:186
  105.6 3.8 %collective-permute-start.36 = (bf16[96,768]{1,0:T(8,128)(2,1)}, bf16[96,768]{1,0:T(8,128)(2,1)S(1)}, u32[]{:S(2)}, u32[]{:S(2)}) collective-permute-start(bf16[96,768]{1,0:T(8,128)(2,1)} %get-tuple-element.137), channel_id=1, source_target_pairs={{0,24},{4,28},{8,16},{12,20},{16,8},{20,12},{24,0},{28,4},{1,25},{... | collective-permute-start | bytes 442376 | tf_op jit(solution)/shard_map/ppermute | solution.py:643
  114.9 5.4 %cross_weights.1 = (bf16[4,96,768]{2,1,0:T(8,128)(2,1)}, bf16[4,96,768]{2,1,0:T(8,128)(2,1)}) custom-call(bf16[2,256,768]{2,1,0:T(8,128)(2,1)} %get-tuple-element.97.refs_0_, bf16[2,256,768]{2,1,0:T(8,128)(2,1)} %copy-done.17, bf16[256,768]{1,0:T(8,128)(2,1)} %copy-done.2, bf16[256,768]{1,0:T(8,128)(2,1)} %copy-done.5, bf16[256,768]{1,0:T(8,128)(2,1)} %copy-done.6, ...), custom_call_target="tpu_custom_call" | custom-call | bytes 5701632 | tf_op jit(solution)/shard_map/cross_weights/pallas_call | solution.py:186
  123.4 7.3 %self_back.1 = (f32[128,768]{1,0:T(8,128)}, bf16[256,768]{1,0:T(8,128)(2,1)}, bf16[256,384]{1,0:T(8,128)(2,1)}, f32[512,192]{1,0:T(8,128)}, f32[512,192]{1,0:T(8...) custom-call(f32[256,768]{1,0:T(8,128)} %get-tuple-element.95.refs_0_, ...), custom_call_target="tpu_custom_call" | custom-call | bytes 11461632 | tf_op jit(solution)/shard_map/self_back/pallas_call | solution.py:186
  134.9 3.8 %collective-permute-done.39 = bf16[96,768]{1,0:T(8,128)(2,1)S(1)} collective-permute-done((bf16[96,768]{1,0:T(8,128)(2,1)S(1)}, bf16[96,768]{1,0:T(8,128)(2,1)S(1)}, u32[]{:S(2)}, u32[]{:S(2)}) %collective-permute-start.39) | collective-permute-done | bytes 147488 | tf_op jit(solution)/shard_map/ppermute | solution.py:643
  142.1 5.2 %self_weights.1 = (bf16[4,96,768]{2,1,0:T(8,128)(2,1)}, bf16[4,96,768]{2,1,0:T(8,128)(2,1)}, bf16[512,576]{1,0:T(8,128)(2,1)}) custom-call(bf16[512,768]{1,0:T(8,128)(2,1)} %get-tuple-element.117.refs_0_.refs_2_, bf16[256,768]{1,0:T(8,128)(2,1)} %get-tuple-element.118.refs_1_, bf16[256,768]{1,0:T(8,128)(2,1)} %copy-done.26, ...), custom_call_target="tpu_custom_call" | custom-call | bytes 5111808 | tf_op jit(solution)/shard_map/self_weights/pallas_call | solution.py:186
  147.3 3.4 %input_grad.1 = (f32[2,128,768]{2,1,0:T(8,128)}, bf16[2,128,768]{2,1,0:T(8,128)(2,1)}, f32[8,768]{1,0:T(8,128)}) custom-call(bf16[512,576]{1,0:T(8,128)(2,1)} %get-tuple-element.123.refs_0_, bf16[768,768]{1,0:T(8,128)(2,1)} %copy-done.1, bf16[512,768]{1,0:T(8,128)(2,1)} %get-tuple-element.117.refs_0_.refs_2_, f32[3,768]{1,0:T(4,128)} %refs_3_.5), custom_call_target="tpu_custom_call" | custom-call | bytes 3769344 | tf_op jit(solution)/shard_map/input_grad/pallas_call | solution.py:186
  150.7 3.5 %small_sums.1 = f32[16,768]{1,0:T(8,128)} custom-call(bf16[6,256,512]{2,1,0:T(8,128)(2,1)} %get-tuple-element.130.refs_0_, s32[1,512]{1,0:T(1,128)} %bitcast.109, f32[8,768]{1,0:T(8,128)} %get-tuple-element.131.refs_2_, f32[8,768]{1,0:T(8,128)} %get-tuple-element.132.refs_3_), custom_call_target="tpu_custom_call" | custom-call | bytes 1673216 | tf_op jit(solution)/shard_map/small_sums/pallas_call | solution.py:186
  164.4 10.0 %collective-permute-done.43 = f32[16,768]{1,0:T(8,128)S(1)} collective-permute-done((f32[16,768]{1,0:T(8,128)S(1)}, f32[16,768]{1,0:T(8,128)S(1)}, u32[]{:S(2)}, u32[]{:S(2)}) %collective-permute-start.43) | collective-permute-done | bytes 49184 | tf_op jit(solution)/shard_map/ppermute | solution.py:643
  176.2 3.9 %collective-permute-done.44 = f32[16,768]{1,0:T(8,128)S(1)} collective-permute-done((f32[16,768]{1,0:T(8,128)S(1)}, f32[16,768]{1,0:T(8,128)S(1)}, u32[]{:S(2)}, u32[]{:S(2)}) %collective-permute-start.44) | collective-permute-done | bytes 49184 | tf_op jit(solution)/shard_map/ppermute | solution.py:643
  181.5 9.2 %collective-permute-done.45 = f32[16,768]{1,0:T(8,128)S(1)} collective-permute-done((f32[16,768]{1,0:T(8,128)S(1)}, f32[16,768]{1,0:T(8,128)S(1)}, u32[]{:S(2)}, u32[]{:S(2)}) %collective-permute-start.45) | collective-permute-done | bytes 49184 | tf_op jit(solution)/shard_map/ppermute | solution.py:643
  201.6 5.1 %collective-permute-done.27 = bf16[96,768]{1,0:T(8,128)(2,1)S(1)} collective-permute-done((bf16[96,768]{1,0:T(8,128)(2,1)S(1)}, bf16[96,768]{1,0:T(8,128)(2,1)S(1)}, u32[]{:S(2)}, u32[]{:S(2)}) %collective-permute-start.27) | collective-permute-done | bytes 147488 | tf_op jit(solution)/shard_map/ppermute | solution.py:643
  (201 shorter events, 75.8 us)
Async XLA Ops:
  2.1 21.8 %collective-permute-start.3 = (bf16[768,768]{1,0:T(8,128)(2,1)S(1)}, bf16[768,768]{1,0:T(8,128)(2,1)S(1)}, u32[]{:S(2)}, u32[]{:S(2)}) collective-permute-start(bf16[768,768]{1,0:T(8,128)(2,1)S(1)} %pad_maximum_fusion.refs_5_.refs_1_), channel_id=1, source_target_pairs={{0,1},{1,0},{2,3},{3,2},{4,5},{5,4},{6,7},{7,6},{8,9},{9,8},{10,11... | collective-permute-start | bytes 3538952 | tf_op jit(solution)/shard_map/ppermute | solution.py:640
  5.4 29.2 %collective-permute-start.6 = (bf16[768,768]{1,0:T(8,128)(2,1)S(1)}, bf16[768,768]{1,0:T(8,128)(2,1)S(1)}, u32[]{:S(2)}, u32[]{:S(2)}) collective-permute-start(bf16[768,768]{1,0:T(8,128)(2,1)S(1)} %pad_maximum_fusion.1.refs_4_.refs_7_.refs_8_.refs_3_), channel_id=1, source_target_pairs={{0,1},{1,0},{2,3},{3,2},{4,5},{5,4},{6,7},{7,6},{8,9},{9,8},{10,11... | collective-permute-start | bytes 3538952 | tf_op jit(solution)/shard_map/ppermute | solution.py:640
  6.4 12.7 %collective-permute-start.7 = (bf16[256,768]{1,0:T(8,128)(2,1)S(1)}, bf16[256,768]{1,0:T(8,128)(2,1)S(1)}, u32[]{:S(2)}, u32[]{:S(2)}) collective-permute-start(bf16[256,768]{1,0:T(8,128)(2,1)S(1)} %pad_maximum_fusion.2.refs_0_.refs_2_), channel_id=1, source_target_pairs={{0,2},{1,3},{2,0},{3,1},{4,6},{5,7},{6,4},{7,5},{8,10},{9,11},{10,... | collective-permute-start | bytes 1179656 | tf_op jit(solution)/shard_map/ppermute | solution.py:640
  11.0 21.8 %collective-permute-start.8 = (bf16[256,768]{1,0:T(8,128)(2,1)S(1)}, bf16[256,768]{1,0:T(8,128)(2,1)S(1)}, u32[]{:S(2)}, u32[]{:S(2)}) collective-permute-start(bf16[256,768]{1,0:T(8,128)(2,1)S(1)} %pad_maximum_fusion.2.refs_0_.refs_2_), channel_id=1, source_target_pairs={{0,1},{1,0},{2,3},{3,2},{4,5},{5,4},{6,7},{7,6},{8,9},{9,8},{10,11... | collective-permute-start | bytes 1179656 | tf_op jit(solution)/shard_map/ppermute | solution.py:640
  12.4 42.6 %collective-permute-start.12 = (bf16[768,768]{1,0:T(8,128)(2,1)}, bf16[768,768]{1,0:T(8,128)(2,1)}, u32[]{:S(2)}, u32[]{:S(2)}) collective-permute-start(bf16[768,768]{1,0:T(8,128)(2,1)} %refs_2_.1), channel_id=1, source_target_pairs={{0,1},{1,0},{2,3},{3,2},{4,5},{5,4},{6,7},{7,6},{8,9},{9,8},{10,11... | collective-permute-start | bytes 3538952 | tf_op jit(solution)/shard_map/ppermute | solution.py:640
  19.2 39.6 %collective-permute-start.11 = (bf16[768,768]{1,0:T(8,128)(2,1)}, bf16[768,768]{1,0:T(8,128)(2,1)}, u32[]{:S(2)}, u32[]{:S(2)}) collective-permute-start(bf16[768,768]{1,0:T(8,128)(2,1)} %refs_4_.8), channel_id=1, source_target_pairs={{0,1},{1,0},{2,3},{3,2},{4,5},{5,4},{6,7},{7,6},{8,9},{9,8},{10,11... | collective-permute-start | bytes 3538952 | tf_op jit(solution)/shard_map/ppermute | solution.py:640
  32.8 11.7 %collective-permute-start.5 = (bf16[256,768]{1,0:T(8,128)(2,1)}, bf16[256,768]{1,0:T(8,128)(2,1)S(1)}, u32[]{:S(2)}, u32[]{:S(2)}) collective-permute-start(bf16[256,768]{1,0:T(8,128)(2,1)} %get-tuple-element.75.refs_4_), channel_id=1, source_target_pairs={{0,2},{1,3},{2,0},{3,1},{4,6},{5,7},{6,4},{7,5},{8,10},{9,11},{10,... | collective-permute-start | bytes 1179656 | tf_op jit(solution)/shard_map/ppermute | solution.py:640
  71.1 13.1 %collective-permute-start.14 = (bf16[256,768]{1,0:T(8,128)(2,1)}, bf16[256,768]{1,0:T(8,128)(2,1)S(1)}, u32[]{:S(2)}, u32[]{:S(2)}) collective-permute-start(bf16[256,768]{1,0:T(8,128)(2,1)} %get-tuple-element.86.refs_4_), channel_id=1, source_target_pairs={{0,2},{1,3},{2,0},{3,1},{4,6},{5,7},{6,4},{7,5},{8,10},{9,11},{10,... | collective-permute-start | bytes 1179656 | tf_op jit(solution)/shard_map/ppermute | solution.py:640
  78.6 25.9 %collective-permute-start.33 = (bf16[4,96,768]{2,1,0:T(8,128)(2,1)}, bf16[4,96,768]{2,1,0:T(8,128)(2,1)S(1)}, u32[]{:S(2)}, u32[]{:S(2)}) collective-permute-start(bf16[4,96,768]{2,1,0:T(8,128)(2,1)} %get-tuple-element.91), channel_id=1, source_target_pairs={{0,4},{4,0},{8,12},{12,8},{16,20},{20,16},{24,28},{28,24},{1,5},{5... | collective-permute-start | bytes 1769480 | tf_op jit(solution)/shard_map/ppermute | solution.py:643
  83.8 28.9 %collective-permute-start.37 = (bf16[4,96,768]{2,1,0:T(8,128)(2,1)}, bf16[4,96,768]{2,1,0:T(8,128)(2,1)S(1)}, u32[]{:S(2)}, u32[]{:S(2)}) collective-permute-start(bf16[4,96,768]{2,1,0:T(8,128)(2,1)} %get-tuple-element.88), channel_id=1, source_target_pairs={{0,4},{4,0},{8,12},{12,8},{16,20},{20,16},{24,28},{28,24},{1,5},{5... | collective-permute-start | bytes 1769480 | tf_op jit(solution)/shard_map/ppermute | solution.py:643
  97.6 16.0 %collective-permute-start.17 = (bf16[2,256,768]{2,1,0:T(8,128)(2,1)S(1)}, bf16[2,256,768]{2,1,0:T(8,128)(2,1)S(1)}, u32[]{:S(2)}, u32[]{:S(2)}) collective-permute-start(bf16[2,256,768]{2,1,0:T(8,128)(2,1)S(1)} %copy-done.16), channel_id=1, source_target_pairs={{0,1},{1,0},{2,3},{3,2},{4,5},{5,4},{6,7},{7,6},{8,9},{9,8},{10,11... | collective-permute-start | bytes 2359304 | tf_op jit(solution)/shard_map/ppermute | solution.py:640
  102.7 28.0 %collective-permute-start.13 = (bf16[128,768]{1,0:T(8,128)(2,1)}, bf16[128,768]{1,0:T(8,128)(2,1)S(1)}, u32[]{:S(2)}, u32[]{:S(2)}) collective-permute-start(bf16[128,768]{1,0:T(8,128)(2,1)} %get-tuple-element.85), channel_id=1, source_target_pairs={{0,2},{1,3},{2,0},{3,1},{4,6},{5,7},{6,4},{7,5},{8,10},{9,11},{10,... | collective-permute-start | bytes 589832 | tf_op jit(solution)/shard_map/ppermute | solution.py:640
  104.5 15.8 %collective-permute-start.16 = (bf16[256,768]{1,0:T(8,128)(2,1)S(1)}, bf16[256,768]{1,0:T(8,128)(2,1)S(1)}, u32[]{:S(2)}, u32[]{:S(2)}) collective-permute-start(bf16[256,768]{1,0:T(8,128)(2,1)S(1)} %copy-done.23), channel_id=1, source_target_pairs={{0,2},{1,3},{2,0},{3,1},{4,6},{5,7},{6,4},{7,5},{8,10},{9,11},{10,... | collective-permute-start | bytes 1179656 | tf_op jit(solution)/shard_map/ppermute | solution.py:640
  105.6 25.3 %collective-permute-start.36 = (bf16[96,768]{1,0:T(8,128)(2,1)}, bf16[96,768]{1,0:T(8,128)(2,1)S(1)}, u32[]{:S(2)}, u32[]{:S(2)}) collective-permute-start(bf16[96,768]{1,0:T(8,128)(2,1)} %get-tuple-element.137), channel_id=1, source_target_pairs={{0,24},{4,28},{8,16},{12,20},{16,8},{20,12},{24,0},{28,4},{1,25},{... | collective-permute-start | bytes 442376 | tf_op jit(solution)/shard_map/ppermute | solution.py:643
  112.7 18.9 %collective-permute-start.35 = (bf16[96,768]{1,0:T(8,128)(2,1)S(1)}, bf16[96,768]{1,0:T(8,128)(2,1)S(1)}, u32[]{:S(2)}, u32[]{:S(2)}) collective-permute-start(bf16[96,768]{1,0:T(8,128)(2,1)S(1)} %get-tuple-element.138), channel_id=1, source_target_pairs={{0,16},{4,20},{8,24},{12,28},{16,0},{20,4},{24,8},{28,12},{1,17},{... | collective-permute-start | bytes 442376 | tf_op jit(solution)/shard_map/ppermute | solution.py:643
  113.5 18.6 %collective-permute-start.34 = (bf16[96,768]{1,0:T(8,128)(2,1)S(1)}, bf16[96,768]{1,0:T(8,128)(2,1)S(1)}, u32[]{:S(2)}, u32[]{:S(2)}) collective-permute-start(bf16[96,768]{1,0:T(8,128)(2,1)S(1)} %get-tuple-element.136), channel_id=1, source_target_pairs={{0,8},{4,12},{8,0},{12,4},{16,24},{20,28},{24,16},{28,20},{1,9},{5... | collective-permute-start | bytes 442376 | tf_op jit(solution)/shard_map/ppermute | solution.py:643
  120.4 13.0 %collective-permute-start.40 = (bf16[96,768]{1,0:T(8,128)(2,1)}, bf16[96,768]{1,0:T(8,128)(2,1)S(1)}, u32[]{:S(2)}, u32[]{:S(2)}) collective-permute-start(bf16[96,768]{1,0:T(8,128)(2,1)} %get-tuple-element.134), channel_id=1, source_target_pairs={{0,24},{4,28},{8,16},{12,20},{16,8},{20,12},{24,0},{28,4},{1,25},{... | collective-permute-start | bytes 442376 | tf_op jit(solution)/shard_map/ppermute | solution.py:643
  133.4 24.7 %collective-permute-start.29 = (bf16[4,96,768]{2,1,0:T(8,128)(2,1)}, bf16[4,96,768]{2,1,0:T(8,128)(2,1)S(1)}, u32[]{:S(2)}, u32[]{:S(2)}) collective-permute-start(bf16[4,96,768]{2,1,0:T(8,128)(2,1)} %get-tuple-element.108), channel_id=1, source_target_pairs={{0,4},{4,0},{8,12},{12,8},{16,20},{20,16},{24,28},{28,24},{1,5},{5... | collective-permute-start | bytes 1769480 | tf_op jit(solution)/shard_map/ppermute | solution.py:643
  158.2 17.8 %collective-permute-start.32 = (bf16[96,768]{1,0:T(8,128)(2,1)S(1)}, bf16[96,768]{1,0:T(8,128)(2,1)S(1)}, u32[]{:S(2)}, u32[]{:S(2)}) collective-permute-start(bf16[96,768]{1,0:T(8,128)(2,1)S(1)} %get-tuple-element.140), channel_id=1, source_target_pairs={{0,24},{4,28},{8,16},{12,20},{16,8},{20,12},{24,0},{28,4},{1,25},{... | collective-permute-start | bytes 442376 | tf_op jit(solution)/shard_map/ppermute | solution.py:643
  160.7 15.4 %collective-permute-start.31 = (bf16[96,768]{1,0:T(8,128)(2,1)S(1)}, bf16[96,768]{1,0:T(8,128)(2,1)S(1)}, u32[]{:S(2)}, u32[]{:S(2)}) collective-permute-start(bf16[96,768]{1,0:T(8,128)(2,1)S(1)} %get-tuple-element.141), channel_id=1, source_target_pairs={{0,16},{4,20},{8,24},{12,28},{16,0},{20,4},{24,8},{28,12},{1,17},{... | collective-permute-start | bytes 442376 | tf_op jit(solution)/shard_map/ppermute | solution.py:643
  160.7 15.4 %collective-permute-start.30 = (bf16[96,768]{1,0:T(8,128)(2,1)S(1)}, bf16[96,768]{1,0:T(8,128)(2,1)S(1)}, u32[]{:S(2)}, u32[]{:S(2)}) collective-permute-start(bf16[96,768]{1,0:T(8,128)(2,1)S(1)} %get-tuple-element.139), channel_id=1, source_target_pairs={{0,8},{4,12},{8,0},{12,4},{16,24},{20,28},{24,16},{28,20},{1,9},{5... | collective-permute-start | bytes 442376 | tf_op jit(solution)/shard_map/ppermute | solution.py:643
  162.7 11.7 %collective-permute-start.43 = (f32[16,768]{1,0:T(8,128)S(1)}, f32[16,768]{1,0:T(8,128)S(1)}, u32[]{:S(2)}, u32[]{:S(2)}) collective-permute-start(f32[16,768]{1,0:T(8,128)S(1)} %add.211), channel_id=1, source_target_pairs={{0,16},{4,20},{8,24},{12,28},{16,0},{20,4},{24,8},{28,12},{1,17},{... | collective-permute-start | bytes 147464 | tf_op jit(solution)/shard_map/ppermute | solution.py:643
  164.4 27.5 %collective-permute-start.21 = (bf16[2,128,768]{2,1,0:T(8,128)(2,1)S(1)}, bf16[2,128,768]{2,1,0:T(8,128)(2,1)S(1)}, u32[]{:S(2)}, u32[]{:S(2)}) collective-permute-start(bf16[2,128,768]{2,1,0:T(8,128)(2,1)S(1)} %copy-done.41), channel_id=1, source_target_pairs={{0,1},{1,0},{2,3},{3,2},{4,5},{5,4},{6,7},{7,6},{8,9},{9,8},{10,11... | collective-permute-start | bytes 1179656 | tf_op jit(solution)/shard_map/ppermute | solution.py:640
  174.4 18.4 %collective-permute-start.25 = (bf16[4,96,768]{2,1,0:T(8,128)(2,1)S(1)}, bf16[4,96,768]{2,1,0:T(8,128)(2,1)S(1)}, u32[]{:S(2)}, u32[]{:S(2)}) collective-permute-start(bf16[4,96,768]{2,1,0:T(8,128)(2,1)S(1)} %copy-done.39), channel_id=1, source_target_pairs={{0,4},{4,0},{8,12},{12,8},{16,20},{20,16},{24,28},{28,24},{1,5},{5... | collective-permute-start | bytes 1769480 | tf_op jit(solution)/shard_map/ppermute | solution.py:643
  (64 other events, 401.3 us)

commit v3 on v2

--- a/solution.py
+++ b/solution.py
@@ -360,15 +360,6 @@
     ).astype(bf16)
 
 
-def ffn_out(idx, a_ref, b_ref, down, x2_ref, keep_ref, out_ref, sum_ref, *, Q):
-    y = idx[0]
-    n = down[0].shape[0] // 2
-    sum_ref[...] = dot_nt(a_ref[...], down[0][pl.ds(0, n), :]) + dot_nt(b_ref[0], down[0][pl.ds(n, n), :])
-    out_ref[...] = sum_ref[at(1 - y, Q), :].astype(bf16)
-    out_ref.flush()
-    keep_ref[...] = sum_ref[at(y, Q), :] + x2_ref[at(y, Q), :]
-
-
 def attend_back(k_ref, v_ref, do_ref, p_ref, ds_ref, dq_ref, rows, nk):
     low, wide = pair_masks(bf16), pair_masks(f32)
     keys = pl.ds(0, nk)
@@ -464,7 +455,7 @@
     gain_ref[1:, :] = gain3_ref[1:, :]
 
 
-def small_sums(idx, ds_ref, bucket_ref, gain1_ref, gain23_ref, out_ref, *, Q, buckets):
+def table_sums(idx, ds_ref, bucket_ref, Q, buckets, wide):
     y, core = idx[0], idx[1]
     L = 4 * Q
     heads = ds_ref.shape[0]
@@ -482,25 +473,28 @@
     lines = pltpu.roll(jnp.concatenate(lines, axis=0), (4 - core) * Q, 1)
     lines = exact_dot(lines, backwards(L), ((1,), (0,)))
     sums = exact_dot(lines, bucket_rows(bucket_ref, buckets), ((1,), (1,)))
-    out_ref[...] = jnp.zeros(out_ref.shape, f32)
-    out_ref[0:1, :] = gain1_ref[0:1, :]
-    out_ref[1:3, :] = gain23_ref[0:2, :]
-    row = lax.broadcasted_iota(jnp.int32, (out_ref.shape[0], buckets), 0)
-    table = out_ref[:, 0:buckets]
-    for grp in range(2):
-        first = (2 * y + (core if grp == 0 else 1 - core)) * (heads // 2)
-        for h in range(heads // 2):
-            k = grp * (heads // 2) + h
-            table = jnp.where(row == first + h + 3, jnp.broadcast_to(sums[k : k + 1, :], row.shape), table)
-    out_ref[:, 0:buckets] = table
-
-
-def self_weights(idx, h_ref, gs_ref, gsr_ref, o_ref, dq_ref, dk_ref, dv_ref, recv_ref, *rest, Q, split):
+    lane = lax.broadcasted_iota(jnp.int32, (buckets, wide), 1)
+    spread = (lax.broadcasted_iota(jnp.int32, (buckets, wide), 0) == lane % buckets).astype(f32)
+    sums = exact_dot(sums, spread, ((1,), (0,)))
+    row = lax.broadcasted_iota(jnp.int32, (8, wide), 0)
+    other = (row >= heads // 2).astype(jnp.int32)
+    owner = (2 * y + core) * (1 - other) + (2 * y + 1 - core) * other
+    head = owner * (heads // 2) + row - other * (heads // 2)
+    mine = (row < heads) & (lax.broadcasted_iota(jnp.int32, (8, wide), 1) // buckets == head)
+    return jnp.sum(jnp.where(mine, sums, 0.0), axis=0, keepdims=True)
+
+
+def shares(idx):
+    y, core = idx[0], idx[1]
+    return (2 * y + core, 2 * (1 - y) + core), (2 * y + 1 - core, 2 * (1 - y) + 1 - core)
+
+
+def self_weights(idx, h_ref, gs_ref, gsr_ref, o_ref, dq_ref, dk_ref, dv_ref, recv_ref, w_ref, g_ref, ds_ref, bucket_ref, gain23_ref, *rest, Q, split, buckets, wide):
     core = idx[1]
     if split:
-        keep_ref, send_ref, d_ref, sum_ref = rest
+        keep_ref, send_ref, in_keep_ref, in_send_ref, small_ref, sum_ref, d_ref = rest
     else:
-        sum_ref, d_ref = rest
+        sum_ref, in_keep_ref, in_send_ref, small_ref, d_ref = rest
     W = dk_ref.shape[1]
     for b in range(2):
         rows = pl.ds(b * Q, Q)
@@ -509,88 +503,8 @@
     keys = pl.ds(0, 4 * Q)
     d_ref[:, W : 2 * W] = (dk_ref[...] + recv_ref[keys, 0:W].astype(f32)).astype(bf16)
     d_ref[:, 2 * W : 3 * W] = (dv_ref[...] + recv_ref[keys, W:].astype(f32)).astype(bf16)
-    d_ref.flush()
-    sum_ref[:, 0 : 3 * W] = dot_tn(h_ref[...], d_ref[...])
-    sum_ref[:, 3 * W : 4 * W] = dot_tn(gs_ref[...], o_ref[:, 0:W]) + dot_tn(
-        gsr_ref[...], recv_ref[pl.ds(4 * Q, 2 * Q), W:]
-    )
-    if split:
-        split_rows(idx, sum_ref, keep_ref, send_ref)
-
-
-def split_rows(idx, sum_ref, keep_ref, send_ref):
-    x, z = idx[2], idx[3]
-    n = keep_ref.shape[1]
-    for i in range(keep_ref.shape[0]):
-        place = 2 * lax.bitwise_xor(z, i)
-        send_ref[i] = sum_ref[at(place + 1 - x, n), :].astype(send_ref.dtype)
-    send_ref.flush()
-    for i in range(keep_ref.shape[0]):
-        place = 2 * lax.bitwise_xor(z, i)
-        keep_ref[i] = sum_ref[at(place + x, n), :].astype(keep_ref.dtype)
-
-
-def cross_weights(idx, sendh_ref, recvh_ref, e_ref, dq_ref, d_ref, o_ref, recv_ref, *rest, Q, split):
-    if split:
-        keep_ref, send_ref, sum_ref = rest
-    else:
-        (sum_ref,) = rest
-    W = dq_ref.shape[1] // 2
-    low = pl.ds(4 * Q, 2 * Q)
-    sum_ref[:, 0:W] = dot_tn(sendh_ref[1], dq_ref[:, 0:W]) + dot_tn(recvh_ref[1], recv_ref[low, 0:W])
-    sum_ref[:, W : 3 * W] = dot_tn(e_ref[...], d_ref[...])
-    sum_ref[:, 3 * W : 4 * W] = dot_tn(sendh_ref[0], o_ref[:, 0:W]) + dot_tn(recvh_ref[0], recv_ref[low, W:])
-    if split:
-        split_rows(idx, sum_ref, keep_ref, send_ref)
-
-
-def down_weights(idx, g_ref, a_ref, r_ref, *rest, Q, split):
-    core = idx[1]
-    if split:
-        keep_ref, send_ref, sum_ref, all_ref = rest
-    else:
-        sum_ref, all_ref = rest
-    for b in range(2):
-        all_ref[at(2 * b + core, Q), :] = a_ref[pl.ds(b * Q, Q), :]
-        all_ref[at(2 * b + 1 - core, Q), :] = r_ref[0, pl.ds(b * Q, Q), :]
-    sum_ref[...] = dot_tn(g_ref[...], all_ref[...])
-    if split:
-        split_rows(idx, sum_ref, keep_ref, send_ref)
-
-
-def up_weights(idx, h_ref, d_ref, hr_ref, dr_ref, *rest, Q, split):
-    if split:
-        keep_ref, send_ref, sum_ref = rest
-    else:
-        (sum_ref,) = rest
-    sum_ref[...] = dot_tn(h_ref[0], d_ref[...]) + dot_tn(hr_ref[0], dr_ref[0])
-    if split:
-        split_rows(idx, sum_ref, keep_ref, send_ref)
-
-
-def shares(idx):
-    y, core = idx[0], idx[1]
-    return (2 * y + core, 2 * (1 - y) + core), (2 * y + 1 - core, 2 * (1 - y) + 1 - core)
-
-
-def encoder_grad(idx, dk_ref, dv_ref, recv_ref, wk_ref, wv_ref, keep_ref, send_ref, d_ref, *, Q):
-    W = dk_ref.shape[1]
-    keys = pl.ds(0, 4 * Q)
-    d_ref[:, 0:W] = (dk_ref[...] + recv_ref[keys, 0:W].astype(f32)).astype(bf16)
-    d_ref[:, W:] = (dv_ref[...] + recv_ref[keys, W:].astype(f32)).astype(bf16)
-    d_ref.flush()
-    keep, send = shares(idx)
-    for out, places in ((send_ref, send), (keep_ref, keep)):
-        for i, place in enumerate(places):
-            take = d_ref[at(place, Q), :]
-            out[i] = (dot(take[:, :W], wk_ref[...]) + dot(take[:, W:], wv_ref[...])).astype(out.dtype)
-        out.flush()
-
-
-def input_grad(idx, d_ref, w_ref, h_ref, g_ref, keep_ref, send_ref, gain_ref, *, Q):
-    keep, send = shares(idx)
     total = None
-    for out, places in ((send_ref, send), (keep_ref, keep)):
+    for out, places in zip((in_keep_ref, in_send_ref), shares(idx)):
         for i, place in enumerate(places):
             rows = at(place, Q)
             grad = dot(d_ref[rows, :], w_ref[...])
@@ -598,11 +512,86 @@
             term = jnp.sum(grad * h_ref[rows, :].astype(f32), axis=0, keepdims=True)
             total = term if total is None else total + term
         out.flush()
-    gain_ref[...] = jnp.broadcast_to(total / g_ref[0:1, :], gain_ref.shape)
-
-
-def after(value, *others):
-    return lax.optimization_barrier((value, others))[0]
+    small_ref[...] = jnp.zeros(small_ref.shape, f32)
+    small_ref[0:1, :] = total / g_ref[0:1, :]
+    small_ref[1:3, :] = gain23_ref[0:2, :]
+    small_ref[3:4, 0:wide] = table_sums(idx, ds_ref, bucket_ref, Q, buckets, wide)
+    small_ref.flush()
+    sum_ref[:, 0 : 3 * W] = dot_tn(h_ref[...], d_ref[...])
+    sum_ref[:, 3 * W : 4 * W] = dot_tn(gs_ref[...], o_ref[:, 0:W]) + dot_tn(
+        gsr_ref[...], recv_ref[pl.ds(4 * Q, 2 * Q), W:]
+    )
+    if split:
+        last = pl.ds(keep_ref.shape[0] * keep_ref.shape[1], 16)
+        small = small_ref[...]
+        high = small.astype(bf16)
+        send_ref[last, :] = jnp.concatenate([high.astype(f32), small - high.astype(f32)]).astype(bf16)
+        split_rows(idx, sum_ref, keep_ref, send_ref)
+
+
+def split_rows(idx, sum_ref, keep_ref, send_ref):
+    x, z_here = idx[2], idx[3]
+    n = keep_ref.shape[1]
+    places = [lax.bitwise_xor(z_here, i) for i in (0, 2, 1, 3)]
+    for i, z in enumerate(places):
+        block = sum_ref[at(2 * z + 1 - x, n), :].astype(send_ref.dtype)
+        if len(send_ref.shape) == 3:
+            send_ref[i] = block
+        else:
+            send_ref[pl.ds(i * n, n), :] = block
+    send_ref.flush()
+    for i, z in enumerate(places):
+        keep_ref[i] = sum_ref[at(2 * z + x, n), :].astype(keep_ref.dtype)
+
+
+def cross_weights(idx, sendh_ref, recvh_ref, e_ref, dq_ref, dk_ref, dv_ref, o_ref, recv_ref, wk_ref, wv_ref, a_ref, b_ref, down, x2_ref, *rest, Q, split):
+    y = idx[0]
+    outs, (d_ref, rows_ref) = list(rest[:-2]), rest[-2:]
+    if split:
+        keep_ref, send_ref, ekeep_ref, esend_ref, okeep_ref, osend_ref, sum_ref = outs
+    else:
+        sum_ref, ekeep_ref, esend_ref, okeep_ref, osend_ref = outs
+    W = dk_ref.shape[1]
+    low, keys = pl.ds(4 * Q, 2 * Q), pl.ds(0, 4 * Q)
+    d_ref[:, 0:W] = (dk_ref[...] + recv_ref[keys, 0:W].astype(f32)).astype(bf16)
+    d_ref[:, W:] = (dv_ref[...] + recv_ref[keys, W:].astype(f32)).astype(bf16)
+    sum_ref[:, W : 3 * W] = dot_tn(e_ref[...], d_ref[...])
+    sum_ref[:, 0:W] = dot_tn(sendh_ref[1], dq_ref[:, 0:W]) + dot_tn(recvh_ref[1], recv_ref[low, 0:W])
+    sum_ref[:, 3 * W : 4 * W] = dot_tn(sendh_ref[0], o_ref[:, 0:W]) + dot_tn(recvh_ref[0], recv_ref[low, W:])
+    if split:
+        split_rows(idx, sum_ref, keep_ref, send_ref)
+        keep_ref.flush()
+    keep, send = shares(idx)
+    for out, places in ((esend_ref, send), (ekeep_ref, keep)):
+        for i, place in enumerate(places):
+            take = d_ref[at(place, Q), :]
+            out[i] = (dot(take[:, :W], wk_ref[...]) + dot(take[:, W:], wv_ref[...])).astype(out.dtype)
+        out.flush()
+    n = down[0].shape[0] // 2
+    rows_ref[...] = dot_nt(a_ref[...], down[0][pl.ds(0, n), :]) + dot_nt(b_ref[0], down[0][pl.ds(n, n), :])
+    osend_ref[...] = rows_ref[at(1 - y, Q), :].astype(bf16)
+    osend_ref.flush()
+    okeep_ref[...] = rows_ref[at(y, Q), :] + x2_ref[at(y, Q), :]
+
+
+def ffn_weights(idx, g_ref, a_ref, h_ref, d_ref, hr_ref, ar_ref, dr_ref, *rest, Q, split):
+    core = idx[1]
+    F = a_ref.shape[1]
+    if split:
+        keep_ref, send_ref, sum_ref, all_ref = rest
+    else:
+        sum_ref, all_ref = rest
+    for b in range(2):
+        all_ref[at(2 * b + core, Q), :] = a_ref[pl.ds(b * Q, Q), :]
+        all_ref[at(2 * b + 1 - core, Q), :] = ar_ref[0, pl.ds(b * Q, Q), :]
+    sum_ref[:, F:] = dot_tn(g_ref[...], all_ref[...])
+    sum_ref[:, 0:F] = dot_tn(h_ref[0], d_ref[...]) + dot_tn(hr_ref[0], dr_ref[0])
+    if split:
+        split_rows(idx, sum_ref, keep_ref, send_ref)
+
+
+def together(*values):
+    return lax.optimization_barrier(values)
 
 
 def local(
@@ -646,38 +635,13 @@
         static["Q"] = Q
         return kernel_call(functools.partial(body, **static), name, outs, *args, scratch=scratch, Q=Q)
 
-    def quarters(v):
-        across = over_mp(v, 2)
-        return v, across, over_mp(v, 1), over_mp(across, 1)
-
-    x4 = quarters(decoder_in[0])
-    w_self = jnp.concatenate([self_query.T, self_key.T, self_value.T, self_out.T])
+    x_here = decoder_in[0]
+    x_core = over_mp(x_here, 1)
+    x_across = over_mp(x_here, 2)
+    table_p = over_mp(bias_table.T, 1)
+    wq, table_p = together(self_query.T, table_p)
+    w_self = jnp.concatenate([wq, self_key.T, self_value.T, self_out.T])
     w_self_p = over_mp(w_self, 1)
-    table_p = over_mp(bias_table.T, 1)
-    eg4 = quarters(jnp.concatenate([encoder_states[0], out_grad[0]]))
-    w_cross = jnp.concatenate([cross_query.T, cross_key.T, cross_value.T, cross_out.T])
-    w_cross_p = over_mp(w_cross, 1)
-    up_p = over_mp(ffn_up, 1)
-    down_p = over_mp(ffn_down, 1)
-
-    def x_rows():
-        return Quarters(x4, Q)
-
-    def e_rows():
-        return Quarters(eg4, Q)
-
-    def g_rows():
-        return Quarters(eg4, Q, Q)
-
-    def self_w(*picks):
-        return Joined(w_self, w_self_p, picks, 4)
-
-    def cross_w(*picks):
-        return Joined(w_cross, w_cross_p, picks, 4)
-
-    up = Joined(ffn_up, up_p, (0,), 1)
-    down = Joined(ffn_down, down_p, (0,), 1)
-
     bucket_line = offset_buckets.reshape(1, L)
     bias, cross_mask = call(
         bias_body,
@@ -689,6 +653,27 @@
         dec_segments,
         enc_segments,
     )
+    x_across, bias = together(x_across, bias)
+    x4 = (x_here, x_across, x_core, over_mp(x_across, 1))
+
+    def x_rows():
+        return Quarters(x4, Q)
+
+    eg_here = jnp.concatenate([encoder_states[0], out_grad[0]])
+    eg_across = over_mp(eg_here, 2)
+    w_cross = jnp.concatenate([cross_query.T, cross_key.T, cross_value.T, cross_out.T])
+
+    def e_rows():
+        return Quarters(eg4, Q)
+
+    def g_rows():
+        return Quarters(eg4, Q, Q)
+
+    def self_w(*picks):
+        return Joined(w_self, w_self_p, picks, 4)
+
+    def cross_w(*picks):
+        return Joined(w_cross, w_cross_p, picks, 4)
 
     both_rows, both_all = shape((2 * Q, 2 * W)), shape((L, 2 * W))
     square = shape((2 * heads, 2 * Q, L))
@@ -706,6 +691,11 @@
         bias,
     )
     recv1 = over_mp(part1, 2)
+    w_cross_p = over_mp(w_cross, 1)
+    eg_across, q1 = together(eg_across, q1)
+    eg4 = (eg_here, eg_across, over_mp(eg_here, 1), over_mp(eg_across, 1))
+    up = Joined(ffn_up, over_mp(ffn_up, 1), (0,), 1)
+    down_p = over_mp(ffn_down, 1)
     k2, v2 = call(encoder_keys, "encoder_keys", [both_all, both_all], e_rows(), cross_w(1, 2))
     part2, x1, h2, q2, p2, o2 = call(
         cross_forward,
@@ -721,6 +711,8 @@
         cross_mask,
     )
     recv2 = over_mp(part2, 2)
+    down_p, h2 = together(down_p, h2)
+    down = Joined(ffn_down, down_p, (0,), 1)
     (grad_act,) = call(act_grads, "act_grads", [shape((2, 2 * Q, F))], g_rows(), down)
     part3, x2, a_own, du_own, send3 = call(
         ffn_both,
@@ -737,55 +729,54 @@
     recv_ffn = over_mp(send3, 1)
     quarter, quarter_f = shape((Q, D)), shape((Q, D), f32)
 
-    def grad_kernel(body, name, cols, *args, extra=(), scratch=(), **static):
+    def grad_kernel(body, name, cols, *args, extra=(), scratch=(), send_rows=0, **static):
         if split:
             keep = shape((dp_size // 2, D // dp_size, cols))
-            outs = [keep, keep, *extra]
+            outs = [keep, shape((send_rows, cols)) if send_rows else keep, *extra]
             scratch = [pltpu.VMEM((D, cols), f32), *scratch]
         else:
             outs = [shape((D, cols), f32), *extra]
         res = call(body, name, outs, *args, scratch=scratch, split=split, **static)
         return (res[:2], res[2:]) if split else (res[:1], res[1:])
 
-    def reduce_x(parts):
-        if not split:
-            return parts
-        keep, send = parts
-        recv = over_dp(send, 1)
-        return [(keep[i].astype(f32) + recv[i].astype(f32)) for i in range(dp_size // 2)]
-
-    def reduce_z(sums, count):
-        if not split:
-            total = lax.psum_scatter(sums[0], "dp", scatter_dimension=0, tiled=True)
-        else:
-            total = sums[0]
-            for i in range(1, dp_size // 2):
-                total = total + over_dp(sums[i].astype(bf16), 2 * i).astype(f32)
+    def over_x(parts):
+        return (parts[0], over_dp(parts[1], 1)) if split else parts
+
+    def first_half(pair):
+        return (pair[0][2:].astype(f32) + pair[1][2:].astype(f32)).astype(bf16)
+
+    def second_half(pair, recv):
+        return (pair[0][1].astype(f32) + pair[1][1].astype(f32) + recv[1].astype(f32)).astype(bf16)
+
+    def finish(pair, recv, last):
+        return pair[0][0].astype(f32) + pair[1][0].astype(f32) + recv[0].astype(f32) + last.astype(f32)
+
+    def scatter(parts):
+        return lax.psum_scatter(parts[0], "dp", scatter_dimension=0, tiled=True)
+
+    def columns(total, count):
         width = total.shape[1] // count
         return [total[:, i * width : (i + 1) * width] for i in range(count)]
 
-    down_parts, _ = grad_kernel(
-        down_weights, "down_weights", F, g_rows(), a_own, Part(recv_ffn, 1, 1), scratch=[pltpu.VMEM((L, F), bf16)]
-    )
-    up_parts, _ = grad_kernel(
-        up_weights, "up_weights", F, Part(send3, 0, 1), du_own, Part(recv_ffn, 0, 1), Part(recv_ffn, 2, 1)
-    )
-    y_keep, y_send = call(
-        ffn_out,
-        "ffn_out",
-        [quarter_f, quarter],
+    ffn_parts, _ = grad_kernel(
+        ffn_weights,
+        "ffn_weights",
+        2 * F,
+        g_rows(),
         a_own,
-        Part(send3, 1, 1),
-        down,
-        x2,
-        scratch=[pltpu.VMEM((2 * Q, D), f32)],
-    )
-    output = (y_keep + over_mp(y_send, 2).astype(f32)).astype(bf16)
-
+        Part(send3, 0, 1),
+        du_own,
+        Part(recv_ffn, 0, 1),
+        Part(recv_ffn, 1, 1),
+        Part(recv_ffn, 2, 1),
+        scratch=[pltpu.VMEM((L, F), bf16)],
+    )
     own_f = shape((L, W), f32)
     packed = shape((6 * Q, 2 * W))
     turned_f = pltpu.VMEM((2 * W, L), f32)
-    recv3 = after(recv3, down_parts, up_parts)
+    if split:
+        recv3, ffn_keep = together(recv3, ffn_parts[0])
+        ffn_parts = (ffn_keep, ffn_parts[1])
     part4, dx2, send4, do2, ds2, dq2, gain3 = call(
         cross_back,
         "cross_back",
@@ -802,34 +793,16 @@
         h2,
     )
     recv4 = over_mp(part4, 2)
+    if split:
+        do2, ffn_send = together(do2, ffn_parts[1])
+        ffn_parts = (ffn_parts[0], ffn_send)
     recv_h = over_mp(send4, 1)
     dk2, dv2, send_k = call(
         keys_body, "cross_keys", [own_f, own_f, packed], ds2, p2, q2, do2, dq2, o2, scratch=[turned_f, turned_f]
     )
     recv_k = over_mp(send_k, 1)
     pair_f, pair = shape((2, Q, D), f32), shape((2, Q, D))
-    enc_keep, enc_send, d2 = call(
-        encoder_grad,
-        "encoder_grad",
-        [pair_f, pair, both_all],
-        dk2,
-        dv2,
-        recv_k,
-        Part(w_cross, W, W),
-        Part(w_cross, 2 * W, W),
-    )
-    cross_parts, _ = grad_kernel(
-        cross_weights, "cross_weights", 4 * W, send4, recv_h, e_rows(), dq2, d2, o2, recv_k
-    )
-
-    def finish_rows(keep, send):
-        recv = over_mp(send, 1).astype(f32)
-        across = over_mp((keep[1] + recv[1]).astype(bf16), 2)
-        return keep[0] + recv[0] + across.astype(f32)
-
-    grad_encoder = finish_rows(enc_keep, enc_send).astype(bf16)
-
-    recv4 = after(recv4, cross_parts)
+    recv4, dk2 = together(recv4, dk2)
     dx1, gs, dq1, dk1, dv1, send_s, gain23, ds1 = call(
         self_back,
         "self_back",
@@ -850,31 +823,116 @@
     )
     recv_s = over_mp(send_s, 1)
     gs_oth = over_mp(gs, 1)
-    self_parts, (d1,) = grad_kernel(
-        self_weights, "self_weights", 4 * W, h1, gs, gs_oth, o1, dq1, dk1, dv1, recv_s, extra=[shape((L, 3 * W))]
-    )
-    in_keep, in_send, gain1 = call(
-        input_grad, "input_grad", [pair_f, pair, line], d1, Part(w_self, 0, 3 * W), h1, norm_gains
-    )
-    grad_rows, _ = norm_back(decoder_in[0].astype(f32), norm_gains[0:1], finish_rows(in_keep, in_send))
+    n = D // dp_size
+    if split:
+        ffn_pair = over_x(ffn_parts)
+    self_parts, (in_keep, in_send, small) = grad_kernel(
+        self_weights,
+        "self_weights",
+        4 * W,
+        h1,
+        gs,
+        gs_oth,
+        o1,
+        dq1,
+        dk1,
+        dv1,
+        recv_s,
+        Part(w_self, 0, 3 * W),
+        norm_gains,
+        ds1,
+        bucket_line,
+        gain23,
+        buckets=buckets,
+        wide=4 * heads * buckets,
+        extra=[pair_f, pair, shape((8, D), f32)],
+        scratch=[pltpu.VMEM((L, 3 * W), bf16)],
+        send_rows=D // 2 + 16,
+    )
+    if split:
+        recv_k, in_keep, ffn_half = together(recv_k, in_keep, first_half(ffn_pair))
+        ffn_recv = over_dp(ffn_half, 2)
+    cross_parts, (enc_keep, enc_send, out_keep, out_send) = grad_kernel(
+        cross_weights,
+        "cross_weights",
+        4 * W,
+        send4,
+        recv_h,
+        e_rows(),
+        dq2,
+        dk2,
+        dv2,
+        o2,
+        recv_k,
+        Part(w_cross, W, W),
+        Part(w_cross, 2 * W, W),
+        a_own,
+        Part(send3, 1, 1),
+        down,
+        x2,
+        extra=[pair_f, pair, quarter_f, quarter],
+        scratch=[pltpu.VMEM((L, 2 * W), bf16), pltpu.VMEM((2 * Q, D), f32)],
+    )
+
+    def halves(v):
+        high = v.astype(bf16)
+        return [high, (v - high.astype(f32)).astype(bf16)]
+
+    def passed_on(keep, recv):
+        return (keep[1] + recv[1].astype(f32)).astype(bf16)
+
+    def add_tail(v, tail):
+        return v + (tail[:8].astype(f32) + tail[8:].astype(f32))
+
+    if split:
+        self_recv = over_dp(self_parts[1], 1)
+        in_send, enc_send, cross_send, self_recv, ffn_recv = together(
+            in_send, enc_send, cross_parts[1], self_recv, ffn_recv
+        )
+        cross_parts = (cross_parts[0], cross_send)
+    in_recv, enc_recv = over_mp(in_send, 1), over_mp(enc_send, 1)
+    across = jnp.concatenate([passed_on(in_keep, in_recv), passed_on(enc_keep, enc_recv), out_send])
+    across = over_mp(across, 2)
+    if split:
+        keep, recv = self_parts[0], self_recv
+        m = D // 2
+        small = add_tail(small, recv[m:])
+        half = (keep[2:].reshape(2 * n, 4 * W).astype(f32) + recv[2 * n : m].astype(f32)).astype(bf16)
+        half_recv = over_dp(jnp.concatenate([half, *halves(small)]), 2)
+        cross_pair = over_x(cross_parts)
+        half_recv, cross_recv = together(half_recv, cross_pair[1])
+        cross_pair = (cross_pair[0], cross_recv)
+        small = add_tail(small, half_recv[2 * n :])
+        ffn_last = over_dp(second_half(ffn_pair, ffn_recv), 4)
+        quarter_sum = keep[1].astype(f32) + recv[n : 2 * n].astype(f32) + half_recv[n : 2 * n].astype(f32)
+        last = over_dp(jnp.concatenate([quarter_sum.astype(bf16), *halves(small)]), 4)
+        last, ffn_last = together(last, ffn_last)
+        small = add_tail(small, last[n:])
+        self_total = (
+            keep[0].astype(f32) + recv[:n].astype(f32) + half_recv[:n].astype(f32) + last[:n].astype(f32)
+        )
+        ffn_total = finish(ffn_pair, ffn_recv, ffn_last)
+        cross_recv = over_dp(first_half(cross_pair), 2)
+        cross_total = finish(cross_pair, cross_recv, over_dp(second_half(cross_pair, cross_recv), 4))
+    else:
+        small = lax.psum(small, "dp")
+        ffn_total, cross_total, self_total = map(scatter, (ffn_parts, cross_parts, self_parts))
+    grad_up, grad_down = ffn_total[:, :F], ffn_total[:, F:]
+
+    def sum_rows(keep, recv, last):
+        return keep[0] + recv[0].astype(f32) + last.astype(f32)
+
+    grad_rows, _ = norm_back(decoder_in[0].astype(f32), norm_gains[0:1], sum_rows(in_keep, in_recv, across[:Q]))
     grad_decoder = (dx1 + grad_rows).astype(bf16)
-
-    (small,) = call(
-        small_sums, "small_sums", [shape((16, D), f32)], ds1, bucket_line, gain1, gain23, buckets=buckets
-    )
+    grad_encoder = sum_rows(enc_keep, enc_recv, across[Q : 2 * Q]).astype(bf16)
+    output = (out_keep + across[2 * Q :].astype(f32)).astype(bf16)
+
     small = small + over_mp(small, 1)
     small = small + over_mp(small, 2)
-    flip = dp_size // 2
-    while flip:
-        small = small + over_dp(small, flip)
-        flip //= 2
     gain_total = small[:3]
-    table_total = small[3 : 3 + 4 * heads, :buckets].T
-
-    (grad_down,) = reduce_z(reduce_x(down_parts), 1)
-    (grad_up,) = reduce_z(reduce_x(up_parts), 1)
-    grad_cq, grad_ck, grad_cv, grad_co = reduce_z(reduce_x(cross_parts), 4)
-    grad_sq, grad_sk, grad_sv, grad_so = reduce_z(reduce_x(self_parts), 4)
+    table_total = small[3, : 4 * heads * buckets].reshape(4 * heads, buckets).T
+    grad_cq, grad_ck, grad_cv, grad_co = columns(cross_total, 4)
+    grad_sq, grad_sk, grad_sv, grad_so = columns(self_total, 4)
 
     def row(v):
         return v.reshape((1,) + v.shape)

time: 208 us -> 181 us (0.87)
  starting transfers between devices: 42.9 us -> 28.3 us
  Pallas kernels: 84.8 us -> 74.7 us
  waiting for transfers between devices: 58.8 us -> 53.3 us
  local copies, waits for them, and re-layouts: 11.1 us -> 13.2 us
    ppermute x19 -> x9, starting transfers between devices: 25.4 us -> 10.4 us  [over_dp(): return lax.ppermute(v, 'dp', [(i, i ^ flip) for i in range(dp_size)])]
    pallas_call x17 -> x12, Pallas kernels: 84.8 us -> 74.7 us  [kernel_call(): pl.pallas_call(whole, out_shape=outs, in_specs=[pl.BlockSpec(memory_space...]
    ppermute x19 -> x9, waiting for transfers between devices: 35.4 us -> 28.6 us  [over_dp(): return lax.ppermute(v, 'dp', [(i, i ^ flip) for i in range(dp_size)])]
    convert_element_type x8 -> x10, other arithmetic: 1.92 us -> 4.18 us  [the longest x2 2.2 us: second_half(): (pair[0][1].astype(f32) + pair[1][1].astype(f32) + recv[1].astype(f32)).a...]
    ppermute x27 -> x25, waiting for transfers between devices: 23.4 us -> 24.7 us  [over_mp(): return lax.ppermute(v, 'mp', [(i, i ^ flip) for i in range(4)])]
    unnamed x84 -> x86, local copies, waits for them, and re-layouts: 7.56 us -> 8.76 us
    ppermute x27 -> x25, starting transfers between devices: 17.5 us -> 17.9 us  [over_mp(): return lax.ppermute(v, 'mp', [(i, i ^ flip) for i in range(4)])]
  transfers between devices with their start and end apart: 46 -> 34, of which waited for: 16 -> 16; matrix products, arithmetic and copies ran while one was open for 5% -> 6% of each run, Pallas kernels for 38% -> 34%
where the time goes in v3:
time: 181 us
  Pallas kernels  74.7 us (41%)
  waiting for transfers between devices  53.3 us (29%)
  starting transfers between devices  28.3 us (16%)
  local copies, waits for them, and re-layouts  13.2 us (7%)
  other arithmetic  10.3 us (6%)
    pallas_call x12, Pallas kernels, kernel_call(): pl.pallas_call(whole, out_shape=outs, in_specs=[pl.BlockSpec(memory_space...  74.7 us
    ppermute x9, waiting for transfers between devices, over_dp(): return lax.ppermute(v, 'dp', [(i, i ^ flip) for i in range(dp_size)])  28.6 us
    ppermute x25, waiting for transfers between devices, over_mp(): return lax.ppermute(v, 'mp', [(i, i ^ flip) for i in range(4)])  24.7 us
    ppermute x25, starting transfers between devices, over_mp(): return lax.ppermute(v, 'mp', [(i, i ^ flip) for i in range(4)])  17.9 us
    ppermute x9, starting transfers between devices, over_dp(): return lax.ppermute(v, 'dp', [(i, i ^ flip) for i in range(dp_size)])  10.4 us
    unnamed x86, local copies, waits for them, and re-layouts  8.76 us
  transfers between devices with their start and end apart: 34, of which 16 were waited for; matrix products, arithmetic and copies ran while one was open for 6% of the time, Pallas kernels for 34%

profile of v3, /device:TPU:0, one launch (start us, length us, event | category | flops | bytes accessed | tf_op | source)
XLA Modules:
  0.0 181.0 jit_solution(12855466334664639274)
XLA Ops:
  4.1 2.7 %collective-permute-start.1 = (bf16[128,768]{1,0:T(8,128)(2,1)S(1)}, bf16[128,768]{1,0:T(8,128)(2,1)}, u32[]{:S(2)}, u32[]{:S(2)}) collective-permute-start(bf16[128,768]{1,0:T(8,128)(2,1)S(1)} %bitcast.60), channel_id=1, source_target_pairs={{0,2},{1,3},{2,0},{3,1},{4,6},{5,7},{6,4},{7,5},{8,10},{9,11},{10,... | collective-permute-start | bytes 589832 | tf_op jit(solution)/shard_map/ppermute | solution.py:629
  7.5 4.9 %bias.1 = (f32[6,256,512]{2,1,0:T(8,128)}, f32[256,512]{1,0:T(8,128)}) custom-call(f32[3,32]{1,0:T(4,128)} %bitcast.76, f32[3,32]{1,0:T(4,128)} %copy-done.41, s32[1,512]{1,0:T(1,128)} %bitcast.72, s32[1,512]{1,0:T(1,128)} %refs_3_.2, s32[1,512]{1,0:T(1,128)} %refs_4_.5), custom_call_target="tpu_custom_call" | custom-call | bytes 3676928 | tf_op jit(solution)/shard_map/bias/pallas_call | solution.py:186
  15.3 7.6 %self_forward.1 = (bf16[256,768]{1,0:T(8,128)(2,1)}, bf16[512,768]{1,0:T(8,128)(2,1)}, bf16[256,384]{1,0:T(8,128)(2,1)}, bf16[512,384]{1,0:T(8,128)(2,1)}, bf16[...) custom-call(bf16[128,768]{1,0:T(8,128)(2,1)} %bitcast.58, ...), custom_call_target="tpu_custom_call" | custom-call | bytes 10232832 | tf_op jit(solution)/shard_map/self_forward/pallas_call | solution.py:186
  27.5 3.5 %encoder_keys.1 = (bf16[512,384]{1,0:T(8,128)(2,1)}, bf16[512,384]{1,0:T(8,128)(2,1)}) custom-call(bf16[256,768]{1,0:T(8,128)(2,1)} %copy-done.2, bf16[256,768]{1,0:T(8,128)(2,1)} %copy-done.5, bf16[256,768]{1,0:T(8,128)(2,1)} %copy-done.6, bf16[256,768]{1,0:T(8,128)(2,1)} %copy-done.7, bf16[768,768]{1,0:T(8,128)(2,1)} %copy-done, bf16[768,768]{1,0:T(8,128)(2,1)} %copy-done.4), custom_call_target="tpu_custom_call" | custom-call | bytes 4718592 | tf_op jit(solution)/shard_map/encoder_keys/pallas_call | solution.py:186
  31.0 4.9 %collective-permute-done.8.refs_5_ = bf16[256,768]{1,0:T(8,128)(2,1)S(1)} collective-permute-done((bf16[256,768]{1,0:T(8,128)(2,1)}, bf16[256,768]{1,0:T(8,128)(2,1)S(1)}, u32[]{:S(2)}, u32[]{:S(2)}) %collective-permute-start.8) | collective-permute-done | bytes 393248 | tf_op jit(solution)/shard_map/ppermute | solution.py:629
  36.7 8.0 %cross_forward.1 = (bf16[256,768]{1,0:T(8,128)(2,1)}, f32[256,768]{1,0:T(8,128)}, bf16[256,768]{1,0:T(8,128)(2,1)}, bf16[256,384]{1,0:T(8,128)(2,1)}, bf16[6,256...) custom-call(bf16[128,768]{1,0:T(8,128)(2,1)} %bitcast.59, bf16[128,768]{1,0:T(8,128)(2,1)} %collective-permute-done.1.refs_1_, ...), custom_call_target="tpu_custom_call" | custom-call | bytes 8791040 | tf_op jit(solution)/shard_map/cross_forward/pallas_call | solution.py:186
  46.2 3.7 %act_grads.1.refs_6_ = bf16[2,256,768]{2,1,0:T(8,128)(2,1)} custom-call(bf16[256,768]{1,0:T(8,128)(2,1)} %copy-done.2, bf16[256,768]{1,0:T(8,128)(2,1)} %copy-done.5, bf16[256,768]{1,0:T(8,128)(2,1)} %copy-done.6, bf16[256,768]{1,0:T(8,128)(2,1)} %copy-done.7, bf16[768,768]{1,0:T(8,128)(2,1)} %refs_15_.1, ...), custom_call_target="tpu_custom_call" | custom-call | bytes 4718592 | tf_op jit(solution)/shard_map/act_grads/pallas_call | solution.py:186
  50.0 5.6 %collective-permute-done.10.refs_2_ = bf16[256,768]{1,0:T(8,128)(2,1)S(1)} collective-permute-done((bf16[256,768]{1,0:T(8,128)(2,1)}, bf16[256,768]{1,0:T(8,128)(2,1)S(1)}, u32[]{:S(2)}, u32[]{:S(2)}) %collective-permute-start.10) | collective-permute-done | bytes 393248 | tf_op jit(solution)/shard_map/ppermute | solution.py:629
  56.3 6.2 %ffn_both.1 = (bf16[256,768]{1,0:T(8,128)(2,1)}, f32[256,768]{1,0:T(8,128)}, bf16[256,768]{1,0:T(8,128)(2,1)}, bf16[256,768]{1,0:T(8,128)(2,1)}, bf16[3,256,768]{2,1,0:T(8,128)(2,1)}) custom-call(f32[256,768]{1,0:T(8,128)} %get-tuple-element.105.refs_0_.refs_3_, bf16[256,768]{1,0:T(8,128)(2,1)} %get-tuple-element.106.refs_1_, bf16[256,768]{1,0:T(8,128)(2,1)} %copy-done.32, ...), custom_call_target="tpu_custom_call" | custom-call | bytes 7873536 | tf_op jit(solution)/shard_map/ffn_both/pallas_call | solution.py:186
  66.7 5.6 %ffn_weights.1 = (bf16[4,96,1536]{2,1,0:T(8,128)(2,1)}, bf16[4,96,1536]{2,1,0:T(8,128)(2,1)}) custom-call(bf16[256,768]{1,0:T(8,128)(2,1)} %copy-done.2, bf16[256,768]{1,0:T(8,128)(2,1)} %copy-done.5, bf16[256,768]{1,0:T(8,128)(2,1)} %copy-done.6, bf16[256,768]{1,0:T(8,128)(2,1)} %copy-done.7, bf16[256,768]{1,0:T(8,128)(2,1)} %get-tuple-element.110.refs_4_.refs_13_, ...), custom_call_target="tpu_custom_call" | custom-call | bytes 9437184 | tf_op jit(solution)/shard_map/ffn_weights/pallas_call | solution.py:186
  72.4 2.0 %collective-permute-done.13.refs_5_ = bf16[256,768]{1,0:T(8,128)(2,1)S(1)} collective-permute-done((bf16[256,768]{1,0:T(8,128)(2,1)}, bf16[256,768]{1,0:T(8,128)(2,1)S(1)}, u32[]{:S(2)}, u32[]{:S(2)}) %collective-permute-start.13) | collective-permute-done | bytes 393248 | tf_op jit(solution)/shard_map/ppermute | solution.py:629
  75.1 7.7 %cross_back.1 = (bf16[256,768]{1,0:T(8,128)(2,1)}, f32[256,768]{1,0:T(8,128)}, bf16[2,256,768]{2,1,0:T(8,128)(2,1)}, bf16[256,384]{1,0:T(8,128)(2,1)}, bf16[6,25...) custom-call(bf16[256,768]{1,0:T(8,128)(2,1)} %copy-done.2, bf16[256,768]{1,0:T(8,128)(2,1)} %copy-done.5, ...), custom_call_target="tpu_custom_call" | custom-call | bytes 12223488 | tf_op jit(solution)/shard_map/cross_back/pallas_call | solution.py:186
  85.9 4.5 %cross_keys.1 = (f32[512,192]{1,0:T(8,128)}, f32[512,192]{1,0:T(8,128)}, bf16[768,384]{1,0:T(8,128)(2,1)}) custom-call(bf16[6,256,512]{2,1,0:T(8,128)(2,1)} %get-tuple-element.121.refs_0_, bf16[6,256,512]{2,1,0:T(8,128)(2,1)} %get-tuple-element.116.refs_12_.refs_1_, bf16[256,384]{1,0:T(8,128)(2,1)} %get-tuple-element.122.refs_2_, ...), custom_call_target="tpu_custom_call" | custom-call | bytes 5308416 | tf_op jit(solution)/shard_map/cross_keys/pallas_call | solution.py:186
  90.4 4.6 %collective-permute-done.16.refs_2_ = bf16[256,768]{1,0:T(8,128)(2,1)S(1)} collective-permute-done((bf16[256,768]{1,0:T(8,128)(2,1)}, bf16[256,768]{1,0:T(8,128)(2,1)S(1)}, u32[]{:S(2)}, u32[]{:S(2)}) %collective-permute-start.16) | collective-permute-done | bytes 393248 | tf_op jit(solution)/shard_map/ppermute | solution.py:629
  95.8 7.2 %self_back.1 = (f32[128,768]{1,0:T(8,128)}, bf16[256,768]{1,0:T(8,128)(2,1)}, bf16[256,384]{1,0:T(8,128)(2,1)}, f32[512,192]{1,0:T(8,128)}, f32[512,192]{1,0:T(8...) custom-call(f32[256,768]{1,0:T(8,128)} %get-tuple-element.132.refs_0_, ...), custom_call_target="tpu_custom_call" | custom-call | bytes 11461632 | tf_op jit(solution)/shard_map/self_back/pallas_call | solution.py:186
  104.1 2.3 %collective-permute-done.18.refs_2_ = bf16[256,768]{1,0:T(8,128)(2,1)S(1)} collective-permute-done((bf16[256,768]{1,0:T(8,128)(2,1)}, bf16[256,768]{1,0:T(8,128)(2,1)S(1)}, u32[]{:S(2)}, u32[]{:S(2)}) %collective-permute-start.18) | collective-permute-done | bytes 393248 | tf_op jit(solution)/shard_map/ppermute | solution.py:629
  107.4 8.0 %self_weights.1 = (bf16[4,96,768]{2,1,0:T(8,128)(2,1)}, bf16[400,768]{1,0:T(8,128)(2,1)}, f32[2,128,768]{2,1,0:T(8,128)}, bf16[2,128,768]{2,1,0:T(8,128)(2,1)}, f32[8,768]{1,0:T(8,128)}) custom-call(bf16[512,768]{1,0:T(8,128)(2,1)} %get-tuple-element.131.refs_0_, bf16[256,768]{1,0:T(8,128)(2,1)} %get-tuple-element.140.refs_1_, bf16[256,768]{1,0:T(8,128)(2,1)} %copy-done.28, ...), custom_call_target="tpu_custom_call" | custom-call | bytes 8539136 | tf_op jit(solution)/shard_map/self_weights/pallas_call | solution.py:186
  120.5 7.7 %cross_weights.1 = (bf16[4,96,768]{2,1,0:T(8,128)(2,1)}, bf16[4,96,768]{2,1,0:T(8,128)(2,1)}, f32[2,128,768]{2,1,0:T(8,128)}, bf16[2,128,768]{2,1,0:T(8,128)(2,1...) custom-call(bf16[2,256,768]{2,1,0:T(8,128)(2,1)} %get-tuple-element.118.refs_0_, bf16[2,256,768]{2,1,0:T(8,128)(2,1)} %copy-done.15, ...), custom_call_target="tpu_custom_call" | custom-call | bytes 14942208 | tf_op jit(solution)/shard_map/cross_weights/pallas_call | solution.py:186
  128.1 3.5 %collective-permute-done.21 = bf16[400,768]{1,0:T(8,128)(2,1)S(1)} collective-permute-done((bf16[400,768]{1,0:T(8,128)(2,1)}, bf16[400,768]{1,0:T(8,128)(2,1)S(1)}, u32[]{:S(2)}, u32[]{:S(2)}) %collective-permute-start.21) | collective-permute-done | bytes 614432 | tf_op jit(solution)/shard_map/ppermute | solution.py:632
  134.2 2.7 %collective-permute-start.29 = (bf16[96,1536]{1,0:T(8,128)(2,1)S(1)}, bf16[96,1536]{1,0:T(8,128)(2,1)S(1)}, u32[]{:S(2)}, u32[]{:S(2)}) collective-permute-start(bf16[96,1536]{1,0:T(8,128)(2,1)S(1)} %fusion.11), channel_id=1, source_target_pairs={{0,16},{4,20},{8,24},{12,28},{16,0},{20,4},{24,8},{28,12},{1,17},{... | collective-permute-start | bytes 884744 | tf_op jit(solution)/shard_map/ppermute | solution.py:632
  143.2 8.1 %collective-permute-done.26 = bf16[208,768]{1,0:T(8,128)(2,1)S(1)} collective-permute-done((bf16[208,768]{1,0:T(8,128)(2,1)S(1)}, bf16[208,768]{1,0:T(8,128)(2,1)S(1)}, u32[]{:S(2)}, u32[]{:S(2)}) %collective-permute-start.26) | collective-permute-done | bytes 319520 | tf_op jit(solution)/shard_map/ppermute | solution.py:632
  151.4 1.9 %collective-permute-done.27 = bf16[4,96,768]{2,1,0:T(8,128)(2,1)S(1)} collective-permute-done((bf16[4,96,768]{2,1,0:T(8,128)(2,1)S(1)}, bf16[4,96,768]{2,1,0:T(8,128)(2,1)S(1)}, u32[]{:S(2)}, u32[]{:S(2)}) %collective-permute-start.27) | collective-permute-done | bytes 589856 | tf_op jit(solution)/shard_map/ppermute | solution.py:632
  155.0 7.8 %collective-permute-done.28 = bf16[112,768]{1,0:T(8,128)(2,1)S(1)} collective-permute-done((bf16[112,768]{1,0:T(8,128)(2,1)S(1)}, bf16[112,768]{1,0:T(8,128)(2,1)S(1)}, u32[]{:S(2)}, u32[]{:S(2)}) %collective-permute-start.28) | collective-permute-done | bytes 172064 | tf_op jit(solution)/shard_map/ppermute | solution.py:632
  172.7 6.5 %collective-permute-done.31 = bf16[96,768]{1,0:T(8,128)(2,1)S(1)} collective-permute-done((bf16[96,768]{1,0:T(8,128)(2,1)S(1)}, bf16[96,768]{1,0:T(8,128)(2,1)S(1)}, u32[]{:S(2)}, u32[]{:S(2)}) %collective-permute-start.31) | collective-permute-done | bytes 147488 | tf_op jit(solution)/shard_map/ppermute | solution.py:632
  (177 shorter events, 52.6 us)
Async XLA Ops:
  3.7 11.1 %collective-permute-start.5 = (bf16[768,768]{1,0:T(8,128)(2,1)S(1)}, bf16[768,768]{1,0:T(8,128)(2,1)}, u32[]{:S(2)}, u32[]{:S(2)}) collective-permute-start(bf16[768,768]{1,0:T(8,128)(2,1)S(1)} %pad_maximum_fusion.refs_5_.refs_8_), channel_id=1, source_target_pairs={{0,1},{1,0},{2,3},{3,2},{4,5},{5,4},{6,7},{7,6},{8,9},{9,8},{10,11... | collective-permute-start | bytes 3538952 | tf_op jit(solution)/shard_map/ppermute | solution.py:629
  4.1 8.3 %collective-permute-start.1 = (bf16[128,768]{1,0:T(8,128)(2,1)S(1)}, bf16[128,768]{1,0:T(8,128)(2,1)}, u32[]{:S(2)}, u32[]{:S(2)}) collective-permute-start(bf16[128,768]{1,0:T(8,128)(2,1)S(1)} %bitcast.60), channel_id=1, source_target_pairs={{0,2},{1,3},{2,0},{3,1},{4,6},{5,7},{6,4},{7,5},{8,10},{9,11},{10,... | collective-permute-start | bytes 589832 | tf_op jit(solution)/shard_map/ppermute | solution.py:629
  6.9 18.8 %collective-permute-start.9 = (bf16[768,768]{1,0:T(8,128)(2,1)S(1)}, bf16[768,768]{1,0:T(8,128)(2,1)S(1)}, u32[]{:S(2)}, u32[]{:S(2)}) collective-permute-start(bf16[768,768]{1,0:T(8,128)(2,1)S(1)} %pad_maximum_fusion.1.refs_4_.refs_7_.refs_8_.refs_11_.refs_12_), channel_id=1, source_target_pairs={{0,1},{1,0},{2,3},{3,2},{4,5},{5,4},{6,7},{7,6},{8,9},{9,8},{10,11... | collective-permute-start | bytes 3538952 | tf_op jit(solution)/shard_map/ppermute | solution.py:629
  12.6 11.5 %collective-permute-start = (bf16[256,768]{1,0:T(8,128)(2,1)S(1)}, bf16[256,768]{1,0:T(8,128)(2,1)S(1)}, u32[]{:S(2)}, u32[]{:S(2)}) collective-permute-start(bf16[256,768]{1,0:T(8,128)(2,1)S(1)} %pad_maximum_fusion.3.refs_0_.refs_2_), channel_id=1, source_target_pairs={{0,2},{1,3},{2,0},{3,1},{4,6},{5,7},{6,4},{7,5},{8,10},{9,11},{10,... | collective-permute-start | bytes 1179656 | tf_op jit(solution)/shard_map/ppermute | solution.py:629
  14.1 10.0 %collective-permute-start.6 = (bf16[256,768]{1,0:T(8,128)(2,1)S(1)}, bf16[256,768]{1,0:T(8,128)(2,1)S(1)}, u32[]{:S(2)}, u32[]{:S(2)}) collective-permute-start(bf16[256,768]{1,0:T(8,128)(2,1)S(1)} %pad_maximum_fusion.3.refs_0_.refs_2_), channel_id=1, source_target_pairs={{0,1},{1,0},{2,3},{3,2},{4,5},{5,4},{6,7},{7,6},{8,9},{9,8},{10,11... | collective-permute-start | bytes 1179656 | tf_op jit(solution)/shard_map/ppermute | solution.py:629
  14.4 31.9 %collective-permute-start.12 = (bf16[768,768]{1,0:T(8,128)(2,1)S(1)}, bf16[768,768]{1,0:T(8,128)(2,1)}, u32[]{:S(2)}, u32[]{:S(2)}) collective-permute-start(bf16[768,768]{1,0:T(8,128)(2,1)S(1)} %copy-done.10), channel_id=1, source_target_pairs={{0,1},{1,0},{2,3},{3,2},{4,5},{5,4},{6,7},{7,6},{8,9},{9,8},{10,11... | collective-permute-start | bytes 3538952 | tf_op jit(solution)/shard_map/ppermute | solution.py:629
  15.0 34.9 %collective-permute-start.11 = (bf16[768,768]{1,0:T(8,128)(2,1)}, bf16[768,768]{1,0:T(8,128)(2,1)}, u32[]{:S(2)}, u32[]{:S(2)}) collective-permute-start(bf16[768,768]{1,0:T(8,128)(2,1)} %refs_4_.8), channel_id=1, source_target_pairs={{0,1},{1,0},{2,3},{3,2},{4,5},{5,4},{6,7},{7,6},{8,9},{9,8},{10,11... | collective-permute-start | bytes 3538952 | tf_op jit(solution)/shard_map/ppermute | solution.py:629
  24.1 11.7 %collective-permute-start.8 = (bf16[256,768]{1,0:T(8,128)(2,1)}, bf16[256,768]{1,0:T(8,128)(2,1)S(1)}, u32[]{:S(2)}, u32[]{:S(2)}) collective-permute-start(bf16[256,768]{1,0:T(8,128)(2,1)} %get-tuple-element.101.refs_4_), channel_id=1, source_target_pairs={{0,2},{1,3},{2,0},{3,1},{4,6},{5,7},{6,4},{7,5},{8,10},{9,11},{10,... | collective-permute-start | bytes 1179656 | tf_op jit(solution)/shard_map/ppermute | solution.py:629
  44.6 11.0 %collective-permute-start.10 = (bf16[256,768]{1,0:T(8,128)(2,1)}, bf16[256,768]{1,0:T(8,128)(2,1)S(1)}, u32[]{:S(2)}, u32[]{:S(2)}) collective-permute-start(bf16[256,768]{1,0:T(8,128)(2,1)} %get-tuple-element.106.refs_1_), channel_id=1, source_target_pairs={{0,2},{1,3},{2,0},{3,1},{4,6},{5,7},{6,4},{7,5},{8,10},{9,11},{10,... | collective-permute-start | bytes 1179656 | tf_op jit(solution)/shard_map/ppermute | solution.py:629
  62.6 11.7 %collective-permute-start.13 = (bf16[256,768]{1,0:T(8,128)(2,1)}, bf16[256,768]{1,0:T(8,128)(2,1)S(1)}, u32[]{:S(2)}, u32[]{:S(2)}) collective-permute-start(bf16[256,768]{1,0:T(8,128)(2,1)} %get-tuple-element.109.refs_4_), channel_id=1, source_target_pairs={{0,2},{1,3},{2,0},{3,1},{4,6},{5,7},{6,4},{7,5},{8,10},{9,11},{10,... | collective-permute-start | bytes 1179656 | tf_op jit(solution)/shard_map/ppermute | solution.py:629
  82.8 33.2 %collective-permute-start.20 = (bf16[4,96,1536]{2,1,0:T(8,128)(2,1)}, bf16[4,96,1536]{2,1,0:T(8,128)(2,1)S(1)}, u32[]{:S(2)}, u32[]{:S(2)}) collective-permute-start(bf16[4,96,1536]{2,1,0:T(8,128)(2,1)} %get-tuple-element.149), channel_id=1, source_target_pairs={{0,4},{4,0},{8,12},{12,8},{16,20},{20,16},{24,28},{28,24},{1,5},{5... | collective-permute-start | bytes 3538952 | tf_op jit(solution)/shard_map/ppermute | solution.py:632
  84.4 10.6 %collective-permute-start.16 = (bf16[256,768]{1,0:T(8,128)(2,1)}, bf16[256,768]{1,0:T(8,128)(2,1)S(1)}, u32[]{:S(2)}, u32[]{:S(2)}) collective-permute-start(bf16[256,768]{1,0:T(8,128)(2,1)} %get-tuple-element.120.refs_1_), channel_id=1, source_target_pairs={{0,2},{1,3},{2,0},{3,1},{4,6},{5,7},{6,4},{7,5},{8,10},{9,11},{10,... | collective-permute-start | bytes 1179656 | tf_op jit(solution)/shard_map/ppermute | solution.py:629
  103.6 13.5 %collective-permute-start.17 = (bf16[768,384]{1,0:T(8,128)(2,1)}, bf16[768,384]{1,0:T(8,128)(2,1)S(1)}, u32[]{:S(2)}, u32[]{:S(2)}) collective-permute-start(bf16[768,384]{1,0:T(8,128)(2,1)} %get-tuple-element.130), channel_id=1, source_target_pairs={{0,1},{1,0},{2,3},{3,2},{4,5},{5,4},{6,7},{7,6},{8,9},{9,8},{10,11... | collective-permute-start | bytes 1769480 | tf_op jit(solution)/shard_map/ppermute | solution.py:629
  103.6 15.9 %collective-permute-start.15 = (bf16[2,256,768]{2,1,0:T(8,128)(2,1)S(1)}, bf16[2,256,768]{2,1,0:T(8,128)(2,1)S(1)}, u32[]{:S(2)}, u32[]{:S(2)}) collective-permute-start(bf16[2,256,768]{2,1,0:T(8,128)(2,1)S(1)} %copy-done.14), channel_id=1, source_target_pairs={{0,1},{1,0},{2,3},{3,2},{4,5},{5,4},{6,7},{7,6},{8,9},{9,8},{10,11... | collective-permute-start | bytes 2359304 | tf_op jit(solution)/shard_map/ppermute | solution.py:629
  115.5 16.2 %collective-permute-start.21 = (bf16[400,768]{1,0:T(8,128)(2,1)}, bf16[400,768]{1,0:T(8,128)(2,1)S(1)}, u32[]{:S(2)}, u32[]{:S(2)}) collective-permute-start(bf16[400,768]{1,0:T(8,128)(2,1)} %get-tuple-element.156), channel_id=1, source_target_pairs={{0,4},{4,0},{8,12},{12,8},{16,20},{20,16},{24,28},{28,24},{1,5},{5... | collective-permute-start | bytes 1843208 | tf_op jit(solution)/shard_map/ppermute | solution.py:632
  117.0 15.4 %collective-permute-start.22 = (bf16[2,96,1536]{2,1,0:T(8,128)(2,1)}, bf16[2,96,1536]{2,1,0:T(8,128)(2,1)}, u32[]{:S(2)}, u32[]{:S(2)}) collective-permute-start(bf16[2,96,1536]{2,1,0:T(8,128)(2,1)} %add_convert_fusion), channel_id=1, source_target_pairs={{0,8},{4,12},{8,0},{12,4},{16,24},{20,28},{24,16},{28,20},{1,9},{5... | collective-permute-start | bytes 1769480 | tf_op jit(solution)/shard_map/ppermute | solution.py:632
  132.5 7.6 %collective-permute-start.24 = (bf16[2,128,768]{2,1,0:T(8,128)(2,1)}, bf16[2,128,768]{2,1,0:T(8,128)(2,1)S(1)}, u32[]{:S(2)}, u32[]{:S(2)}) collective-permute-start(bf16[2,128,768]{2,1,0:T(8,128)(2,1)} %get-tuple-element.160), channel_id=1, source_target_pairs={{0,1},{1,0},{2,3},{3,2},{4,5},{5,4},{6,7},{7,6},{8,9},{9,8},{10,11... | collective-permute-start | bytes 1179656 | tf_op jit(solution)/shard_map/ppermute | solution.py:629
  134.2 20.8 %collective-permute-start.29 = (bf16[96,1536]{1,0:T(8,128)(2,1)S(1)}, bf16[96,1536]{1,0:T(8,128)(2,1)S(1)}, u32[]{:S(2)}, u32[]{:S(2)}) collective-permute-start(bf16[96,1536]{1,0:T(8,128)(2,1)S(1)} %fusion.11), channel_id=1, source_target_pairs={{0,16},{4,20},{8,24},{12,28},{16,0},{20,4},{24,8},{28,12},{1,17},{... | collective-permute-start | bytes 884744 | tf_op jit(solution)/shard_map/ppermute | solution.py:632
  136.9 14.5 %collective-permute-start.26 = (bf16[208,768]{1,0:T(8,128)(2,1)S(1)}, bf16[208,768]{1,0:T(8,128)(2,1)S(1)}, u32[]{:S(2)}, u32[]{:S(2)}) collective-permute-start(bf16[208,768]{1,0:T(8,128)(2,1)S(1)} %pad_maximum_fusion.4), channel_id=1, source_target_pairs={{0,8},{4,12},{8,0},{12,4},{16,24},{20,28},{24,16},{28,20},{1,9},{5... | collective-permute-start | bytes 958472 | tf_op jit(solution)/shard_map/ppermute | solution.py:632
  138.5 14.7 %collective-permute-start.27 = (bf16[4,96,768]{2,1,0:T(8,128)(2,1)S(1)}, bf16[4,96,768]{2,1,0:T(8,128)(2,1)S(1)}, u32[]{:S(2)}, u32[]{:S(2)}) collective-permute-start(bf16[4,96,768]{2,1,0:T(8,128)(2,1)S(1)} %copy-done.42), channel_id=1, source_target_pairs={{0,4},{4,0},{8,12},{12,8},{16,20},{20,16},{24,28},{28,24},{1,5},{5... | collective-permute-start | bytes 1769480 | tf_op jit(solution)/shard_map/ppermute | solution.py:632
  141.7 29.7 %collective-permute-start.25 = (bf16[384,768]{1,0:T(8,128)(2,1)}, bf16[384,768]{1,0:T(8,128)(2,1)S(1)}, u32[]{:S(2)}, u32[]{:S(2)}) collective-permute-start(bf16[384,768]{1,0:T(8,128)(2,1)} %pad_maximum_fusion.2), channel_id=1, source_target_pairs={{0,2},{1,3},{2,0},{3,1},{4,6},{5,7},{6,4},{7,5},{8,10},{9,11},{10,... | collective-permute-start | bytes 1769480 | tf_op jit(solution)/shard_map/ppermute | solution.py:629
  153.4 9.5 %collective-permute-start.28 = (bf16[112,768]{1,0:T(8,128)(2,1)S(1)}, bf16[112,768]{1,0:T(8,128)(2,1)S(1)}, u32[]{:S(2)}, u32[]{:S(2)}) collective-permute-start(bf16[112,768]{1,0:T(8,128)(2,1)S(1)} %pad_maximum_fusion.5), channel_id=1, source_target_pairs={{0,16},{4,20},{8,24},{12,28},{16,0},{20,4},{24,8},{28,12},{1,17},{... | collective-permute-start | bytes 516104 | tf_op jit(solution)/shard_map/ppermute | solution.py:632
  154.5 15.6 %collective-permute-start.30 = (bf16[2,96,768]{2,1,0:T(8,128)(2,1)}, bf16[2,96,768]{2,1,0:T(8,128)(2,1)}, u32[]{:S(2)}, u32[]{:S(2)}) collective-permute-start(bf16[2,96,768]{2,1,0:T(8,128)(2,1)} %add_convert_fusion.1), channel_id=1, source_target_pairs={{0,8},{4,12},{8,0},{12,4},{16,24},{20,28},{24,16},{28,20},{1,9},{5... | collective-permute-start | bytes 884744 | tf_op jit(solution)/shard_map/ppermute | solution.py:632
  171.3 7.9 %collective-permute-start.31 = (bf16[96,768]{1,0:T(8,128)(2,1)S(1)}, bf16[96,768]{1,0:T(8,128)(2,1)S(1)}, u32[]{:S(2)}, u32[]{:S(2)}) collective-permute-start(bf16[96,768]{1,0:T(8,128)(2,1)S(1)} %fusion.21), channel_id=1, source_target_pairs={{0,16},{4,20},{8,24},{12,28},{16,0},{20,4},{24,8},{28,12},{1,17},{... | collective-permute-start | bytes 442376 | tf_op jit(solution)/shard_map/ppermute | solution.py:632
  (53 other events, 230.3 us)

commit v4 on v3

--- a/solution.py
+++ b/solution.py
@@ -800,7 +800,6 @@
     dk2, dv2, send_k = call(
         keys_body, "cross_keys", [own_f, own_f, packed], ds2, p2, q2, do2, dq2, o2, scratch=[turned_f, turned_f]
     )
-    recv_k = over_mp(send_k, 1)
     pair_f, pair = shape((2, Q, D), f32), shape((2, Q, D))
     recv4, dk2 = together(recv4, dk2)
     dx1, gs, dq1, dk1, dv1, send_s, gain23, ds1 = call(
@@ -824,8 +823,34 @@
     recv_s = over_mp(send_s, 1)
     gs_oth = over_mp(gs, 1)
     n = D // dp_size
-    if split:
-        ffn_pair = over_x(ffn_parts)
+    send_k, ds1 = together(send_k, ds1)
+    recv_k = over_mp(send_k, 1)
+    cross_parts, (enc_keep, enc_send, out_keep, out_send) = grad_kernel(
+        cross_weights,
+        "cross_weights",
+        4 * W,
+        send4,
+        recv_h,
+        e_rows(),
+        dq2,
+        dk2,
+        dv2,
+        o2,
+        recv_k,
+        Part(w_cross, W, W),
+        Part(w_cross, 2 * W, W),
+        a_own,
+        Part(send3, 1, 1),
+        down,
+        x2,
+        extra=[pair_f, pair, quarter_f, quarter],
+        scratch=[pltpu.VMEM((L, 2 * W), bf16), pltpu.VMEM((2 * Q, D), f32)],
+    )
+    if split:
+        ffn_pair, cross_pair = over_x(ffn_parts), over_x(cross_parts)
+        recv_s, cross_keep, ffn_half = together(recv_s, cross_pair[0], first_half(ffn_pair))
+        cross_pair = (cross_keep, cross_pair[1])
+        ffn_recv = over_dp(ffn_half, 2)
     self_parts, (in_keep, in_send, small) = grad_kernel(
         self_weights,
         "self_weights",
@@ -849,31 +874,6 @@
         scratch=[pltpu.VMEM((L, 3 * W), bf16)],
         send_rows=D // 2 + 16,
     )
-    if split:
-        recv_k, in_keep, ffn_half = together(recv_k, in_keep, first_half(ffn_pair))
-        ffn_recv = over_dp(ffn_half, 2)
-    cross_parts, (enc_keep, enc_send, out_keep, out_send) = grad_kernel(
-        cross_weights,
-        "cross_weights",
-        4 * W,
-        send4,
-        recv_h,
-        e_rows(),
-        dq2,
-        dk2,
-        dv2,
-        o2,
-        recv_k,
-        Part(w_cross, W, W),
-        Part(w_cross, 2 * W, W),
-        a_own,
-        Part(send3, 1, 1),
-        down,
-        x2,
-        extra=[pair_f, pair, quarter_f, quarter],
-        scratch=[pltpu.VMEM((L, 2 * W), bf16), pltpu.VMEM((2 * Q, D), f32)],
-    )
-
     def halves(v):
         high = v.astype(bf16)
         return [high, (v - high.astype(f32)).astype(bf16)]
@@ -886,34 +886,28 @@
 
     if split:
         self_recv = over_dp(self_parts[1], 1)
-        in_send, enc_send, cross_send, self_recv, ffn_recv = together(
-            in_send, enc_send, cross_parts[1], self_recv, ffn_recv
-        )
-        cross_parts = (cross_parts[0], cross_send)
+        in_send, enc_send, ffn_recv = together(in_send, enc_send, ffn_recv)
     in_recv, enc_recv = over_mp(in_send, 1), over_mp(enc_send, 1)
     across = jnp.concatenate([passed_on(in_keep, in_recv), passed_on(enc_keep, enc_recv), out_send])
     across = over_mp(across, 2)
     if split:
+        self_recv, in_recv, enc_recv = together(self_recv, in_recv, enc_recv)
         keep, recv = self_parts[0], self_recv
         m = D // 2
         small = add_tail(small, recv[m:])
-        half = (keep[2:].reshape(2 * n, 4 * W).astype(f32) + recv[2 * n : m].astype(f32)).astype(bf16)
-        half_recv = over_dp(jnp.concatenate([half, *halves(small)]), 2)
-        cross_pair = over_x(cross_parts)
-        half_recv, cross_recv = together(half_recv, cross_pair[1])
-        cross_pair = (cross_pair[0], cross_recv)
-        small = add_tail(small, half_recv[2 * n :])
+        tail = halves(small)
+        self_total = keep[0].astype(f32) + recv[:n].astype(f32)
+        for i in range(1, dp_size // 2):
+            block = (keep[i].astype(f32) + recv[i * n : (i + 1) * n].astype(f32)).astype(bf16)
+            last = over_dp(jnp.concatenate([block, *tail]), (0, 4, 2, 6)[i])
+            self_total = self_total + last[:n].astype(f32)
+            small = add_tail(small, last[n:])
         ffn_last = over_dp(second_half(ffn_pair, ffn_recv), 4)
-        quarter_sum = keep[1].astype(f32) + recv[n : 2 * n].astype(f32) + half_recv[n : 2 * n].astype(f32)
-        last = over_dp(jnp.concatenate([quarter_sum.astype(bf16), *halves(small)]), 4)
-        last, ffn_last = together(last, ffn_last)
-        small = add_tail(small, last[n:])
-        self_total = (
-            keep[0].astype(f32) + recv[:n].astype(f32) + half_recv[:n].astype(f32) + last[:n].astype(f32)
-        )
         ffn_total = finish(ffn_pair, ffn_recv, ffn_last)
         cross_recv = over_dp(first_half(cross_pair), 2)
-        cross_total = finish(cross_pair, cross_recv, over_dp(second_half(cross_pair, cross_recv), 4))
+        cross_last = over_dp(second_half(cross_pair, cross_recv), 4)
+        small, across, cross_last = together(small, across, cross_last)
+        cross_total = finish(cross_pair, cross_recv, cross_last)
     else:
         small = lax.psum(small, "dp")
         ffn_total, cross_total, self_total = map(scatter, (ffn_parts, cross_parts, self_parts))

time: 181 us -> 177 us (0.978); the launches traced: 181 us -> 174 us
  other arithmetic: 10.3 us -> 3.94 us
  starting transfers between devices: 28.3 us -> 32.9 us
  waiting for transfers between devices: 53.3 us -> 49.4 us
    ppermute x9 -> x10, starting transfers between devices: 10.4 us -> 15.5 us  [over_dp(): return lax.ppermute(v, 'dp', [(i, i ^ flip) for i in range(dp_size)])]
    ppermute x9 -> x10, waiting for transfers between devices: 28.6 us -> 23.6 us  [over_dp(): return lax.ppermute(v, 'dp', [(i, i ^ flip) for i in range(dp_size)])]
    convert_element_type x2, other arithmetic: 2.2 us -> 0.18 us  [second_half(): (pair[0][1].astype(f32) + pair[1][1].astype(f32) + recv[1].astype(f32)).a...]
    add x2, other arithmetic: 2.16 us -> 0.22 us  [finish(): pair[0][0].astype(f32) + pair[1][0].astype(f32) + recv[0].astype(f32)]
    unnamed x86 -> x80, local copies, waits for them, and re-layouts: 8.76 us -> 7.71 us
  transfers between devices with their start and end apart: 34 -> 35, of which waited for: 16 -> 17; matrix products, arithmetic and copies ran while one was open for 6% -> 3% of each run, Pallas kernels for 34% -> 35%
where the time goes in v4:
time: 177 us; the launch traced here: 174 us
  Pallas kernels  74.8 us (42%)
  waiting for transfers between devices  49.4 us (28%)
  starting transfers between devices  32.9 us (19%)
  local copies, waits for them, and re-layouts  12.2 us (7%)
  other arithmetic  3.94 us (2%)
    pallas_call x12, Pallas kernels, kernel_call(): pl.pallas_call(whole, out_shape=outs, in_specs=[pl.BlockSpec(memory_space...  74.8 us
    ppermute x25, waiting for transfers between devices, over_mp(): return lax.ppermute(v, 'mp', [(i, i ^ flip) for i in range(4)])  25.7 us
    ppermute x10, waiting for transfers between devices, over_dp(): return lax.ppermute(v, 'dp', [(i, i ^ flip) for i in range(dp_size)])  23.6 us
    ppermute x25, starting transfers between devices, over_mp(): return lax.ppermute(v, 'mp', [(i, i ^ flip) for i in range(4)])  17.4 us
    ppermute x10, starting transfers between devices, over_dp(): return lax.ppermute(v, 'dp', [(i, i ^ flip) for i in range(dp_size)])  15.5 us
    unnamed x80, local copies, waits for them, and re-layouts  7.71 us
  transfers between devices with their start and end apart: 35, of which 17 were waited for; matrix products, arithmetic and copies ran while one was open for 3% of the time, Pallas kernels for 35%

profile of v4, /device:TPU:0, one launch (start us, length us, event | category | flops | bytes accessed | tf_op | source)
XLA Modules:
  0.0 174.4 jit_solution(198261840947987043)
XLA Ops:
  4.1 2.7 %collective-permute-start.1 = (bf16[128,768]{1,0:T(8,128)(2,1)S(1)}, bf16[128,768]{1,0:T(8,128)(2,1)}, u32[]{:S(2)}, u32[]{:S(2)}) collective-permute-start(bf16[128,768]{1,0:T(8,128)(2,1)S(1)} %bitcast.63), channel_id=1, source_target_pairs={{0,2},{1,3},{2,0},{3,1},{4,6},{5,7},{6,4},{7,5},{8,10},{9,11},{10,... | collective-permute-start | bytes 589832 | tf_op jit(solution)/shard_map/ppermute | solution.py:629
  7.5 4.9 %bias.1 = (f32[6,256,512]{2,1,0:T(8,128)}, f32[256,512]{1,0:T(8,128)}) custom-call(f32[3,32]{1,0:T(4,128)} %bitcast.79, f32[3,32]{1,0:T(4,128)} %copy-done.35, s32[1,512]{1,0:T(1,128)} %bitcast.75, s32[1,512]{1,0:T(1,128)} %refs_3_.2, s32[1,512]{1,0:T(1,128)} %refs_4_.5), custom_call_target="tpu_custom_call" | custom-call | bytes 3676928 | tf_op jit(solution)/shard_map/bias/pallas_call | solution.py:186
  15.3 7.6 %self_forward.1 = (bf16[256,768]{1,0:T(8,128)(2,1)}, bf16[512,768]{1,0:T(8,128)(2,1)}, bf16[256,384]{1,0:T(8,128)(2,1)}, bf16[512,384]{1,0:T(8,128)(2,1)}, bf16[...) custom-call(bf16[128,768]{1,0:T(8,128)(2,1)} %bitcast.61, ...), custom_call_target="tpu_custom_call" | custom-call | bytes 10232832 | tf_op jit(solution)/shard_map/self_forward/pallas_call | solution.py:186
  27.5 3.5 %encoder_keys.1 = (bf16[512,384]{1,0:T(8,128)(2,1)}, bf16[512,384]{1,0:T(8,128)(2,1)}) custom-call(bf16[256,768]{1,0:T(8,128)(2,1)} %copy-done.2, bf16[256,768]{1,0:T(8,128)(2,1)} %copy-done.5, bf16[256,768]{1,0:T(8,128)(2,1)} %copy-done.6, bf16[256,768]{1,0:T(8,128)(2,1)} %copy-done.7, bf16[768,768]{1,0:T(8,128)(2,1)} %copy-done, bf16[768,768]{1,0:T(8,128)(2,1)} %copy-done.4), custom_call_target="tpu_custom_call" | custom-call | bytes 4718592 | tf_op jit(solution)/shard_map/encoder_keys/pallas_call | solution.py:186
  31.0 4.8 %collective-permute-done.8.refs_5_ = bf16[256,768]{1,0:T(8,128)(2,1)S(1)} collective-permute-done((bf16[256,768]{1,0:T(8,128)(2,1)}, bf16[256,768]{1,0:T(8,128)(2,1)S(1)}, u32[]{:S(2)}, u32[]{:S(2)}) %collective-permute-start.8) | collective-permute-done | bytes 393248 | tf_op jit(solution)/shard_map/ppermute | solution.py:629
  36.6 8.0 %cross_forward.1 = (bf16[256,768]{1,0:T(8,128)(2,1)}, f32[256,768]{1,0:T(8,128)}, bf16[256,768]{1,0:T(8,128)(2,1)}, bf16[256,384]{1,0:T(8,128)(2,1)}, bf16[6,256...) custom-call(bf16[128,768]{1,0:T(8,128)(2,1)} %bitcast.62, bf16[128,768]{1,0:T(8,128)(2,1)} %collective-permute-done.1.refs_1_, ...), custom_call_target="tpu_custom_call" | custom-call | bytes 8791040 | tf_op jit(solution)/shard_map/cross_forward/pallas_call | solution.py:186
  46.2 3.7 %act_grads.1.refs_6_ = bf16[2,256,768]{2,1,0:T(8,128)(2,1)} custom-call(bf16[256,768]{1,0:T(8,128)(2,1)} %copy-done.2, bf16[256,768]{1,0:T(8,128)(2,1)} %copy-done.5, bf16[256,768]{1,0:T(8,128)(2,1)} %copy-done.6, bf16[256,768]{1,0:T(8,128)(2,1)} %copy-done.7, bf16[768,768]{1,0:T(8,128)(2,1)} %refs_15_.1, ...), custom_call_target="tpu_custom_call" | custom-call | bytes 4718592 | tf_op jit(solution)/shard_map/act_grads/pallas_call | solution.py:186
  50.0 5.6 %collective-permute-done.10.refs_2_ = bf16[256,768]{1,0:T(8,128)(2,1)S(1)} collective-permute-done((bf16[256,768]{1,0:T(8,128)(2,1)}, bf16[256,768]{1,0:T(8,128)(2,1)S(1)}, u32[]{:S(2)}, u32[]{:S(2)}) %collective-permute-start.10) | collective-permute-done | bytes 393248 | tf_op jit(solution)/shard_map/ppermute | solution.py:629
  56.3 6.2 %ffn_both.1 = (bf16[256,768]{1,0:T(8,128)(2,1)}, f32[256,768]{1,0:T(8,128)}, bf16[256,768]{1,0:T(8,128)(2,1)}, bf16[256,768]{1,0:T(8,128)(2,1)}, bf16[3,256,768]{2,1,0:T(8,128)(2,1)}) custom-call(f32[256,768]{1,0:T(8,128)} %get-tuple-element.107.refs_0_.refs_3_, bf16[256,768]{1,0:T(8,128)(2,1)} %get-tuple-element.108.refs_1_, bf16[256,768]{1,0:T(8,128)(2,1)} %copy-done.26, ...), custom_call_target="tpu_custom_call" | custom-call | bytes 7873536 | tf_op jit(solution)/shard_map/ffn_both/pallas_call | solution.py:186
  66.7 5.6 %ffn_weights.1 = (bf16[4,96,1536]{2,1,0:T(8,128)(2,1)}, bf16[4,96,1536]{2,1,0:T(8,128)(2,1)}) custom-call(bf16[256,768]{1,0:T(8,128)(2,1)} %copy-done.2, bf16[256,768]{1,0:T(8,128)(2,1)} %copy-done.5, bf16[256,768]{1,0:T(8,128)(2,1)} %copy-done.6, bf16[256,768]{1,0:T(8,128)(2,1)} %copy-done.7, bf16[256,768]{1,0:T(8,128)(2,1)} %get-tuple-element.112.refs_4_.refs_13_, ...), custom_call_target="tpu_custom_call" | custom-call | bytes 9437184 | tf_op jit(solution)/shard_map/ffn_weights/pallas_call | solution.py:186
  72.3 2.1 %collective-permute-done.13.refs_5_ = bf16[256,768]{1,0:T(8,128)(2,1)S(1)} collective-permute-done((bf16[256,768]{1,0:T(8,128)(2,1)}, bf16[256,768]{1,0:T(8,128)(2,1)S(1)}, u32[]{:S(2)}, u32[]{:S(2)}) %collective-permute-start.13) | collective-permute-done | bytes 393248 | tf_op jit(solution)/shard_map/ppermute | solution.py:629
  75.1 7.8 %cross_back.1 = (bf16[256,768]{1,0:T(8,128)(2,1)}, f32[256,768]{1,0:T(8,128)}, bf16[2,256,768]{2,1,0:T(8,128)(2,1)}, bf16[256,384]{1,0:T(8,128)(2,1)}, bf16[6,25...) custom-call(bf16[256,768]{1,0:T(8,128)(2,1)} %copy-done.2, bf16[256,768]{1,0:T(8,128)(2,1)} %copy-done.5, ...), custom_call_target="tpu_custom_call" | custom-call | bytes 12223488 | tf_op jit(solution)/shard_map/cross_back/pallas_call | solution.py:186
  86.0 4.5 %cross_keys.1 = (f32[512,192]{1,0:T(8,128)}, f32[512,192]{1,0:T(8,128)}, bf16[768,384]{1,0:T(8,128)(2,1)}) custom-call(bf16[6,256,512]{2,1,0:T(8,128)(2,1)} %get-tuple-element.123.refs_0_, bf16[6,256,512]{2,1,0:T(8,128)(2,1)} %get-tuple-element.118.refs_12_.refs_1_, bf16[256,384]{1,0:T(8,128)(2,1)} %get-tuple-element.124.refs_2_, ...), custom_call_target="tpu_custom_call" | custom-call | bytes 5308416 | tf_op jit(solution)/shard_map/cross_keys/pallas_call | solution.py:186
  90.5 4.6 %collective-permute-done.16.refs_2_ = bf16[256,768]{1,0:T(8,128)(2,1)S(1)} collective-permute-done((bf16[256,768]{1,0:T(8,128)(2,1)}, bf16[256,768]{1,0:T(8,128)(2,1)S(1)}, u32[]{:S(2)}, u32[]{:S(2)}) %collective-permute-start.16) | collective-permute-done | bytes 393248 | tf_op jit(solution)/shard_map/ppermute | solution.py:629
  95.8 7.2 %self_back.1 = (f32[128,768]{1,0:T(8,128)}, bf16[256,768]{1,0:T(8,128)(2,1)}, bf16[256,384]{1,0:T(8,128)(2,1)}, f32[512,192]{1,0:T(8,128)}, f32[512,192]{1,0:T(8...) custom-call(f32[256,768]{1,0:T(8,128)} %get-tuple-element.133.refs_0_, ...), custom_call_target="tpu_custom_call" | custom-call | bytes 11461632 | tf_op jit(solution)/shard_map/self_back/pallas_call | solution.py:186
  106.0 8.0 %cross_weights.1 = (bf16[4,96,768]{2,1,0:T(8,128)(2,1)}, bf16[4,96,768]{2,1,0:T(8,128)(2,1)}, f32[2,128,768]{2,1,0:T(8,128)}, bf16[2,128,768]{2,1,0:T(8,128)(2,1...) custom-call(bf16[2,256,768]{2,1,0:T(8,128)(2,1)} %get-tuple-element.120.refs_0_, bf16[2,256,768]{2,1,0:T(8,128)(2,1)} %copy-done.14, ...), custom_call_target="tpu_custom_call" | custom-call | bytes 14942208 | tf_op jit(solution)/shard_map/cross_weights/pallas_call | solution.py:186
  117.4 7.8 %self_weights.1 = (bf16[4,96,768]{2,1,0:T(8,128)(2,1)}, bf16[400,768]{1,0:T(8,128)(2,1)}, f32[2,128,768]{2,1,0:T(8,128)}, bf16[2,128,768]{2,1,0:T(8,128)(2,1)}, f32[8,768]{1,0:T(8,128)}) custom-call(bf16[512,768]{1,0:T(8,128)(2,1)} %get-tuple-element.144.refs_0_, bf16[256,768]{1,0:T(8,128)(2,1)} %get-tuple-element.145.refs_1_, bf16[256,768]{1,0:T(8,128)(2,1)} %copy-done.24, ...), custom_call_target="tpu_custom_call" | custom-call | bytes 8539136 | tf_op jit(solution)/shard_map/self_weights/pallas_call | solution.py:186
  125.2 4.5 %collective-permute-done.29 = bf16[4,96,768]{2,1,0:T(8,128)(2,1)S(1)} collective-permute-done((bf16[4,96,768]{2,1,0:T(8,128)(2,1)}, bf16[4,96,768]{2,1,0:T(8,128)(2,1)S(1)}, u32[]{:S(2)}, u32[]{:S(2)}) %collective-permute-start.29) | collective-permute-done | bytes 589856 | tf_op jit(solution)/shard_map/ppermute | solution.py:632
  131.5 2.6 %collective-permute-start.32 = (bf16[96,1536]{1,0:T(8,128)(2,1)S(1)}, bf16[96,1536]{1,0:T(8,128)(2,1)S(1)}, u32[]{:S(2)}, u32[]{:S(2)}) collective-permute-start(bf16[96,1536]{1,0:T(8,128)(2,1)S(1)} %fusion.10), channel_id=1, source_target_pairs={{0,16},{4,20},{8,24},{12,28},{16,0},{20,4},{24,8},{28,12},{1,17},{... | collective-permute-start | bytes 884744 | tf_op jit(solution)/shard_map/ppermute | solution.py:632
  136.1 8.0 %collective-permute-done.30 = bf16[2,96,768]{2,1,0:T(8,128)(2,1)S(1)} collective-permute-done((bf16[2,96,768]{2,1,0:T(8,128)(2,1)S(1)}, bf16[2,96,768]{2,1,0:T(8,128)(2,1)S(1)}, u32[]{:S(2)}, u32[]{:S(2)}) %collective-permute-start.30) | collective-permute-done | bytes 294944 | tf_op jit(solution)/shard_map/ppermute | solution.py:632
  144.8 5.4 %collective-permute-done.32 = bf16[96,1536]{1,0:T(8,128)(2,1)S(1)} collective-permute-done((bf16[96,1536]{1,0:T(8,128)(2,1)S(1)}, bf16[96,1536]{1,0:T(8,128)(2,1)S(1)}, u32[]{:S(2)}, u32[]{:S(2)}) %collective-permute-start.32) | collective-permute-done | bytes 294944 | tf_op jit(solution)/shard_map/ppermute | solution.py:632
  151.5 6.1 %collective-permute-start.26 = (bf16[112,768]{1,0:T(8,128)(2,1)S(1)}, bf16[112,768]{1,0:T(8,128)(2,1)S(1)}, u32[]{:S(2)}, u32[]{:S(2)}) collective-permute-start(bf16[112,768]{1,0:T(8,128)(2,1)S(1)} %get-tuple-element.196), channel_id=1, source_target_pairs={{0,8},{4,12},{8,0},{12,4},{16,24},{20,28},{24,16},{28,20},{1,9},{5... | collective-permute-start | bytes 516104 | tf_op jit(solution)/shard_map/ppermute | solution.py:632
  159.3 3.3 %collective-permute-done.25 = bf16[112,768]{1,0:T(8,128)(2,1)S(1)} collective-permute-done((bf16[112,768]{1,0:T(8,128)(2,1)S(1)}, bf16[112,768]{1,0:T(8,128)(2,1)S(1)}, u32[]{:S(2)}, u32[]{:S(2)}) %collective-permute-start.25) | collective-permute-done | bytes 172064 | tf_op jit(solution)/shard_map/ppermute | solution.py:632
  162.8 2.1 %collective-permute-done.27 = bf16[112,768]{1,0:T(8,128)(2,1)S(1)} collective-permute-done((bf16[112,768]{1,0:T(8,128)(2,1)S(1)}, bf16[112,768]{1,0:T(8,128)(2,1)S(1)}, u32[]{:S(2)}, u32[]{:S(2)}) %collective-permute-start.27) | collective-permute-done | bytes 172064 | tf_op jit(solution)/shard_map/ppermute | solution.py:632
  (169 shorter events, 46.4 us)
Async XLA Ops:
  3.7 11.1 %collective-permute-start.5 = (bf16[768,768]{1,0:T(8,128)(2,1)S(1)}, bf16[768,768]{1,0:T(8,128)(2,1)}, u32[]{:S(2)}, u32[]{:S(2)}) collective-permute-start(bf16[768,768]{1,0:T(8,128)(2,1)S(1)} %pad_maximum_fusion.refs_5_.refs_8_), channel_id=1, source_target_pairs={{0,1},{1,0},{2,3},{3,2},{4,5},{5,4},{6,7},{7,6},{8,9},{9,8},{10,11... | collective-permute-start | bytes 3538952 | tf_op jit(solution)/shard_map/ppermute | solution.py:629
  6.9 18.8 %collective-permute-start.9 = (bf16[768,768]{1,0:T(8,128)(2,1)S(1)}, bf16[768,768]{1,0:T(8,128)(2,1)S(1)}, u32[]{:S(2)}, u32[]{:S(2)}) collective-permute-start(bf16[768,768]{1,0:T(8,128)(2,1)S(1)} %pad_maximum_fusion.1.refs_4_.refs_7_.refs_8_.refs_11_.refs_12_), channel_id=1, source_target_pairs={{0,1},{1,0},{2,3},{3,2},{4,5},{5,4},{6,7},{7,6},{8,9},{9,8},{10,11... | collective-permute-start | bytes 3538952 | tf_op jit(solution)/shard_map/ppermute | solution.py:629
  12.6 11.5 %collective-permute-start = (bf16[256,768]{1,0:T(8,128)(2,1)S(1)}, bf16[256,768]{1,0:T(8,128)(2,1)S(1)}, u32[]{:S(2)}, u32[]{:S(2)}) collective-permute-start(bf16[256,768]{1,0:T(8,128)(2,1)S(1)} %pad_maximum_fusion.3.refs_0_.refs_2_), channel_id=1, source_target_pairs={{0,2},{1,3},{2,0},{3,1},{4,6},{5,7},{6,4},{7,5},{8,10},{9,11},{10,... | collective-permute-start | bytes 1179656 | tf_op jit(solution)/shard_map/ppermute | solution.py:629
  14.1 10.0 %collective-permute-start.6 = (bf16[256,768]{1,0:T(8,128)(2,1)S(1)}, bf16[256,768]{1,0:T(8,128)(2,1)S(1)}, u32[]{:S(2)}, u32[]{:S(2)}) collective-permute-start(bf16[256,768]{1,0:T(8,128)(2,1)S(1)} %pad_maximum_fusion.3.refs_0_.refs_2_), channel_id=1, source_target_pairs={{0,1},{1,0},{2,3},{3,2},{4,5},{5,4},{6,7},{7,6},{8,9},{9,8},{10,11... | collective-permute-start | bytes 1179656 | tf_op jit(solution)/shard_map/ppermute | solution.py:629
  14.4 31.9 %collective-permute-start.12 = (bf16[768,768]{1,0:T(8,128)(2,1)S(1)}, bf16[768,768]{1,0:T(8,128)(2,1)}, u32[]{:S(2)}, u32[]{:S(2)}) collective-permute-start(bf16[768,768]{1,0:T(8,128)(2,1)S(1)} %copy-done.10), channel_id=1, source_target_pairs={{0,1},{1,0},{2,3},{3,2},{4,5},{5,4},{6,7},{7,6},{8,9},{9,8},{10,11... | collective-permute-start | bytes 3538952 | tf_op jit(solution)/shard_map/ppermute | solution.py:629
  15.0 35.0 %collective-permute-start.11 = (bf16[768,768]{1,0:T(8,128)(2,1)}, bf16[768,768]{1,0:T(8,128)(2,1)}, u32[]{:S(2)}, u32[]{:S(2)}) collective-permute-start(bf16[768,768]{1,0:T(8,128)(2,1)} %refs_4_.8), channel_id=1, source_target_pairs={{0,1},{1,0},{2,3},{3,2},{4,5},{5,4},{6,7},{7,6},{8,9},{9,8},{10,11... | collective-permute-start | bytes 3538952 | tf_op jit(solution)/shard_map/ppermute | solution.py:629
  24.1 11.7 %collective-permute-start.8 = (bf16[256,768]{1,0:T(8,128)(2,1)}, bf16[256,768]{1,0:T(8,128)(2,1)S(1)}, u32[]{:S(2)}, u32[]{:S(2)}) collective-permute-start(bf16[256,768]{1,0:T(8,128)(2,1)} %get-tuple-element.103.refs_4_), channel_id=1, source_target_pairs={{0,2},{1,3},{2,0},{3,1},{4,6},{5,7},{6,4},{7,5},{8,10},{9,11},{10,... | collective-permute-start | bytes 1179656 | tf_op jit(solution)/shard_map/ppermute | solution.py:629
  44.6 11.0 %collective-permute-start.10 = (bf16[256,768]{1,0:T(8,128)(2,1)}, bf16[256,768]{1,0:T(8,128)(2,1)S(1)}, u32[]{:S(2)}, u32[]{:S(2)}) collective-permute-start(bf16[256,768]{1,0:T(8,128)(2,1)} %get-tuple-element.108.refs_1_), channel_id=1, source_target_pairs={{0,2},{1,3},{2,0},{3,1},{4,6},{5,7},{6,4},{7,5},{8,10},{9,11},{10,... | collective-permute-start | bytes 1179656 | tf_op jit(solution)/shard_map/ppermute | solution.py:629
  62.7 11.7 %collective-permute-start.13 = (bf16[256,768]{1,0:T(8,128)(2,1)}, bf16[256,768]{1,0:T(8,128)(2,1)S(1)}, u32[]{:S(2)}, u32[]{:S(2)}) collective-permute-start(bf16[256,768]{1,0:T(8,128)(2,1)} %get-tuple-element.111.refs_4_), channel_id=1, source_target_pairs={{0,2},{1,3},{2,0},{3,1},{4,6},{5,7},{6,4},{7,5},{8,10},{9,11},{10,... | collective-permute-start | bytes 1179656 | tf_op jit(solution)/shard_map/ppermute | solution.py:629
  82.9 31.8 %collective-permute-start.20 = (bf16[4,96,1536]{2,1,0:T(8,128)(2,1)}, bf16[4,96,1536]{2,1,0:T(8,128)(2,1)S(1)}, u32[]{:S(2)}, u32[]{:S(2)}) collective-permute-start(bf16[4,96,1536]{2,1,0:T(8,128)(2,1)} %get-tuple-element.152), channel_id=1, source_target_pairs={{0,4},{4,0},{8,12},{12,8},{16,20},{20,16},{24,28},{28,24},{1,5},{5... | collective-permute-start | bytes 3538952 | tf_op jit(solution)/shard_map/ppermute | solution.py:632
  84.5 10.6 %collective-permute-start.16 = (bf16[256,768]{1,0:T(8,128)(2,1)}, bf16[256,768]{1,0:T(8,128)(2,1)S(1)}, u32[]{:S(2)}, u32[]{:S(2)}) collective-permute-start(bf16[256,768]{1,0:T(8,128)(2,1)} %get-tuple-element.122.refs_1_), channel_id=1, source_target_pairs={{0,2},{1,3},{2,0},{3,1},{4,6},{5,7},{6,4},{7,5},{8,10},{9,11},{10,... | collective-permute-start | bytes 1179656 | tf_op jit(solution)/shard_map/ppermute | solution.py:629
  86.0 17.7 %collective-permute-start.15 = (bf16[2,256,768]{2,1,0:T(8,128)(2,1)}, bf16[2,256,768]{2,1,0:T(8,128)(2,1)S(1)}, u32[]{:S(2)}, u32[]{:S(2)}) collective-permute-start(bf16[2,256,768]{2,1,0:T(8,128)(2,1)} %get-tuple-element.120.refs_0_), channel_id=1, source_target_pairs={{0,1},{1,0},{2,3},{3,2},{4,5},{5,4},{6,7},{7,6},{8,9},{9,8},{10,11... | collective-permute-start | bytes 2359304 | tf_op jit(solution)/shard_map/ppermute | solution.py:629
  103.2 11.7 %collective-permute-start.19 = (bf16[768,384]{1,0:T(8,128)(2,1)}, bf16[768,384]{1,0:T(8,128)(2,1)S(1)}, u32[]{:S(2)}, u32[]{:S(2)}) collective-permute-start(bf16[768,384]{1,0:T(8,128)(2,1)} %get-tuple-element.149), channel_id=1, source_target_pairs={{0,1},{1,0},{2,3},{3,2},{4,5},{5,4},{6,7},{7,6},{8,9},{9,8},{10,11... | collective-permute-start | bytes 1769480 | tf_op jit(solution)/shard_map/ppermute | solution.py:629
  103.7 13.0 %collective-permute-start.18 = (bf16[256,768]{1,0:T(8,128)(2,1)}, bf16[256,768]{1,0:T(8,128)(2,1)S(1)}, u32[]{:S(2)}, u32[]{:S(2)}) collective-permute-start(bf16[256,768]{1,0:T(8,128)(2,1)} %get-tuple-element.145.refs_1_), channel_id=1, source_target_pairs={{0,1},{1,0},{2,3},{3,2},{4,5},{5,4},{6,7},{7,6},{8,9},{9,8},{10,11... | collective-permute-start | bytes 1179656 | tf_op jit(solution)/shard_map/ppermute | solution.py:629
  114.1 15.6 %collective-permute-start.29 = (bf16[4,96,768]{2,1,0:T(8,128)(2,1)}, bf16[4,96,768]{2,1,0:T(8,128)(2,1)S(1)}, u32[]{:S(2)}, u32[]{:S(2)}) collective-permute-start(bf16[4,96,768]{2,1,0:T(8,128)(2,1)} %get-tuple-element.169), channel_id=1, source_target_pairs={{0,4},{4,0},{8,12},{12,8},{16,20},{20,16},{24,28},{28,24},{1,5},{5... | collective-permute-start | bytes 1769480 | tf_op jit(solution)/shard_map/ppermute | solution.py:632
  114.8 16.6 %collective-permute-start.22 = (bf16[2,96,1536]{2,1,0:T(8,128)(2,1)S(1)}, bf16[2,96,1536]{2,1,0:T(8,128)(2,1)S(1)}, u32[]{:S(2)}, u32[]{:S(2)}) collective-permute-start(bf16[2,96,1536]{2,1,0:T(8,128)(2,1)S(1)} %add_convert_fusion), channel_id=1, source_target_pairs={{0,8},{4,12},{8,0},{12,4},{16,24},{20,28},{24,16},{28,20},{1,9},{5... | collective-permute-start | bytes 1769480 | tf_op jit(solution)/shard_map/ppermute | solution.py:632
  129.8 14.3 %collective-permute-start.30 = (bf16[2,96,768]{2,1,0:T(8,128)(2,1)S(1)}, bf16[2,96,768]{2,1,0:T(8,128)(2,1)S(1)}, u32[]{:S(2)}, u32[]{:S(2)}) collective-permute-start(bf16[2,96,768]{2,1,0:T(8,128)(2,1)S(1)} %add_convert_fusion.2), channel_id=1, source_target_pairs={{0,8},{4,12},{8,0},{12,4},{16,24},{20,28},{24,16},{28,20},{1,9},{5... | collective-permute-start | bytes 884744 | tf_op jit(solution)/shard_map/ppermute | solution.py:632
  131.5 18.7 %collective-permute-start.32 = (bf16[96,1536]{1,0:T(8,128)(2,1)S(1)}, bf16[96,1536]{1,0:T(8,128)(2,1)S(1)}, u32[]{:S(2)}, u32[]{:S(2)}) collective-permute-start(bf16[96,1536]{1,0:T(8,128)(2,1)S(1)} %fusion.10), channel_id=1, source_target_pairs={{0,16},{4,20},{8,24},{12,28},{16,0},{20,4},{24,8},{28,12},{1,17},{... | collective-permute-start | bytes 884744 | tf_op jit(solution)/shard_map/ppermute | solution.py:632
  134.9 16.3 %collective-permute-start.21 = (bf16[400,768]{1,0:T(8,128)(2,1)S(1)}, bf16[400,768]{1,0:T(8,128)(2,1)S(1)}, u32[]{:S(2)}, u32[]{:S(2)}) collective-permute-start(bf16[400,768]{1,0:T(8,128)(2,1)S(1)} %copy-done.36), channel_id=1, source_target_pairs={{0,4},{4,0},{8,12},{12,8},{16,20},{20,16},{24,28},{28,24},{1,5},{5... | collective-permute-start | bytes 1843208 | tf_op jit(solution)/shard_map/ppermute | solution.py:632
  135.5 15.7 %collective-permute-start.23 = (bf16[2,128,768]{2,1,0:T(8,128)(2,1)S(1)}, bf16[2,128,768]{2,1,0:T(8,128)(2,1)S(1)}, u32[]{:S(2)}, u32[]{:S(2)}) collective-permute-start(bf16[2,128,768]{2,1,0:T(8,128)(2,1)S(1)} %copy-done.39), channel_id=1, source_target_pairs={{0,1},{1,0},{2,3},{3,2},{4,5},{5,4},{6,7},{7,6},{8,9},{9,8},{10,11... | collective-permute-start | bytes 1179656 | tf_op jit(solution)/shard_map/ppermute | solution.py:629
  135.6 15.7 %collective-permute-start.24 = (bf16[2,128,768]{2,1,0:T(8,128)(2,1)S(1)}, bf16[2,128,768]{2,1,0:T(8,128)(2,1)S(1)}, u32[]{:S(2)}, u32[]{:S(2)}) collective-permute-start(bf16[2,128,768]{2,1,0:T(8,128)(2,1)S(1)} %copy-done.38), channel_id=1, source_target_pairs={{0,1},{1,0},{2,3},{3,2},{4,5},{5,4},{6,7},{7,6},{8,9},{9,8},{10,11... | collective-permute-start | bytes 1179656 | tf_op jit(solution)/shard_map/ppermute | solution.py:629
  144.2 21.7 %collective-permute-start.31 = (bf16[96,768]{1,0:T(8,128)(2,1)S(1)}, bf16[96,768]{1,0:T(8,128)(2,1)S(1)}, u32[]{:S(2)}, u32[]{:S(2)}) collective-permute-start(bf16[96,768]{1,0:T(8,128)(2,1)S(1)} %fusion.22), channel_id=1, source_target_pairs={{0,16},{4,20},{8,24},{12,28},{16,0},{20,4},{24,8},{28,12},{1,17},{... | collective-permute-start | bytes 442376 | tf_op jit(solution)/shard_map/ppermute | solution.py:632
  151.4 11.2 %collective-permute-start.25 = (bf16[112,768]{1,0:T(8,128)(2,1)S(1)}, bf16[112,768]{1,0:T(8,128)(2,1)S(1)}, u32[]{:S(2)}, u32[]{:S(2)}) collective-permute-start(bf16[112,768]{1,0:T(8,128)(2,1)S(1)} %get-tuple-element.195), channel_id=1, source_target_pairs={{0,16},{4,20},{8,24},{12,28},{16,0},{20,4},{24,8},{28,12},{1,17},{... | collective-permute-start | bytes 516104 | tf_op jit(solution)/shard_map/ppermute | solution.py:632
  151.5 11.3 %collective-permute-start.26 = (bf16[112,768]{1,0:T(8,128)(2,1)S(1)}, bf16[112,768]{1,0:T(8,128)(2,1)S(1)}, u32[]{:S(2)}, u32[]{:S(2)}) collective-permute-start(bf16[112,768]{1,0:T(8,128)(2,1)S(1)} %get-tuple-element.196), channel_id=1, source_target_pairs={{0,8},{4,12},{8,0},{12,4},{16,24},{20,28},{24,16},{28,20},{1,9},{5... | collective-permute-start | bytes 516104 | tf_op jit(solution)/shard_map/ppermute | solution.py:632
  (51 other events, 233.7 us)

commit v5 on v4

--- a/solution.py
+++ b/solution.py
@@ -218,7 +218,7 @@
     return lax.dot_general(a, b, (dims, ((), ())), precision=highest, preferred_element_type=f32)
 
 
-def bias_body(idx, to_ref, tp_ref, bucket_ref, segr_ref, enc_ref, bias_ref, cross_ref, *, Q):
+def bias_body(idx, to_ref, tp_ref, bucket_ref, segr_ref, enc_ref, near_ref, bias_ref, cross_ref, *, Q):
     core = idx[1]
     L = 4 * Q
     heads, buckets = to_ref.shape
@@ -235,12 +235,16 @@
         place = (2 * b + core) * Q + lax.broadcasted_iota(jnp.int32, (Q, L), 0)
         col = lax.broadcasted_iota(jnp.int32, (Q, L), 1)
         allowed = (segc == seg) & (col <= place)
+        out, m = (near_ref, 2 * Q) if b == 0 else (bias_ref, L)
+        first = lax.broadcasted_iota(jnp.int32, (heads, m), 1) == 0
         for grp in range(2):
-            turned = pltpu.roll(lines[grp], (2 * b + core) * Q, 1)
+            turned = lines[grp] if b else jnp.where(first, lines[grp][:, :m], lines[grp][:, m:])
+            turned = pltpu.roll(turned, core * Q + (2 * b * Q) % m, 1)
             for h in range(heads):
-                line = jnp.broadcast_to(turned[h : h + 1, :], (Q, L))
+                line = jnp.broadcast_to(turned[h : h + 1, :], (Q, m))
                 line = pltpu.roll(line, 0, 1, stride=1, stride_axis=0)
-                bias_ref[grp * heads + h, rows, :] = jnp.where(allowed, line, masked_score)
+                out[grp * heads + h] = jnp.where(allowed[:, :m], line, masked_score)
+        out.flush()
 
 
 def soft_mix(q_ref, k_ref, v_ref, extra, p_ref, o_ref, rows, nk):
@@ -262,7 +266,7 @@
         o_ref[rows, lanes] = mixed.astype(bf16)
 
 
-def self_forward(idx, x_ref, g_ref, w, bias_ref, part_ref, h_ref, q_ref, k_ref, v_ref, p_ref, o_ref, *, Q):
+def self_forward(idx, x_ref, g_ref, w, near_ref, bias_ref, part_ref, h_ref, q_ref, k_ref, v_ref, p_ref, o_ref, *, Q):
     core = idx[1]
     gain = g_ref[0:1, :]
     for t in range(4):
@@ -283,7 +287,7 @@
     for b in range(2):
         nk = 2 * Q * (b + 1)
         rows = pl.ds(b * Q, Q)
-        soft_mix(q_ref, k_ref, v_ref, lambda h: bias_ref[h, rows, pl.ds(0, nk)], p_ref, o_ref, rows, nk)
+        soft_mix(q_ref, k_ref, v_ref, (lambda h: bias_ref[h]) if b else (lambda h: near_ref[h]), p_ref, o_ref, rows, nk)
     p_ref.flush()
     o_ref.flush()
     part_ref[...] = dot(o_ref[...], w[3][...]).astype(bf16)
@@ -643,10 +647,10 @@
     w_self = jnp.concatenate([wq, self_key.T, self_value.T, self_out.T])
     w_self_p = over_mp(w_self, 1)
     bucket_line = offset_buckets.reshape(1, L)
-    bias, cross_mask = call(
+    near_bias, bias, cross_mask = call(
         bias_body,
         "bias",
-        [shape((2 * heads, 2 * Q, L), f32), shape((2 * Q, L), f32)],
+        [shape((2 * heads, Q, 2 * Q), f32), shape((2 * heads, Q, L), f32), shape((2 * Q, L), f32)],
         bias_table.T,
         table_p,
         bucket_line,
@@ -688,6 +692,7 @@
         x_rows(),
         norm_gains,
         self_w(0, 1, 2, 3),
+        near_bias,
         bias,
     )
     recv1 = over_mp(part1, 2)
@@ -906,10 +911,12 @@
         ffn_total = finish(ffn_pair, ffn_recv, ffn_last)
         cross_recv = over_dp(first_half(cross_pair), 2)
         cross_last = over_dp(second_half(cross_pair, cross_recv), 4)
+        small = small + over_mp(small, 1)
         small, across, cross_last = together(small, across, cross_last)
         cross_total = finish(cross_pair, cross_recv, cross_last)
     else:
         small = lax.psum(small, "dp")
+        small = small + over_mp(small, 1)
         ffn_total, cross_total, self_total = map(scatter, (ffn_parts, cross_parts, self_parts))
     grad_up, grad_down = ffn_total[:, :F], ffn_total[:, F:]
 
@@ -921,7 +928,6 @@
     grad_encoder = sum_rows(enc_keep, enc_recv, across[Q : 2 * Q]).astype(bf16)
     output = (out_keep + across[2 * Q :].astype(f32)).astype(bf16)
 
-    small = small + over_mp(small, 1)
     small = small + over_mp(small, 2)
     gain_total = small[:3]
     table_total = small[3, : 4 * heads * buckets].reshape(4 * heads, buckets).T

time: 177 us -> 173 us (0.977); the launches traced: 174 us -> 173 us
  waiting for transfers between devices: 49.4 us -> 47.6 us
  transfers between devices with their start and end apart: 35 -> 35, of which waited for: 17 -> 18; matrix products, arithmetic and copies ran while one was open for 3% -> 3% of each run, Pallas kernels for 35% -> 35%
where the time goes in v5:
time: 173 us
  Pallas kernels  74.2 us (43%)
  waiting for transfers between devices  47.6 us (28%)
  starting transfers between devices  33.9 us (20%)
  local copies, waits for them, and re-layouts  12.3 us (7%)
  other arithmetic  3.94 us (2%)
    pallas_call x12, Pallas kernels, kernel_call(): pl.pallas_call(whole, out_shape=outs, in_specs=[pl.BlockSpec(memory_space...  74.2 us
    ppermute x25, waiting for transfers between devices, over_mp(): return lax.ppermute(v, 'mp', [(i, i ^ flip) for i in range(4)])  24 us
    ppermute x10, waiting for transfers between devices, over_dp(): return lax.ppermute(v, 'dp', [(i, i ^ flip) for i in range(dp_size)])  23.6 us
    ppermute x25, starting transfers between devices, over_mp(): return lax.ppermute(v, 'mp', [(i, i ^ flip) for i in range(4)])  18.2 us
    ppermute x10, starting transfers between devices, over_dp(): return lax.ppermute(v, 'dp', [(i, i ^ flip) for i in range(dp_size)])  15.7 us
    unnamed x80, local copies, waits for them, and re-layouts  7.84 us
  transfers between devices with their start and end apart: 35, of which 18 were waited for; matrix products, arithmetic and copies ran while one was open for 3% of the time, Pallas kernels for 35%

profile of v5, /device:TPU:0, one launch (start us, length us, event | category | flops | bytes accessed | tf_op | source)
XLA Modules:
  0.0 173.1 jit_solution(3672054081329175807)
XLA Ops:
  4.1 2.7 %collective-permute-start.1 = (bf16[128,768]{1,0:T(8,128)(2,1)S(1)}, bf16[128,768]{1,0:T(8,128)(2,1)}, u32[]{:S(2)}, u32[]{:S(2)}) collective-permute-start(bf16[128,768]{1,0:T(8,128)(2,1)S(1)} %bitcast.63), channel_id=1, source_target_pairs={{0,2},{1,3},{2,0},{3,1},{4,6},{5,7},{6,4},{7,5},{8,10},{9,11},{10,... | collective-permute-start | bytes 589832 | tf_op jit(solution)/shard_map/ppermute | solution.py:633
  7.5 4.2 %bias.1 = (f32[6,128,256]{2,1,0:T(8,128)}, f32[6,128,512]{2,1,0:T(8,128)}, f32[256,512]{1,0:T(8,128)}) custom-call(f32[3,32]{1,0:T(4,128)} %bitcast.79, f32[3,32]{1,0:T(4,128)} %copy-done.35, s32[1,512]{1,0:T(1,128)} %bitcast.75, s32[1,512]{1,0:T(1,128)} %refs_3_.2, s32[1,512]{1,0:T(1,128)} %refs_4_.5), custom_call_target="tpu_custom_call" | custom-call | bytes 2890496 | tf_op jit(solution)/shard_map/bias/pallas_call | solution.py:186
  15.3 7.7 %self_forward.1 = (bf16[256,768]{1,0:T(8,128)(2,1)}, bf16[512,768]{1,0:T(8,128)(2,1)}, bf16[256,384]{1,0:T(8,128)(2,1)}, bf16[512,384]{1,0:T(8,128)(2,1)}, bf16[...) custom-call(bf16[128,768]{1,0:T(8,128)(2,1)} %bitcast.61, ...), custom_call_target="tpu_custom_call" | custom-call | bytes 9446400 | tf_op jit(solution)/shard_map/self_forward/pallas_call | solution.py:186
  27.5 3.5 %encoder_keys.1 = (bf16[512,384]{1,0:T(8,128)(2,1)}, bf16[512,384]{1,0:T(8,128)(2,1)}) custom-call(bf16[256,768]{1,0:T(8,128)(2,1)} %copy-done.2, bf16[256,768]{1,0:T(8,128)(2,1)} %copy-done.5, bf16[256,768]{1,0:T(8,128)(2,1)} %copy-done.6, bf16[256,768]{1,0:T(8,128)(2,1)} %copy-done.7, bf16[768,768]{1,0:T(8,128)(2,1)} %copy-done, bf16[768,768]{1,0:T(8,128)(2,1)} %copy-done.4), custom_call_target="tpu_custom_call" | custom-call | bytes 4718592 | tf_op jit(solution)/shard_map/encoder_keys/pallas_call | solution.py:186
  31.0 4.6 %collective-permute-done.8.refs_5_ = bf16[256,768]{1,0:T(8,128)(2,1)S(1)} collective-permute-done((bf16[256,768]{1,0:T(8,128)(2,1)}, bf16[256,768]{1,0:T(8,128)(2,1)S(1)}, u32[]{:S(2)}, u32[]{:S(2)}) %collective-permute-start.8) | collective-permute-done | bytes 393248 | tf_op jit(solution)/shard_map/ppermute | solution.py:633
  36.4 8.0 %cross_forward.1 = (bf16[256,768]{1,0:T(8,128)(2,1)}, f32[256,768]{1,0:T(8,128)}, bf16[256,768]{1,0:T(8,128)(2,1)}, bf16[256,384]{1,0:T(8,128)(2,1)}, bf16[6,256...) custom-call(bf16[128,768]{1,0:T(8,128)(2,1)} %bitcast.62, bf16[128,768]{1,0:T(8,128)(2,1)} %collective-permute-done.1.refs_1_, ...), custom_call_target="tpu_custom_call" | custom-call | bytes 8791040 | tf_op jit(solution)/shard_map/cross_forward/pallas_call | solution.py:186
  46.2 3.7 %act_grads.1.refs_6_ = bf16[2,256,768]{2,1,0:T(8,128)(2,1)} custom-call(bf16[256,768]{1,0:T(8,128)(2,1)} %copy-done.2, bf16[256,768]{1,0:T(8,128)(2,1)} %copy-done.5, bf16[256,768]{1,0:T(8,128)(2,1)} %copy-done.6, bf16[256,768]{1,0:T(8,128)(2,1)} %copy-done.7, bf16[768,768]{1,0:T(8,128)(2,1)} %refs_15_.1, ...), custom_call_target="tpu_custom_call" | custom-call | bytes 4718592 | tf_op jit(solution)/shard_map/act_grads/pallas_call | solution.py:186
  50.0 5.4 %collective-permute-done.10.refs_2_ = bf16[256,768]{1,0:T(8,128)(2,1)S(1)} collective-permute-done((bf16[256,768]{1,0:T(8,128)(2,1)}, bf16[256,768]{1,0:T(8,128)(2,1)S(1)}, u32[]{:S(2)}, u32[]{:S(2)}) %collective-permute-start.10) | collective-permute-done | bytes 393248 | tf_op jit(solution)/shard_map/ppermute | solution.py:633
  56.1 6.2 %ffn_both.1 = (bf16[256,768]{1,0:T(8,128)(2,1)}, f32[256,768]{1,0:T(8,128)}, bf16[256,768]{1,0:T(8,128)(2,1)}, bf16[256,768]{1,0:T(8,128)(2,1)}, bf16[3,256,768]{2,1,0:T(8,128)(2,1)}) custom-call(f32[256,768]{1,0:T(8,128)} %get-tuple-element.109.refs_0_.refs_3_, bf16[256,768]{1,0:T(8,128)(2,1)} %get-tuple-element.110.refs_1_, bf16[256,768]{1,0:T(8,128)(2,1)} %copy-done.26, ...), custom_call_target="tpu_custom_call" | custom-call | bytes 7873536 | tf_op jit(solution)/shard_map/ffn_both/pallas_call | solution.py:186
  66.5 5.6 %ffn_weights.1 = (bf16[4,96,1536]{2,1,0:T(8,128)(2,1)}, bf16[4,96,1536]{2,1,0:T(8,128)(2,1)}) custom-call(bf16[256,768]{1,0:T(8,128)(2,1)} %copy-done.2, bf16[256,768]{1,0:T(8,128)(2,1)} %copy-done.5, bf16[256,768]{1,0:T(8,128)(2,1)} %copy-done.6, bf16[256,768]{1,0:T(8,128)(2,1)} %copy-done.7, bf16[256,768]{1,0:T(8,128)(2,1)} %get-tuple-element.114.refs_4_.refs_13_, ...), custom_call_target="tpu_custom_call" | custom-call | bytes 9437184 | tf_op jit(solution)/shard_map/ffn_weights/pallas_call | solution.py:186
  72.1 2.0 %collective-permute-done.13.refs_5_ = bf16[256,768]{1,0:T(8,128)(2,1)S(1)} collective-permute-done((bf16[256,768]{1,0:T(8,128)(2,1)}, bf16[256,768]{1,0:T(8,128)(2,1)S(1)}, u32[]{:S(2)}, u32[]{:S(2)}) %collective-permute-start.13) | collective-permute-done | bytes 393248 | tf_op jit(solution)/shard_map/ppermute | solution.py:633
  74.9 7.7 %cross_back.1 = (bf16[256,768]{1,0:T(8,128)(2,1)}, f32[256,768]{1,0:T(8,128)}, bf16[2,256,768]{2,1,0:T(8,128)(2,1)}, bf16[256,384]{1,0:T(8,128)(2,1)}, bf16[6,25...) custom-call(bf16[256,768]{1,0:T(8,128)(2,1)} %copy-done.2, bf16[256,768]{1,0:T(8,128)(2,1)} %copy-done.5, ...), custom_call_target="tpu_custom_call" | custom-call | bytes 12223488 | tf_op jit(solution)/shard_map/cross_back/pallas_call | solution.py:186
  85.9 4.5 %cross_keys.1 = (f32[512,192]{1,0:T(8,128)}, f32[512,192]{1,0:T(8,128)}, bf16[768,384]{1,0:T(8,128)(2,1)}) custom-call(bf16[6,256,512]{2,1,0:T(8,128)(2,1)} %get-tuple-element.125.refs_0_, bf16[6,256,512]{2,1,0:T(8,128)(2,1)} %get-tuple-element.120.refs_12_.refs_1_, bf16[256,384]{1,0:T(8,128)(2,1)} %get-tuple-element.126.refs_2_, ...), custom_call_target="tpu_custom_call" | custom-call | bytes 5308416 | tf_op jit(solution)/shard_map/cross_keys/pallas_call | solution.py:186
  90.4 4.6 %collective-permute-done.16.refs_2_ = bf16[256,768]{1,0:T(8,128)(2,1)S(1)} collective-permute-done((bf16[256,768]{1,0:T(8,128)(2,1)}, bf16[256,768]{1,0:T(8,128)(2,1)S(1)}, u32[]{:S(2)}, u32[]{:S(2)}) %collective-permute-start.16) | collective-permute-done | bytes 393248 | tf_op jit(solution)/shard_map/ppermute | solution.py:633
  95.8 7.2 %self_back.1 = (f32[128,768]{1,0:T(8,128)}, bf16[256,768]{1,0:T(8,128)(2,1)}, bf16[256,384]{1,0:T(8,128)(2,1)}, f32[512,192]{1,0:T(8,128)}, f32[512,192]{1,0:T(8...) custom-call(f32[256,768]{1,0:T(8,128)} %get-tuple-element.135.refs_0_, ...), custom_call_target="tpu_custom_call" | custom-call | bytes 11461632 | tf_op jit(solution)/shard_map/self_back/pallas_call | solution.py:186
  106.0 8.0 %cross_weights.1 = (bf16[4,96,768]{2,1,0:T(8,128)(2,1)}, bf16[4,96,768]{2,1,0:T(8,128)(2,1)}, f32[2,128,768]{2,1,0:T(8,128)}, bf16[2,128,768]{2,1,0:T(8,128)(2,1...) custom-call(bf16[2,256,768]{2,1,0:T(8,128)(2,1)} %get-tuple-element.122.refs_0_, bf16[2,256,768]{2,1,0:T(8,128)(2,1)} %copy-done.14, ...), custom_call_target="tpu_custom_call" | custom-call | bytes 14942208 | tf_op jit(solution)/shard_map/cross_weights/pallas_call | solution.py:186
  117.3 7.8 %self_weights.1 = (bf16[4,96,768]{2,1,0:T(8,128)(2,1)}, bf16[400,768]{1,0:T(8,128)(2,1)}, f32[2,128,768]{2,1,0:T(8,128)}, bf16[2,128,768]{2,1,0:T(8,128)(2,1)}, f32[8,768]{1,0:T(8,128)}) custom-call(bf16[512,768]{1,0:T(8,128)(2,1)} %get-tuple-element.146.refs_0_, bf16[256,768]{1,0:T(8,128)(2,1)} %get-tuple-element.147.refs_1_, bf16[256,768]{1,0:T(8,128)(2,1)} %copy-done.24, ...), custom_call_target="tpu_custom_call" | custom-call | bytes 8539136 | tf_op jit(solution)/shard_map/self_weights/pallas_call | solution.py:186
  125.2 4.5 %collective-permute-done.30 = bf16[4,96,768]{2,1,0:T(8,128)(2,1)S(1)} collective-permute-done((bf16[4,96,768]{2,1,0:T(8,128)(2,1)}, bf16[4,96,768]{2,1,0:T(8,128)(2,1)S(1)}, u32[]{:S(2)}, u32[]{:S(2)}) %collective-permute-start.30) | collective-permute-done | bytes 589856 | tf_op jit(solution)/shard_map/ppermute | solution.py:636
  131.5 2.6 %collective-permute-start.33 = (bf16[96,1536]{1,0:T(8,128)(2,1)S(1)}, bf16[96,1536]{1,0:T(8,128)(2,1)S(1)}, u32[]{:S(2)}, u32[]{:S(2)}) collective-permute-start(bf16[96,1536]{1,0:T(8,128)(2,1)S(1)} %fusion.10), channel_id=1, source_target_pairs={{0,16},{4,20},{8,24},{12,28},{16,0},{20,4},{24,8},{28,12},{1,17},{... | collective-permute-start | bytes 884744 | tf_op jit(solution)/shard_map/ppermute | solution.py:636
  136.0 8.1 %collective-permute-done.31 = bf16[2,96,768]{2,1,0:T(8,128)(2,1)S(1)} collective-permute-done((bf16[2,96,768]{2,1,0:T(8,128)(2,1)S(1)}, bf16[2,96,768]{2,1,0:T(8,128)(2,1)S(1)}, u32[]{:S(2)}, u32[]{:S(2)}) %collective-permute-start.31) | collective-permute-done | bytes 294944 | tf_op jit(solution)/shard_map/ppermute | solution.py:636
  144.8 5.4 %collective-permute-done.33 = bf16[96,1536]{1,0:T(8,128)(2,1)S(1)} collective-permute-done((bf16[96,1536]{1,0:T(8,128)(2,1)S(1)}, bf16[96,1536]{1,0:T(8,128)(2,1)S(1)}, u32[]{:S(2)}, u32[]{:S(2)}) %collective-permute-start.33) | collective-permute-done | bytes 294944 | tf_op jit(solution)/shard_map/ppermute | solution.py:636
  151.5 6.1 %collective-permute-start.26 = (bf16[112,768]{1,0:T(8,128)(2,1)S(1)}, bf16[112,768]{1,0:T(8,128)(2,1)S(1)}, u32[]{:S(2)}, u32[]{:S(2)}) collective-permute-start(bf16[112,768]{1,0:T(8,128)(2,1)S(1)} %get-tuple-element.198), channel_id=1, source_target_pairs={{0,8},{4,12},{8,0},{12,4},{16,24},{20,28},{24,16},{28,20},{1,9},{5... | collective-permute-start | bytes 516104 | tf_op jit(solution)/shard_map/ppermute | solution.py:636
  159.3 3.3 %collective-permute-done.25 = bf16[112,768]{1,0:T(8,128)(2,1)S(1)} collective-permute-done((bf16[112,768]{1,0:T(8,128)(2,1)S(1)}, bf16[112,768]{1,0:T(8,128)(2,1)S(1)}, u32[]{:S(2)}, u32[]{:S(2)}) %collective-permute-start.25) | collective-permute-done | bytes 172064 | tf_op jit(solution)/shard_map/ppermute | solution.py:636
  162.8 2.1 %collective-permute-done.27 = bf16[112,768]{1,0:T(8,128)(2,1)S(1)} collective-permute-done((bf16[112,768]{1,0:T(8,128)(2,1)S(1)}, bf16[112,768]{1,0:T(8,128)(2,1)S(1)}, u32[]{:S(2)}, u32[]{:S(2)}) %collective-permute-start.27) | collective-permute-done | bytes 172064 | tf_op jit(solution)/shard_map/ppermute | solution.py:636
  (169 shorter events, 46.2 us)
Async XLA Ops:
  3.7 11.1 %collective-permute-start.5 = (bf16[768,768]{1,0:T(8,128)(2,1)S(1)}, bf16[768,768]{1,0:T(8,128)(2,1)}, u32[]{:S(2)}, u32[]{:S(2)}) collective-permute-start(bf16[768,768]{1,0:T(8,128)(2,1)S(1)} %pad_maximum_fusion.refs_5_.refs_8_), channel_id=1, source_target_pairs={{0,1},{1,0},{2,3},{3,2},{4,5},{5,4},{6,7},{7,6},{8,9},{9,8},{10,11... | collective-permute-start | bytes 3538952 | tf_op jit(solution)/shard_map/ppermute | solution.py:633
  6.9 18.8 %collective-permute-start.9 = (bf16[768,768]{1,0:T(8,128)(2,1)S(1)}, bf16[768,768]{1,0:T(8,128)(2,1)S(1)}, u32[]{:S(2)}, u32[]{:S(2)}) collective-permute-start(bf16[768,768]{1,0:T(8,128)(2,1)S(1)} %pad_maximum_fusion.1.refs_4_.refs_7_.refs_8_.refs_11_.refs_12_), channel_id=1, source_target_pairs={{0,1},{1,0},{2,3},{3,2},{4,5},{5,4},{6,7},{7,6},{8,9},{9,8},{10,11... | collective-permute-start | bytes 3538952 | tf_op jit(solution)/shard_map/ppermute | solution.py:633
  12.3 11.6 %collective-permute-start = (bf16[256,768]{1,0:T(8,128)(2,1)S(1)}, bf16[256,768]{1,0:T(8,128)(2,1)S(1)}, u32[]{:S(2)}, u32[]{:S(2)}) collective-permute-start(bf16[256,768]{1,0:T(8,128)(2,1)S(1)} %pad_maximum_fusion.3.refs_0_.refs_2_), channel_id=1, source_target_pairs={{0,2},{1,3},{2,0},{3,1},{4,6},{5,7},{6,4},{7,5},{8,10},{9,11},{10,... | collective-permute-start | bytes 1179656 | tf_op jit(solution)/shard_map/ppermute | solution.py:633
  14.4 31.9 %collective-permute-start.12 = (bf16[768,768]{1,0:T(8,128)(2,1)S(1)}, bf16[768,768]{1,0:T(8,128)(2,1)}, u32[]{:S(2)}, u32[]{:S(2)}) collective-permute-start(bf16[768,768]{1,0:T(8,128)(2,1)S(1)} %copy-done.10), channel_id=1, source_target_pairs={{0,1},{1,0},{2,3},{3,2},{4,5},{5,4},{6,7},{7,6},{8,9},{9,8},{10,11... | collective-permute-start | bytes 3538952 | tf_op jit(solution)/shard_map/ppermute | solution.py:633
  15.0 34.9 %collective-permute-start.11 = (bf16[768,768]{1,0:T(8,128)(2,1)}, bf16[768,768]{1,0:T(8,128)(2,1)}, u32[]{:S(2)}, u32[]{:S(2)}) collective-permute-start(bf16[768,768]{1,0:T(8,128)(2,1)} %refs_4_.8), channel_id=1, source_target_pairs={{0,1},{1,0},{2,3},{3,2},{4,5},{5,4},{6,7},{7,6},{8,9},{9,8},{10,11... | collective-permute-start | bytes 3538952 | tf_op jit(solution)/shard_map/ppermute | solution.py:633
  23.9 11.7 %collective-permute-start.8 = (bf16[256,768]{1,0:T(8,128)(2,1)}, bf16[256,768]{1,0:T(8,128)(2,1)S(1)}, u32[]{:S(2)}, u32[]{:S(2)}) collective-permute-start(bf16[256,768]{1,0:T(8,128)(2,1)} %get-tuple-element.105.refs_4_), channel_id=1, source_target_pairs={{0,2},{1,3},{2,0},{3,1},{4,6},{5,7},{6,4},{7,5},{8,10},{9,11},{10,... | collective-permute-start | bytes 1179656 | tf_op jit(solution)/shard_map/ppermute | solution.py:633
  44.4 11.0 %collective-permute-start.10 = (bf16[256,768]{1,0:T(8,128)(2,1)}, bf16[256,768]{1,0:T(8,128)(2,1)S(1)}, u32[]{:S(2)}, u32[]{:S(2)}) collective-permute-start(bf16[256,768]{1,0:T(8,128)(2,1)} %get-tuple-element.110.refs_1_), channel_id=1, source_target_pairs={{0,2},{1,3},{2,0},{3,1},{4,6},{5,7},{6,4},{7,5},{8,10},{9,11},{10,... | collective-permute-start | bytes 1179656 | tf_op jit(solution)/shard_map/ppermute | solution.py:633
  62.4 11.7 %collective-permute-start.13 = (bf16[256,768]{1,0:T(8,128)(2,1)}, bf16[256,768]{1,0:T(8,128)(2,1)S(1)}, u32[]{:S(2)}, u32[]{:S(2)}) collective-permute-start(bf16[256,768]{1,0:T(8,128)(2,1)} %get-tuple-element.113.refs_4_), channel_id=1, source_target_pairs={{0,2},{1,3},{2,0},{3,1},{4,6},{5,7},{6,4},{7,5},{8,10},{9,11},{10,... | collective-permute-start | bytes 1179656 | tf_op jit(solution)/shard_map/ppermute | solution.py:633
  82.6 31.8 %collective-permute-start.20 = (bf16[4,96,1536]{2,1,0:T(8,128)(2,1)}, bf16[4,96,1536]{2,1,0:T(8,128)(2,1)S(1)}, u32[]{:S(2)}, u32[]{:S(2)}) collective-permute-start(bf16[4,96,1536]{2,1,0:T(8,128)(2,1)} %get-tuple-element.154), channel_id=1, source_target_pairs={{0,4},{4,0},{8,12},{12,8},{16,20},{20,16},{24,28},{28,24},{1,5},{5... | collective-permute-start | bytes 3538952 | tf_op jit(solution)/shard_map/ppermute | solution.py:636
  84.4 10.6 %collective-permute-start.16 = (bf16[256,768]{1,0:T(8,128)(2,1)}, bf16[256,768]{1,0:T(8,128)(2,1)S(1)}, u32[]{:S(2)}, u32[]{:S(2)}) collective-permute-start(bf16[256,768]{1,0:T(8,128)(2,1)} %get-tuple-element.124.refs_1_), channel_id=1, source_target_pairs={{0,2},{1,3},{2,0},{3,1},{4,6},{5,7},{6,4},{7,5},{8,10},{9,11},{10,... | collective-permute-start | bytes 1179656 | tf_op jit(solution)/shard_map/ppermute | solution.py:633
  85.9 17.7 %collective-permute-start.15 = (bf16[2,256,768]{2,1,0:T(8,128)(2,1)}, bf16[2,256,768]{2,1,0:T(8,128)(2,1)S(1)}, u32[]{:S(2)}, u32[]{:S(2)}) collective-permute-start(bf16[2,256,768]{2,1,0:T(8,128)(2,1)} %get-tuple-element.122.refs_0_), channel_id=1, source_target_pairs={{0,1},{1,0},{2,3},{3,2},{4,5},{5,4},{6,7},{7,6},{8,9},{9,8},{10,11... | collective-permute-start | bytes 2359304 | tf_op jit(solution)/shard_map/ppermute | solution.py:633
  103.1 11.5 %collective-permute-start.19 = (bf16[768,384]{1,0:T(8,128)(2,1)}, bf16[768,384]{1,0:T(8,128)(2,1)S(1)}, u32[]{:S(2)}, u32[]{:S(2)}) collective-permute-start(bf16[768,384]{1,0:T(8,128)(2,1)} %get-tuple-element.151), channel_id=1, source_target_pairs={{0,1},{1,0},{2,3},{3,2},{4,5},{5,4},{6,7},{7,6},{8,9},{9,8},{10,11... | collective-permute-start | bytes 1769480 | tf_op jit(solution)/shard_map/ppermute | solution.py:633
  103.6 13.0 %collective-permute-start.18 = (bf16[256,768]{1,0:T(8,128)(2,1)}, bf16[256,768]{1,0:T(8,128)(2,1)S(1)}, u32[]{:S(2)}, u32[]{:S(2)}) collective-permute-start(bf16[256,768]{1,0:T(8,128)(2,1)} %get-tuple-element.147.refs_1_), channel_id=1, source_target_pairs={{0,1},{1,0},{2,3},{3,2},{4,5},{5,4},{6,7},{7,6},{8,9},{9,8},{10,11... | collective-permute-start | bytes 1179656 | tf_op jit(solution)/shard_map/ppermute | solution.py:633
  114.0 15.7 %collective-permute-start.30 = (bf16[4,96,768]{2,1,0:T(8,128)(2,1)}, bf16[4,96,768]{2,1,0:T(8,128)(2,1)S(1)}, u32[]{:S(2)}, u32[]{:S(2)}) collective-permute-start(bf16[4,96,768]{2,1,0:T(8,128)(2,1)} %get-tuple-element.171), channel_id=1, source_target_pairs={{0,4},{4,0},{8,12},{12,8},{16,20},{20,16},{24,28},{28,24},{1,5},{5... | collective-permute-start | bytes 1769480 | tf_op jit(solution)/shard_map/ppermute | solution.py:636
  114.6 16.8 %collective-permute-start.22 = (bf16[2,96,1536]{2,1,0:T(8,128)(2,1)S(1)}, bf16[2,96,1536]{2,1,0:T(8,128)(2,1)S(1)}, u32[]{:S(2)}, u32[]{:S(2)}) collective-permute-start(bf16[2,96,1536]{2,1,0:T(8,128)(2,1)S(1)} %add_convert_fusion), channel_id=1, source_target_pairs={{0,8},{4,12},{8,0},{12,4},{16,24},{20,28},{24,16},{28,20},{1,9},{5... | collective-permute-start | bytes 1769480 | tf_op jit(solution)/shard_map/ppermute | solution.py:636
  129.7 14.3 %collective-permute-start.31 = (bf16[2,96,768]{2,1,0:T(8,128)(2,1)S(1)}, bf16[2,96,768]{2,1,0:T(8,128)(2,1)S(1)}, u32[]{:S(2)}, u32[]{:S(2)}) collective-permute-start(bf16[2,96,768]{2,1,0:T(8,128)(2,1)S(1)} %add_convert_fusion.2), channel_id=1, source_target_pairs={{0,8},{4,12},{8,0},{12,4},{16,24},{20,28},{24,16},{28,20},{1,9},{5... | collective-permute-start | bytes 884744 | tf_op jit(solution)/shard_map/ppermute | solution.py:636
  131.5 18.7 %collective-permute-start.33 = (bf16[96,1536]{1,0:T(8,128)(2,1)S(1)}, bf16[96,1536]{1,0:T(8,128)(2,1)S(1)}, u32[]{:S(2)}, u32[]{:S(2)}) collective-permute-start(bf16[96,1536]{1,0:T(8,128)(2,1)S(1)} %fusion.10), channel_id=1, source_target_pairs={{0,16},{4,20},{8,24},{12,28},{16,0},{20,4},{24,8},{28,12},{1,17},{... | collective-permute-start | bytes 884744 | tf_op jit(solution)/shard_map/ppermute | solution.py:636
  134.9 16.3 %collective-permute-start.21 = (bf16[400,768]{1,0:T(8,128)(2,1)S(1)}, bf16[400,768]{1,0:T(8,128)(2,1)S(1)}, u32[]{:S(2)}, u32[]{:S(2)}) collective-permute-start(bf16[400,768]{1,0:T(8,128)(2,1)S(1)} %copy-done.36), channel_id=1, source_target_pairs={{0,4},{4,0},{8,12},{12,8},{16,20},{20,16},{24,28},{28,24},{1,5},{5... | collective-permute-start | bytes 1843208 | tf_op jit(solution)/shard_map/ppermute | solution.py:636
  135.5 15.7 %collective-permute-start.23 = (bf16[2,128,768]{2,1,0:T(8,128)(2,1)S(1)}, bf16[2,128,768]{2,1,0:T(8,128)(2,1)S(1)}, u32[]{:S(2)}, u32[]{:S(2)}) collective-permute-start(bf16[2,128,768]{2,1,0:T(8,128)(2,1)S(1)} %copy-done.39), channel_id=1, source_target_pairs={{0,1},{1,0},{2,3},{3,2},{4,5},{5,4},{6,7},{7,6},{8,9},{9,8},{10,11... | collective-permute-start | bytes 1179656 | tf_op jit(solution)/shard_map/ppermute | solution.py:633
  135.5 15.7 %collective-permute-start.24 = (bf16[2,128,768]{2,1,0:T(8,128)(2,1)S(1)}, bf16[2,128,768]{2,1,0:T(8,128)(2,1)S(1)}, u32[]{:S(2)}, u32[]{:S(2)}) collective-permute-start(bf16[2,128,768]{2,1,0:T(8,128)(2,1)S(1)} %copy-done.38), channel_id=1, source_target_pairs={{0,1},{1,0},{2,3},{3,2},{4,5},{5,4},{6,7},{7,6},{8,9},{9,8},{10,11... | collective-permute-start | bytes 1179656 | tf_op jit(solution)/shard_map/ppermute | solution.py:633
  144.2 22.0 %collective-permute-start.32 = (bf16[96,768]{1,0:T(8,128)(2,1)S(1)}, bf16[96,768]{1,0:T(8,128)(2,1)S(1)}, u32[]{:S(2)}, u32[]{:S(2)}) collective-permute-start(bf16[96,768]{1,0:T(8,128)(2,1)S(1)} %fusion.22), channel_id=1, source_target_pairs={{0,16},{4,20},{8,24},{12,28},{16,0},{20,4},{24,8},{28,12},{1,17},{... | collective-permute-start | bytes 442376 | tf_op jit(solution)/shard_map/ppermute | solution.py:636
  151.4 11.2 %collective-permute-start.25 = (bf16[112,768]{1,0:T(8,128)(2,1)S(1)}, bf16[112,768]{1,0:T(8,128)(2,1)S(1)}, u32[]{:S(2)}, u32[]{:S(2)}) collective-permute-start(bf16[112,768]{1,0:T(8,128)(2,1)S(1)} %get-tuple-element.197), channel_id=1, source_target_pairs={{0,16},{4,20},{8,24},{12,28},{16,0},{20,4},{24,8},{28,12},{1,17},{... | collective-permute-start | bytes 516104 | tf_op jit(solution)/shard_map/ppermute | solution.py:636
  151.5 11.3 %collective-permute-start.26 = (bf16[112,768]{1,0:T(8,128)(2,1)S(1)}, bf16[112,768]{1,0:T(8,128)(2,1)S(1)}, u32[]{:S(2)}, u32[]{:S(2)}) collective-permute-start(bf16[112,768]{1,0:T(8,128)(2,1)S(1)} %get-tuple-element.198), channel_id=1, source_target_pairs={{0,8},{4,12},{8,0},{12,4},{16,24},{20,28},{24,16},{28,20},{1,9},{5... | collective-permute-start | bytes 516104 | tf_op jit(solution)/shard_map/ppermute | solution.py:636
  157.7 9.9 %collective-permute-start.29 = (bf16[384,768]{1,0:T(8,128)(2,1)S(1)}, bf16[384,768]{1,0:T(8,128)(2,1)S(1)}, u32[]{:S(2)}, u32[]{:S(2)}) collective-permute-start(bf16[384,768]{1,0:T(8,128)(2,1)S(1)} %pad_maximum_fusion.2), channel_id=1, source_target_pairs={{0,2},{1,3},{2,0},{3,1},{4,6},{5,7},{6,4},{7,5},{8,10},{9,11},{10,... | collective-permute-start | bytes 1769480 | tf_op jit(solution)/shard_map/ppermute | solution.py:633
  (51 other events, 236.3 us)

commit v6 on v5

--- a/solution.py
+++ b/solution.py
@@ -192,7 +192,7 @@
         + [pltpu.VMEM(o.shape, o.dtype) for o in outs]
         + [pltpu.SemaphoreType.DMA((n_copies,)), pltpu.SemaphoreType.DMA((len(outs),))]
         + list(scratch),
-        compiler_params=pltpu.CompilerParams(vmem_limit_bytes=58 * 1024 * 1024),
+        compiler_params=pltpu.CompilerParams(vmem_limit_bytes=54 * 1024 * 1024),
         cost_estimate=pl.CostEstimate(flops=flops, bytes_accessed=moved, transcendentals=0),
         name=name,
     )(*arrays)

time: 173 us -> 173 us (level)
  waiting for transfers between devices: 47.6 us -> 45.8 us
    ppermute x25, waiting for transfers between devices: 24 us -> 22.2 us  [over_mp(): return lax.ppermute(v, 'mp', [(i, i ^ flip) for i in range(4)])]
    unnamed x80 -> x92, local copies, waits for them, and re-layouts: 7.84 us -> 9.35 us
where the time goes in v6:
time: 173 us
  Pallas kernels  74.4 us (43%)
  waiting for transfers between devices  45.8 us (26%)
  starting transfers between devices  33.8 us (20%)
  local copies, waits for them, and re-layouts  13.8 us (8%)
  other arithmetic  3.96 us (2%)
    pallas_call x12, Pallas kernels, kernel_call(): pl.pallas_call(whole, out_shape=outs, in_specs=[pl.BlockSpec(memory_space...  74.4 us
    ppermute x10, waiting for transfers between devices, over_dp(): return lax.ppermute(v, 'dp', [(i, i ^ flip) for i in range(dp_size)])  23.6 us
    ppermute x25, waiting for transfers between devices, over_mp(): return lax.ppermute(v, 'mp', [(i, i ^ flip) for i in range(4)])  22.2 us
    ppermute x25, starting transfers between devices, over_mp(): return lax.ppermute(v, 'mp', [(i, i ^ flip) for i in range(4)])  18.2 us
    ppermute x10, starting transfers between devices, over_dp(): return lax.ppermute(v, 'dp', [(i, i ^ flip) for i in range(dp_size)])  15.7 us
    unnamed x92, local copies, waits for them, and re-layouts  9.35 us
  transfers between devices with their start and end apart: 35, of which 18 were waited for; matrix products, arithmetic and copies ran while one was open for 3% of the time, Pallas kernels for 35%

profile of v6, /device:TPU:0, one launch (start us, length us, event | category | flops | bytes accessed | tf_op | source)
XLA Modules:
  0.0 173.1 jit_solution(14647972589021602129)
XLA Ops:
  4.1 2.7 %collective-permute-start.1 = (bf16[128,768]{1,0:T(8,128)(2,1)S(1)}, bf16[128,768]{1,0:T(8,128)(2,1)S(1)}, u32[]{:S(2)}, u32[]{:S(2)}) collective-permute-start(bf16[128,768]{1,0:T(8,128)(2,1)S(1)} %bitcast.63), channel_id=1, source_target_pairs={{0,2},{1,3},{2,0},{3,1},{4,6},{5,7},{6,4},{7,5},{8,10},{9,11},{10,... | collective-permute-start | bytes 589832 | tf_op jit(solution)/shard_map/ppermute | solution.py:633
  7.5 4.4 %bias.1 = (f32[6,128,256]{2,1,0:T(8,128)}, f32[6,128,512]{2,1,0:T(8,128)}, f32[256,512]{1,0:T(8,128)}) custom-call(f32[3,32]{1,0:T(4,128)} %bitcast.79, f32[3,32]{1,0:T(4,128)} %copy-done.40, s32[1,512]{1,0:T(1,128)} %bitcast.75, s32[1,512]{1,0:T(1,128)} %refs_3_.2, s32[1,512]{1,0:T(1,128)} %refs_4_.5), custom_call_target="tpu_custom_call" | custom-call | bytes 2890496 | tf_op jit(solution)/shard_map/bias/pallas_call | solution.py:186
  15.8 7.7 %self_forward.1 = (bf16[256,768]{1,0:T(8,128)(2,1)}, bf16[512,768]{1,0:T(8,128)(2,1)}, bf16[256,384]{1,0:T(8,128)(2,1)}, bf16[512,384]{1,0:T(8,128)(2,1)}, bf16[...) custom-call(bf16[128,768]{1,0:T(8,128)(2,1)} %bitcast.61, ...), custom_call_target="tpu_custom_call" | custom-call | bytes 9446400 | tf_op jit(solution)/shard_map/self_forward/pallas_call | solution.py:186
  27.4 3.5 %encoder_keys.1 = (bf16[512,384]{1,0:T(8,128)(2,1)}, bf16[512,384]{1,0:T(8,128)(2,1)}) custom-call(bf16[256,768]{1,0:T(8,128)(2,1)} %copy-done.2, bf16[256,768]{1,0:T(8,128)(2,1)} %copy-done.5, bf16[256,768]{1,0:T(8,128)(2,1)} %copy-done.6, bf16[256,768]{1,0:T(8,128)(2,1)} %copy-done.7, bf16[768,768]{1,0:T(8,128)(2,1)} %copy-done, bf16[768,768]{1,0:T(8,128)(2,1)} %copy-done.4), custom_call_target="tpu_custom_call" | custom-call | bytes 4718592 | tf_op jit(solution)/shard_map/encoder_keys/pallas_call | solution.py:186
  30.9 4.7 %collective-permute-done.8.refs_5_ = bf16[256,768]{1,0:T(8,128)(2,1)S(1)} collective-permute-done((bf16[256,768]{1,0:T(8,128)(2,1)}, bf16[256,768]{1,0:T(8,128)(2,1)S(1)}, u32[]{:S(2)}, u32[]{:S(2)}) %collective-permute-start.8) | collective-permute-done | bytes 393248 | tf_op jit(solution)/shard_map/ppermute | solution.py:633
  36.4 8.0 %cross_forward.1 = (bf16[256,768]{1,0:T(8,128)(2,1)}, f32[256,768]{1,0:T(8,128)}, bf16[256,768]{1,0:T(8,128)(2,1)}, bf16[256,384]{1,0:T(8,128)(2,1)}, bf16[6,256...) custom-call(bf16[128,768]{1,0:T(8,128)(2,1)} %bitcast.62, bf16[128,768]{1,0:T(8,128)(2,1)} %copy-done.16, ...), custom_call_target="tpu_custom_call" | custom-call | bytes 8791040 | tf_op jit(solution)/shard_map/cross_forward/pallas_call | solution.py:186
  47.2 3.7 %act_grads.1.refs_6_ = bf16[2,256,768]{2,1,0:T(8,128)(2,1)} custom-call(bf16[256,768]{1,0:T(8,128)(2,1)} %copy-done.2, bf16[256,768]{1,0:T(8,128)(2,1)} %copy-done.5, bf16[256,768]{1,0:T(8,128)(2,1)} %copy-done.6, bf16[256,768]{1,0:T(8,128)(2,1)} %copy-done.7, bf16[768,768]{1,0:T(8,128)(2,1)} %refs_15_.1, bf16[768,768]{1,0:T(8,128)(2,1)} %copy-done.11), custom_call_target="tpu_custom_call" | custom-call | bytes 4718592 | tf_op jit(solution)/shard_map/act_grads/pallas_call | solution.py:186
  51.0 4.4 %collective-permute-done.10.refs_2_ = bf16[256,768]{1,0:T(8,128)(2,1)S(1)} collective-permute-done((bf16[256,768]{1,0:T(8,128)(2,1)}, bf16[256,768]{1,0:T(8,128)(2,1)S(1)}, u32[]{:S(2)}, u32[]{:S(2)}) %collective-permute-start.10) | collective-permute-done | bytes 393248 | tf_op jit(solution)/shard_map/ppermute | solution.py:633
  56.1 6.2 %ffn_both.1 = (bf16[256,768]{1,0:T(8,128)(2,1)}, f32[256,768]{1,0:T(8,128)}, bf16[256,768]{1,0:T(8,128)(2,1)}, bf16[256,768]{1,0:T(8,128)(2,1)}, bf16[3,256,768]{2,1,0:T(8,128)(2,1)}) custom-call(f32[256,768]{1,0:T(8,128)} %get-tuple-element.109.refs_0_.refs_3_, bf16[256,768]{1,0:T(8,128)(2,1)} %get-tuple-element.110.refs_1_, bf16[256,768]{1,0:T(8,128)(2,1)} %copy-done.31, ...), custom_call_target="tpu_custom_call" | custom-call | bytes 7873536 | tf_op jit(solution)/shard_map/ffn_both/pallas_call | solution.py:186
  66.5 5.6 %ffn_weights.1 = (bf16[4,96,1536]{2,1,0:T(8,128)(2,1)}, bf16[4,96,1536]{2,1,0:T(8,128)(2,1)}) custom-call(bf16[256,768]{1,0:T(8,128)(2,1)} %copy-done.2, bf16[256,768]{1,0:T(8,128)(2,1)} %copy-done.5, bf16[256,768]{1,0:T(8,128)(2,1)} %copy-done.6, bf16[256,768]{1,0:T(8,128)(2,1)} %copy-done.7, bf16[256,768]{1,0:T(8,128)(2,1)} %get-tuple-element.114.refs_4_.refs_13_, ...), custom_call_target="tpu_custom_call" | custom-call | bytes 9437184 | tf_op jit(solution)/shard_map/ffn_weights/pallas_call | solution.py:186
  72.1 2.0 %collective-permute-done.13.refs_5_ = bf16[256,768]{1,0:T(8,128)(2,1)S(1)} collective-permute-done((bf16[256,768]{1,0:T(8,128)(2,1)}, bf16[256,768]{1,0:T(8,128)(2,1)S(1)}, u32[]{:S(2)}, u32[]{:S(2)}) %collective-permute-start.13) | collective-permute-done | bytes 393248 | tf_op jit(solution)/shard_map/ppermute | solution.py:633
  74.9 7.8 %cross_back.1 = (bf16[256,768]{1,0:T(8,128)(2,1)}, f32[256,768]{1,0:T(8,128)}, bf16[2,256,768]{2,1,0:T(8,128)(2,1)}, bf16[256,384]{1,0:T(8,128)(2,1)}, bf16[6,25...) custom-call(bf16[256,768]{1,0:T(8,128)(2,1)} %copy-done.2, bf16[256,768]{1,0:T(8,128)(2,1)} %copy-done.5, ...), custom_call_target="tpu_custom_call" | custom-call | bytes 12223488 | tf_op jit(solution)/shard_map/cross_back/pallas_call | solution.py:186
  86.0 4.5 %cross_keys.1 = (f32[512,192]{1,0:T(8,128)}, f32[512,192]{1,0:T(8,128)}, bf16[768,384]{1,0:T(8,128)(2,1)}) custom-call(bf16[6,256,512]{2,1,0:T(8,128)(2,1)} %get-tuple-element.125.refs_0_, bf16[6,256,512]{2,1,0:T(8,128)(2,1)} %get-tuple-element.120.refs_12_.refs_1_, bf16[256,384]{1,0:T(8,128)(2,1)} %get-tuple-element.126.refs_2_, ...), custom_call_target="tpu_custom_call" | custom-call | bytes 5308416 | tf_op jit(solution)/shard_map/cross_keys/pallas_call | solution.py:186
  90.5 4.6 %collective-permute-done.16.refs_2_ = bf16[256,768]{1,0:T(8,128)(2,1)S(1)} collective-permute-done((bf16[256,768]{1,0:T(8,128)(2,1)}, bf16[256,768]{1,0:T(8,128)(2,1)S(1)}, u32[]{:S(2)}, u32[]{:S(2)}) %collective-permute-start.16) | collective-permute-done | bytes 393248 | tf_op jit(solution)/shard_map/ppermute | solution.py:633
  95.8 7.2 %self_back.1 = (f32[128,768]{1,0:T(8,128)}, bf16[256,768]{1,0:T(8,128)(2,1)}, bf16[256,384]{1,0:T(8,128)(2,1)}, f32[512,192]{1,0:T(8,128)}, f32[512,192]{1,0:T(8...) custom-call(f32[256,768]{1,0:T(8,128)} %get-tuple-element.135.refs_0_, ...), custom_call_target="tpu_custom_call" | custom-call | bytes 11461632 | tf_op jit(solution)/shard_map/self_back/pallas_call | solution.py:186
  106.0 8.0 %cross_weights.1 = (bf16[4,96,768]{2,1,0:T(8,128)(2,1)}, bf16[4,96,768]{2,1,0:T(8,128)(2,1)}, f32[2,128,768]{2,1,0:T(8,128)}, bf16[2,128,768]{2,1,0:T(8,128)(2,1...) custom-call(bf16[2,256,768]{2,1,0:T(8,128)(2,1)} %get-tuple-element.122.refs_0_, bf16[2,256,768]{2,1,0:T(8,128)(2,1)} %copy-done.19, ...), custom_call_target="tpu_custom_call" | custom-call | bytes 14942208 | tf_op jit(solution)/shard_map/cross_weights/pallas_call | solution.py:186
  117.3 7.8 %self_weights.1 = (bf16[4,96,768]{2,1,0:T(8,128)(2,1)}, bf16[400,768]{1,0:T(8,128)(2,1)}, f32[2,128,768]{2,1,0:T(8,128)}, bf16[2,128,768]{2,1,0:T(8,128)(2,1)}, f32[8,768]{1,0:T(8,128)}) custom-call(bf16[512,768]{1,0:T(8,128)(2,1)} %get-tuple-element.146.refs_0_, bf16[256,768]{1,0:T(8,128)(2,1)} %get-tuple-element.147.refs_1_, bf16[256,768]{1,0:T(8,128)(2,1)} %copy-done.29, ...), custom_call_target="tpu_custom_call" | custom-call | bytes 8539136 | tf_op jit(solution)/shard_map/self_weights/pallas_call | solution.py:186
  125.1 4.5 %collective-permute-done.30 = bf16[4,96,768]{2,1,0:T(8,128)(2,1)S(1)} collective-permute-done((bf16[4,96,768]{2,1,0:T(8,128)(2,1)}, bf16[4,96,768]{2,1,0:T(8,128)(2,1)S(1)}, u32[]{:S(2)}, u32[]{:S(2)}) %collective-permute-start.30) | collective-permute-done | bytes 589856 | tf_op jit(solution)/shard_map/ppermute | solution.py:636
  131.5 2.7 %collective-permute-start.33 = (bf16[96,1536]{1,0:T(8,128)(2,1)S(1)}, bf16[96,1536]{1,0:T(8,128)(2,1)S(1)}, u32[]{:S(2)}, u32[]{:S(2)}) collective-permute-start(bf16[96,1536]{1,0:T(8,128)(2,1)S(1)} %fusion.10), channel_id=1, source_target_pairs={{0,16},{4,20},{8,24},{12,28},{16,0},{20,4},{24,8},{28,12},{1,17},{... | collective-permute-start | bytes 884744 | tf_op jit(solution)/shard_map/ppermute | solution.py:636
  136.0 8.0 %collective-permute-done.31 = bf16[2,96,768]{2,1,0:T(8,128)(2,1)S(1)} collective-permute-done((bf16[2,96,768]{2,1,0:T(8,128)(2,1)S(1)}, bf16[2,96,768]{2,1,0:T(8,128)(2,1)S(1)}, u32[]{:S(2)}, u32[]{:S(2)}) %collective-permute-start.31) | collective-permute-done | bytes 294944 | tf_op jit(solution)/shard_map/ppermute | solution.py:636
  144.8 5.4 %collective-permute-done.33 = bf16[96,1536]{1,0:T(8,128)(2,1)S(1)} collective-permute-done((bf16[96,1536]{1,0:T(8,128)(2,1)S(1)}, bf16[96,1536]{1,0:T(8,128)(2,1)S(1)}, u32[]{:S(2)}, u32[]{:S(2)}) %collective-permute-start.33) | collective-permute-done | bytes 294944 | tf_op jit(solution)/shard_map/ppermute | solution.py:636
  151.5 6.1 %collective-permute-start.26 = (bf16[112,768]{1,0:T(8,128)(2,1)S(1)}, bf16[112,768]{1,0:T(8,128)(2,1)S(1)}, u32[]{:S(2)}, u32[]{:S(2)}) collective-permute-start(bf16[112,768]{1,0:T(8,128)(2,1)S(1)} %get-tuple-element.198), channel_id=1, source_target_pairs={{0,8},{4,12},{8,0},{12,4},{16,24},{20,28},{24,16},{28,20},{1,9},{5... | collective-permute-start | bytes 516104 | tf_op jit(solution)/shard_map/ppermute | solution.py:636
  159.2 3.4 %collective-permute-done.25 = bf16[112,768]{1,0:T(8,128)(2,1)S(1)} collective-permute-done((bf16[112,768]{1,0:T(8,128)(2,1)S(1)}, bf16[112,768]{1,0:T(8,128)(2,1)S(1)}, u32[]{:S(2)}, u32[]{:S(2)}) %collective-permute-start.25) | collective-permute-done | bytes 172064 | tf_op jit(solution)/shard_map/ppermute | solution.py:636
  162.8 2.1 %collective-permute-done.27 = bf16[112,768]{1,0:T(8,128)(2,1)S(1)} collective-permute-done((bf16[112,768]{1,0:T(8,128)(2,1)S(1)}, bf16[112,768]{1,0:T(8,128)(2,1)S(1)}, u32[]{:S(2)}, u32[]{:S(2)}) %collective-permute-start.27) | collective-permute-done | bytes 172064 | tf_op jit(solution)/shard_map/ppermute | solution.py:636
  (181 shorter events, 47.0 us)
Async XLA Ops:
  3.7 11.0 %collective-permute-start.5 = (bf16[768,768]{1,0:T(8,128)(2,1)S(1)}, bf16[768,768]{1,0:T(8,128)(2,1)S(1)}, u32[]{:S(2)}, u32[]{:S(2)}) collective-permute-start(bf16[768,768]{1,0:T(8,128)(2,1)S(1)} %pad_maximum_fusion.refs_5_.refs_8_), channel_id=1, source_target_pairs={{0,1},{1,0},{2,3},{3,2},{4,5},{5,4},{6,7},{7,6},{8,9},{9,8},{10,11... | collective-permute-start | bytes 3538952 | tf_op jit(solution)/shard_map/ppermute | solution.py:633
  6.9 18.7 %collective-permute-start.9 = (bf16[768,768]{1,0:T(8,128)(2,1)S(1)}, bf16[768,768]{1,0:T(8,128)(2,1)S(1)}, u32[]{:S(2)}, u32[]{:S(2)}) collective-permute-start(bf16[768,768]{1,0:T(8,128)(2,1)S(1)} %pad_maximum_fusion.1.refs_4_.refs_7_.refs_8_.refs_11_.refs_12_), channel_id=1, source_target_pairs={{0,1},{1,0},{2,3},{3,2},{4,5},{5,4},{6,7},{7,6},{8,9},{9,8},{10,11... | collective-permute-start | bytes 3538952 | tf_op jit(solution)/shard_map/ppermute | solution.py:633
  12.3 11.6 %collective-permute-start = (bf16[256,768]{1,0:T(8,128)(2,1)S(1)}, bf16[256,768]{1,0:T(8,128)(2,1)S(1)}, u32[]{:S(2)}, u32[]{:S(2)}) collective-permute-start(bf16[256,768]{1,0:T(8,128)(2,1)S(1)} %pad_maximum_fusion.3.refs_0_.refs_2_), channel_id=1, source_target_pairs={{0,2},{1,3},{2,0},{3,1},{4,6},{5,7},{6,4},{7,5},{8,10},{9,11},{10,... | collective-permute-start | bytes 1179656 | tf_op jit(solution)/shard_map/ppermute | solution.py:633
  14.3 31.9 %collective-permute-start.12 = (bf16[768,768]{1,0:T(8,128)(2,1)S(1)}, bf16[768,768]{1,0:T(8,128)(2,1)S(1)}, u32[]{:S(2)}, u32[]{:S(2)}) collective-permute-start(bf16[768,768]{1,0:T(8,128)(2,1)S(1)} %copy-done.10), channel_id=1, source_target_pairs={{0,1},{1,0},{2,3},{3,2},{4,5},{5,4},{6,7},{7,6},{8,9},{9,8},{10,11... | collective-permute-start | bytes 3538952 | tf_op jit(solution)/shard_map/ppermute | solution.py:633
  14.7 36.3 %collective-permute-start.11 = (bf16[768,768]{1,0:T(8,128)(2,1)S(1)}, bf16[768,768]{1,0:T(8,128)(2,1)}, u32[]{:S(2)}, u32[]{:S(2)}) collective-permute-start(bf16[768,768]{1,0:T(8,128)(2,1)S(1)} %copy-done.15), channel_id=1, source_target_pairs={{0,1},{1,0},{2,3},{3,2},{4,5},{5,4},{6,7},{7,6},{8,9},{9,8},{10,11... | collective-permute-start | bytes 3538952 | tf_op jit(solution)/shard_map/ppermute | solution.py:633
  23.9 11.7 %collective-permute-start.8 = (bf16[256,768]{1,0:T(8,128)(2,1)}, bf16[256,768]{1,0:T(8,128)(2,1)S(1)}, u32[]{:S(2)}, u32[]{:S(2)}) collective-permute-start(bf16[256,768]{1,0:T(8,128)(2,1)} %get-tuple-element.105.refs_4_), channel_id=1, source_target_pairs={{0,2},{1,3},{2,0},{3,1},{4,6},{5,7},{6,4},{7,5},{8,10},{9,11},{10,... | collective-permute-start | bytes 1179656 | tf_op jit(solution)/shard_map/ppermute | solution.py:633
  44.4 11.0 %collective-permute-start.10 = (bf16[256,768]{1,0:T(8,128)(2,1)}, bf16[256,768]{1,0:T(8,128)(2,1)S(1)}, u32[]{:S(2)}, u32[]{:S(2)}) collective-permute-start(bf16[256,768]{1,0:T(8,128)(2,1)} %get-tuple-element.110.refs_1_), channel_id=1, source_target_pairs={{0,2},{1,3},{2,0},{3,1},{4,6},{5,7},{6,4},{7,5},{8,10},{9,11},{10,... | collective-permute-start | bytes 1179656 | tf_op jit(solution)/shard_map/ppermute | solution.py:633
  62.4 11.7 %collective-permute-start.13 = (bf16[256,768]{1,0:T(8,128)(2,1)}, bf16[256,768]{1,0:T(8,128)(2,1)S(1)}, u32[]{:S(2)}, u32[]{:S(2)}) collective-permute-start(bf16[256,768]{1,0:T(8,128)(2,1)} %get-tuple-element.113.refs_4_), channel_id=1, source_target_pairs={{0,2},{1,3},{2,0},{3,1},{4,6},{5,7},{6,4},{7,5},{8,10},{9,11},{10,... | collective-permute-start | bytes 1179656 | tf_op jit(solution)/shard_map/ppermute | solution.py:633
  82.7 31.8 %collective-permute-start.20 = (bf16[4,96,1536]{2,1,0:T(8,128)(2,1)S(1)}, bf16[4,96,1536]{2,1,0:T(8,128)(2,1)S(1)}, u32[]{:S(2)}, u32[]{:S(2)}) collective-permute-start(bf16[4,96,1536]{2,1,0:T(8,128)(2,1)S(1)} %copy-done.41), channel_id=1, source_target_pairs={{0,4},{4,0},{8,12},{12,8},{16,20},{20,16},{24,28},{28,24},{1,5},{5... | collective-permute-start | bytes 3538952 | tf_op jit(solution)/shard_map/ppermute | solution.py:636
  84.5 10.6 %collective-permute-start.16 = (bf16[256,768]{1,0:T(8,128)(2,1)}, bf16[256,768]{1,0:T(8,128)(2,1)S(1)}, u32[]{:S(2)}, u32[]{:S(2)}) collective-permute-start(bf16[256,768]{1,0:T(8,128)(2,1)} %get-tuple-element.124.refs_1_), channel_id=1, source_target_pairs={{0,2},{1,3},{2,0},{3,1},{4,6},{5,7},{6,4},{7,5},{8,10},{9,11},{10,... | collective-permute-start | bytes 1179656 | tf_op jit(solution)/shard_map/ppermute | solution.py:633
  86.0 17.7 %collective-permute-start.15 = (bf16[2,256,768]{2,1,0:T(8,128)(2,1)}, bf16[2,256,768]{2,1,0:T(8,128)(2,1)S(1)}, u32[]{:S(2)}, u32[]{:S(2)}) collective-permute-start(bf16[2,256,768]{2,1,0:T(8,128)(2,1)} %get-tuple-element.122.refs_0_), channel_id=1, source_target_pairs={{0,1},{1,0},{2,3},{3,2},{4,5},{5,4},{6,7},{7,6},{8,9},{9,8},{10,11... | collective-permute-start | bytes 2359304 | tf_op jit(solution)/shard_map/ppermute | solution.py:633
  103.1 11.5 %collective-permute-start.19 = (bf16[768,384]{1,0:T(8,128)(2,1)}, bf16[768,384]{1,0:T(8,128)(2,1)S(1)}, u32[]{:S(2)}, u32[]{:S(2)}) collective-permute-start(bf16[768,384]{1,0:T(8,128)(2,1)} %get-tuple-element.151), channel_id=1, source_target_pairs={{0,1},{1,0},{2,3},{3,2},{4,5},{5,4},{6,7},{7,6},{8,9},{9,8},{10,11... | collective-permute-start | bytes 1769480 | tf_op jit(solution)/shard_map/ppermute | solution.py:633
  103.6 12.9 %collective-permute-start.18 = (bf16[256,768]{1,0:T(8,128)(2,1)}, bf16[256,768]{1,0:T(8,128)(2,1)S(1)}, u32[]{:S(2)}, u32[]{:S(2)}) collective-permute-start(bf16[256,768]{1,0:T(8,128)(2,1)} %get-tuple-element.147.refs_1_), channel_id=1, source_target_pairs={{0,1},{1,0},{2,3},{3,2},{4,5},{5,4},{6,7},{7,6},{8,9},{9,8},{10,11... | collective-permute-start | bytes 1179656 | tf_op jit(solution)/shard_map/ppermute | solution.py:633
  114.0 15.7 %collective-permute-start.30 = (bf16[4,96,768]{2,1,0:T(8,128)(2,1)}, bf16[4,96,768]{2,1,0:T(8,128)(2,1)S(1)}, u32[]{:S(2)}, u32[]{:S(2)}) collective-permute-start(bf16[4,96,768]{2,1,0:T(8,128)(2,1)} %get-tuple-element.171), channel_id=1, source_target_pairs={{0,4},{4,0},{8,12},{12,8},{16,20},{20,16},{24,28},{28,24},{1,5},{5... | collective-permute-start | bytes 1769480 | tf_op jit(solution)/shard_map/ppermute | solution.py:636
  114.6 16.8 %collective-permute-start.22 = (bf16[2,96,1536]{2,1,0:T(8,128)(2,1)S(1)}, bf16[2,96,1536]{2,1,0:T(8,128)(2,1)S(1)}, u32[]{:S(2)}, u32[]{:S(2)}) collective-permute-start(bf16[2,96,1536]{2,1,0:T(8,128)(2,1)S(1)} %add_convert_fusion), channel_id=1, source_target_pairs={{0,8},{4,12},{8,0},{12,4},{16,24},{20,28},{24,16},{28,20},{1,9},{5... | collective-permute-start | bytes 1769480 | tf_op jit(solution)/shard_map/ppermute | solution.py:636
  129.7 14.3 %collective-permute-start.31 = (bf16[2,96,768]{2,1,0:T(8,128)(2,1)S(1)}, bf16[2,96,768]{2,1,0:T(8,128)(2,1)S(1)}, u32[]{:S(2)}, u32[]{:S(2)}) collective-permute-start(bf16[2,96,768]{2,1,0:T(8,128)(2,1)S(1)} %add_convert_fusion.2), channel_id=1, source_target_pairs={{0,8},{4,12},{8,0},{12,4},{16,24},{20,28},{24,16},{28,20},{1,9},{5... | collective-permute-start | bytes 884744 | tf_op jit(solution)/shard_map/ppermute | solution.py:636
  131.5 18.7 %collective-permute-start.33 = (bf16[96,1536]{1,0:T(8,128)(2,1)S(1)}, bf16[96,1536]{1,0:T(8,128)(2,1)S(1)}, u32[]{:S(2)}, u32[]{:S(2)}) collective-permute-start(bf16[96,1536]{1,0:T(8,128)(2,1)S(1)} %fusion.10), channel_id=1, source_target_pairs={{0,16},{4,20},{8,24},{12,28},{16,0},{20,4},{24,8},{28,12},{1,17},{... | collective-permute-start | bytes 884744 | tf_op jit(solution)/shard_map/ppermute | solution.py:636
  134.9 16.3 %collective-permute-start.21 = (bf16[400,768]{1,0:T(8,128)(2,1)S(1)}, bf16[400,768]{1,0:T(8,128)(2,1)S(1)}, u32[]{:S(2)}, u32[]{:S(2)}) collective-permute-start(bf16[400,768]{1,0:T(8,128)(2,1)S(1)} %copy-done.42), channel_id=1, source_target_pairs={{0,4},{4,0},{8,12},{12,8},{16,20},{20,16},{24,28},{28,24},{1,5},{5... | collective-permute-start | bytes 1843208 | tf_op jit(solution)/shard_map/ppermute | solution.py:636
  135.5 15.7 %collective-permute-start.23 = (bf16[2,128,768]{2,1,0:T(8,128)(2,1)S(1)}, bf16[2,128,768]{2,1,0:T(8,128)(2,1)S(1)}, u32[]{:S(2)}, u32[]{:S(2)}) collective-permute-start(bf16[2,128,768]{2,1,0:T(8,128)(2,1)S(1)} %copy-done.45), channel_id=1, source_target_pairs={{0,1},{1,0},{2,3},{3,2},{4,5},{5,4},{6,7},{7,6},{8,9},{9,8},{10,11... | collective-permute-start | bytes 1179656 | tf_op jit(solution)/shard_map/ppermute | solution.py:633
  135.5 15.7 %collective-permute-start.24 = (bf16[2,128,768]{2,1,0:T(8,128)(2,1)S(1)}, bf16[2,128,768]{2,1,0:T(8,128)(2,1)S(1)}, u32[]{:S(2)}, u32[]{:S(2)}) collective-permute-start(bf16[2,128,768]{2,1,0:T(8,128)(2,1)S(1)} %copy-done.44), channel_id=1, source_target_pairs={{0,1},{1,0},{2,3},{3,2},{4,5},{5,4},{6,7},{7,6},{8,9},{9,8},{10,11... | collective-permute-start | bytes 1179656 | tf_op jit(solution)/shard_map/ppermute | solution.py:633
  144.2 22.0 %collective-permute-start.32 = (bf16[96,768]{1,0:T(8,128)(2,1)S(1)}, bf16[96,768]{1,0:T(8,128)(2,1)S(1)}, u32[]{:S(2)}, u32[]{:S(2)}) collective-permute-start(bf16[96,768]{1,0:T(8,128)(2,1)S(1)} %fusion.22), channel_id=1, source_target_pairs={{0,16},{4,20},{8,24},{12,28},{16,0},{20,4},{24,8},{28,12},{1,17},{... | collective-permute-start | bytes 442376 | tf_op jit(solution)/shard_map/ppermute | solution.py:636
  151.4 11.2 %collective-permute-start.25 = (bf16[112,768]{1,0:T(8,128)(2,1)S(1)}, bf16[112,768]{1,0:T(8,128)(2,1)S(1)}, u32[]{:S(2)}, u32[]{:S(2)}) collective-permute-start(bf16[112,768]{1,0:T(8,128)(2,1)S(1)} %get-tuple-element.197), channel_id=1, source_target_pairs={{0,16},{4,20},{8,24},{12,28},{16,0},{20,4},{24,8},{28,12},{1,17},{... | collective-permute-start | bytes 516104 | tf_op jit(solution)/shard_map/ppermute | solution.py:636
  151.5 11.3 %collective-permute-start.26 = (bf16[112,768]{1,0:T(8,128)(2,1)S(1)}, bf16[112,768]{1,0:T(8,128)(2,1)S(1)}, u32[]{:S(2)}, u32[]{:S(2)}) collective-permute-start(bf16[112,768]{1,0:T(8,128)(2,1)S(1)} %get-tuple-element.198), channel_id=1, source_target_pairs={{0,8},{4,12},{8,0},{12,4},{16,24},{20,28},{24,16},{28,20},{1,9},{5... | collective-permute-start | bytes 516104 | tf_op jit(solution)/shard_map/ppermute | solution.py:636
  157.7 9.9 %collective-permute-start.29 = (bf16[384,768]{1,0:T(8,128)(2,1)S(1)}, bf16[384,768]{1,0:T(8,128)(2,1)S(1)}, u32[]{:S(2)}, u32[]{:S(2)}) collective-permute-start(bf16[384,768]{1,0:T(8,128)(2,1)S(1)} %pad_maximum_fusion.2), channel_id=1, source_target_pairs={{0,2},{1,3},{2,0},{3,1},{4,6},{5,7},{6,4},{7,5},{8,10},{9,11},{10,... | collective-permute-start | bytes 1769480 | tf_op jit(solution)/shard_map/ppermute | solution.py:633
  (57 other events, 267.5 us)
